TPU v7x, 32 devices: a whole 2x2x4 slice. The times are simulated.
32 devices in a mesh: rep: 8 (over y, x, core), fsdp: 4 (over z).
Axes of the slice: x: 2, y: 2, z: 4, core: 2. Of those that a mesh axis runs over, the one named last changes fastest.
Arguments:
- tokens: bfloat16 [4096, 4096], P(('rep', 'fsdp')), may hold values from -6 to 6
- queries: bfloat16 [4096, 2048], P(('rep', 'fsdp')), may hold values from -10 to 10
- rotated_key_rows: bfloat16 [4096, 512], P(('rep', 'fsdp')), may hold values from -3 to 3
- targets: bfloat16 [4096, 2048], P(('rep', 'fsdp')), may hold values from -6 to 6
- value_weights: float32 [4096, 512], P('fsdp'), may hold values from -4 to 4
- momentum: float32 [4096, 512], P('fsdp'), may hold values from -0.6 to 0.6
- first_moment: float32 [8, 4096, 512], P('rep', 'fsdp'), may hold values from -1.8 to 1.8
- second_moment: float32 [8, 4096, 512], P('rep', 'fsdp'), may hold values from 0.02 to 0.5
Outputs:
- new_weights: float32 [4096, 512], P('fsdp')
- new_momentum: float32 [4096, 512], P('fsdp')
All inputs are finite; a program needn't handle non-finite values.
Results may differ from a plain program's by a relative error of at most 0.0045.
Values may be sent and summed in bfloat16 or wider, within the bound.
No kernel may reach another device: no remote copies, remote signals or barrier semaphores. Data moves between devices by JAX's collectives and lax.ppermute only.
A program may use at most 64 MiB of HBM per device.

v0:
```python
import math

import jax
import jax.numpy as jnp
from jax import lax
from jax.sharding import PartitionSpec as P

D = 4096
HEAD_SIZE = 128


first_decay = 0.9
second_decay = 0.95
weight_decay = 0.1
inner_rate = 0.05
outer_rate = 0.7
momentum_keep = 0.9
epsilon = 1e-08


def per_device(
    tokens, queries, rotated_key_rows, targets, value_weights, momentum, first_moment, second_moment
):
    kv_width = value_weights.shape[1]
    seq_len = tokens.shape[0]
    groups = rotated_key_rows.shape[1] // HEAD_SIZE
    heads_per_group = queries.shape[1] // rotated_key_rows.shape[1]
    replica_tokens = seq_len * lax.axis_size("fsdp")
    inv_root = 1.0 / math.sqrt(D)
    score_scale = 1.0 / math.sqrt(HEAD_SIZE)
    cot_scale = math.sqrt(D / replica_tokens)
    compact = value_weights.astype(jnp.bfloat16)
    feature_cols = tokens
    value_sum = jnp.dot(
        feature_cols,
        lax.all_gather(compact, "fsdp", axis=0, tiled=True),
        preferred_element_type=jnp.float32,
    )
    value_result = (value_sum * inv_root).astype(jnp.bfloat16)
    query_head_count = queries.reshape(seq_len, groups, heads_per_group, HEAD_SIZE)
    key_head_count = rotated_key_rows.reshape(seq_len, groups, HEAD_SIZE)
    value_head_count = value_result.reshape(seq_len, groups, HEAD_SIZE)
    scores = (
        jnp.einsum(
            "tgjd,sgd->gjts", query_head_count, key_head_count, preferred_element_type=jnp.float32
        )
        * score_scale
    )
    causal = lax.broadcasted_iota(jnp.int32, (seq_len, seq_len), 0) >= lax.broadcasted_iota(
        jnp.int32, (seq_len, seq_len), 1
    )
    scores = jnp.where(causal, scores, -jnp.inf)
    row_top = jnp.max(scores, axis=-1, keepdims=True)
    expo = jnp.exp(scores - row_top)
    probs = (expo / jnp.sum(expo, axis=-1, keepdims=True)).astype(jnp.bfloat16)
    outputs = jnp.einsum(
        "gjts,sgd->tgjd", probs, value_head_count, preferred_element_type=jnp.float32
    )
    objective = targets.reshape(seq_len, groups, heads_per_group, HEAD_SIZE).astype(jnp.float32)
    residual_term = ((outputs - objective) * cot_scale).astype(jnp.bfloat16)
    value_grad = jnp.einsum(
        "gjts,tgjd->sgd", probs, residual_term, preferred_element_type=jnp.float32
    )
    value_grad = value_grad.astype(jnp.bfloat16).reshape(seq_len, kv_width)
    feature_cols = tokens
    gradient = lax.psum_scatter(
        jnp.einsum(
            "si,sc->ic", feature_cols, value_grad, preferred_element_type=jnp.float32
        ).astype(jnp.bfloat16),
        "fsdp",
        scatter_dimension=0,
        tiled=True,
    ).astype(jnp.float32)
    gradient = gradient * inv_root
    first_new = first_decay * first_moment[0] + (1.0 - first_decay) * gradient
    second_new = second_decay * second_moment[0] + (1.0 - second_decay) * gradient * gradient
    direction = first_new / (jnp.sqrt(second_new) + epsilon) + weight_decay * value_weights
    mean_direction = lax.psum(direction, "rep") / lax.axis_size("rep")
    new_momentum = momentum_keep * momentum + mean_direction
    new_weights = value_weights - outer_rate * inner_rate * (
        mean_direction + momentum_keep * new_momentum
    )
    return (new_weights, new_momentum)


def solution(mesh):
    in_specs = (
        P(("rep", "fsdp"), None),
        P(("rep", "fsdp"), None),
        P(("rep", "fsdp"), None),
        P(("rep", "fsdp"), None),
        P("fsdp", None),
        P("fsdp", None),
        P("rep", "fsdp", None),
        P("rep", "fsdp", None),
    )
    out_specs = (P("fsdp", None), P("fsdp", None))
    return jax.shard_map(
        per_device, mesh=mesh, in_specs=in_specs, out_specs=out_specs, check_vma=False
    )
```

profile of v0, /device:TPU:0, one launch (start us, length us, event | category | flops | bytes accessed | tf_op | source)
XLA Modules:
  0.0 259.8 jit_solution(3074234993048620050)
XLA Ops:
  7.2 0.0 copy-start
  7.2 0.0 copy-start.3
  7.2 0.0 copy-start.4
  7.2 0.0 copy-start.2
  7.2 0.0 all-gather.2.cloned.1.call-start
  7.3 2.8 %convert_element_type.33 = bf16[1024,512]{1,0:T(8,128)(2,1)} convert(f32[1024,512]{1,0:T(8,128)} %param.12) | non-fusion elementwise | flops 524288 | bytes 3145728 | tf_op jit(solution)/shard_map/convert_element_type | solution.py:32
  10.1 0.0 all-gather.2.cloned.1.call-update
  10.1 0.0 reduce-scatter.2.cloned.1.call-start
  10.2 0.0 copy-done.3
  10.2 0.4 reshape.27
  10.5 0.0 copy-done.4
  10.6 0.0 copy-done.2
  10.6 0.2 copy.28
  10.8 1.4 fusion.37
  12.3 0.0 copy-start.5
  12.3 81.5 %all-gather.2.cloned.1.call-done = bf16[4096,512]{1,0:T(8,128)(2,1)} async-done(((bf16[1024,512]{1,0:T(8,128)(2,1)}), bf16[4096,512]{1,0:T(8,128)(2,1)}) %all-gather.2.cloned.1.call-update) | async-done | bytes 4194320 | tf_op jit(solution)/shard_map/all_gather | solution.py:36
  93.7 0.0 copy-done
  93.7 2.9 %fusion.19 = bf16[128,512]{1,0:T(8,128)(2,1)S(1)} fusion(bf16[128,4096]{1,0:T(8,128)(2,1)S(1)} %copy-done, bf16[4096,512]{1,0:T(8,128)(2,1)} %all-gather.2.cloned.1.call-done), kind=kOutput, calls=%fused_computation.28 | convolution fusion | flops 537001984 | bytes 5373952 | tf_op jit(solution)/shard_map/dot_general | solution.py:34
  96.7 0.1 copy.25
  96.8 0.0 copy-done.5
  96.8 0.4 fusion.18
  97.2 3.2 %fusion.1 = bf16[4096,512]{0,1:T(8,128)(2,1)} fusion(bf16[128,512]{0,1:T(8,128)(2,1)S(1)} %bitcast.47, bf16[128,4096]{1,0:T(8,128)(2,1)S(1)} %copy-done), kind=kOutput, calls=%fused_computation.2 | convolution fusion | flops 538968064 | bytes 5373952 | tf_op jit(solution)/shard_map/si,sc->ic/dot_general | solution.py:67
  100.4 0.0 reduce-scatter.2.cloned.1.call-update
  100.4 0.0 all-reduce.2.cloned.1.call-start
  100.5 1.9 copy.18
  102.4 2.9 %copy.10 = f32[1,1024,512]{1,2,0:T(8,128)} copy(f32[1,1024,512]{2,1,0:T(8,128)} %param.14) | data formatting | bytes 4194304 | tf_op args[6]
  105.3 3.0 %copy.15 = f32[1,1024,512]{1,2,0:T(8,128)} copy(f32[1,1024,512]{2,1,0:T(8,128)} %param.15) | data formatting | bytes 4194304 | tf_op args[7]
  108.3 67.5 %reduce-scatter.2.cloned.1.call-done = bf16[1024,512]{0,1:T(8,128)(2,1)} async-done(((bf16[4096,512]{0,1:T(8,128)(2,1)}), bf16[1024,512]{0,1:T(8,128)(2,1)}) %reduce-scatter.2.cloned.1.call-update) | async-done | bytes 1048592 | tf_op jit(solution)/shard_map/reduce_scatter | solution.py:66
  175.9 5.3 %fusion.4 = f32[1024,512]{0,1:T(8,128)} fusion(bf16[1024,512]{0,1:T(8,128)(2,1)} %reduce-scatter.2.cloned.1.call-done, f32[1024,512]{0,1:T(8,128)S(1)} %copy.18, f32[1,1024,512]{1,2,0:T(8,128)} %copy.15, f32[1,1024,512]{1,2,0:T(8,128)} %copy.10), kind=kLoop, calls=%fused_computation.8 | loop fusion | flops 6815744 | bytes 9437184 | tf_op jit(solution)/shard_map/add | solution.py:77
  181.2 0.0 all-reduce.2.cloned.1.call-update
  181.2 2.9 %copy.17 = f32[1024,512]{0,1:T(8,128)} copy(f32[1024,512]{1,0:T(8,128)} %param.13) | data formatting | bytes 4194304 | tf_op args[5]
  184.1 59.2 %all-reduce.2.cloned.1.call-done = f32[1024,512]{0,1:T(8,128)} async-done(((f32[1024,512]{0,1:T(8,128)}), f32[1024,512]{0,1:T(8,128)}) %all-reduce.2.cloned.1.call-update) | async-done | bytes 2097168 | tf_op jit(solution)/shard_map/psum | solution.py:78
  243.3 5.2 %multiply_add_fusion = (f32[1024,512]{0,1:T(8,128)}, f32[1024,512]{0,1:T(8,128)}) fusion(f32[1024,512]{0,1:T(8,128)} %copy.17, f32[1024,512]{0,1:T(8,128)} %all-reduce.2.cloned.1.call-done, f32[1024,512]{0,1:T(8,128)S(1)} %copy.18), kind=kLoop, calls=%fused_computation.14 | loop fusion | flops 3670016 | bytes 10485760 | tf_op jit(solution)/shard_map/add | solution.py:79
  248.5 0.0 copy-start.1
  248.5 3.0 %copy.19 = f32[1024,512]{1,0:T(8,128)} copy(f32[1024,512]{0,1:T(8,128)} %get-tuple-element.5) | data formatting | bytes 4194304
  251.5 0.0 copy-done.1
  251.5 1.8 copy.20
  (2 shorter events, 0.1 us)
Async XLA Ops:
  7.2 86.6 %copy-start = (bf16[128,4096]{1,0:T(8,128)(2,1)S(1)}, bf16[128,4096]{1,0:T(8,128)(2,1)}, u32[]{:S(2)}) copy-start(bf16[128,4096]{1,0:T(8,128)(2,1)} %param.8) | copy-start | bytes 3145732
  7.2 3.0 %copy-start.3 = (bf16[128,2048]{1,0:T(8,128)(2,1)S(1)}, bf16[128,2048]{1,0:T(8,128)(2,1)}, u32[]{:S(2)}) copy-start(bf16[128,2048]{1,0:T(8,128)(2,1)} %param.9) | copy-start | bytes 1572868
  7.2 3.4 %copy-start.4 = (bf16[128,512]{1,0:T(8,128)(2,1)S(1)}, bf16[128,512]{1,0:T(8,128)(2,1)}, u32[]{:S(2)}) copy-start(bf16[128,512]{1,0:T(8,128)(2,1)} %param.10) | copy-start | bytes 393220
  7.2 3.4 %copy-start.2 = (bf16[128,2048]{1,0:T(8,128)(2,1)S(1)}, bf16[128,2048]{1,0:T(8,128)(2,1)}, u32[]{:S(2)}) copy-start(bf16[128,2048]{1,0:T(8,128)(2,1)} %param.11) | copy-start | bytes 1572868
  7.2 86.5 %all-gather.2.cloned.1.call-start = ((), (), s32[]{:S(2)}) async-start(), calls=%async_computation.1 | async-start | bytes 5242880 | tf_op jit(solution)/shard_map/all_gather | solution.py:36
  10.1 165.8 %reduce-scatter.2.cloned.1.call-start = ((), (), s32[]{:S(2)}) async-start(), calls=%async_computation.2 | async-start | bytes 5242880 | tf_op jit(solution)/shard_map/reduce_scatter | solution.py:66
  12.3 84.5 %copy-start.5 = (f32[4,4,128,128]{2,3,1,0:T(8,128)S(1)}, f32[4,4,128,128]{2,3,1,0:T(8,128)}, u32[]{:S(2)}) copy-start(f32[4,4,128,128]{2,3,1,0:T(8,128)} %get-tuple-element.7) | copy-start | bytes 3145732
  100.4 142.8 %all-reduce.2.cloned.1.call-start = ((), (), s32[]{:S(2)}) async-start(), calls=%async_computation.3 | async-start | bytes 4194304 | tf_op jit(solution)/shard_map/psum | solution.py:78
  248.5 3.0 %copy-start.1 = (f32[1024,512]{0,1:T(8,128)S(1)}, f32[1024,512]{0,1:T(8,128)}, u32[]{:S(2)}) copy-start(f32[1024,512]{0,1:T(8,128)} %get-tuple-element.4) | copy-start | bytes 6291460
Sparse Core Ops, SparseCore 0:
  10.2 83.4 all-gather.1
  100.6 75.2 reduce-scatter.1
  181.3 61.9 all-reduce.1
where the time goes:
time: 260 us
  waiting for transfers between devices  208 us (80%)
  local copies, waits for them, and re-layouts  16.3 us (6%)
  between operations  13.9 us (5%)
  other arithmetic  13.3 us (5%)
  matrix products  7.96 us (3%)
    all_gather x1, waiting for transfers between devices, per_device(): lax.all_gather(compact, 'fsdp', axis=0, tiled=True)  81.5 us
    reduce_scatter x1, waiting for transfers between devices, per_device(): lax.psum_scatter(jnp.einsum('si,sc->ic', feature_cols, value_grad, prefer...  67.5 us
    psum x1, waiting for transfers between devices, per_device(): mean_direction = lax.psum(direction, 'rep') / lax.axis_size('rep')  59.2 us
    unnamed x18, local copies, waits for them, and re-layouts  15.6 us
    add x1, other arithmetic, per_device(): first_new / (jnp.sqrt(second_new) + epsilon) + weight_decay * value_weights  5.28 us
    add x1, other arithmetic, per_device(): new_momentum = momentum_keep * momentum + mean_direction  5.2 us
  transfers between devices with their start and end apart: 3, of which 3 were waited for; matrix products, arithmetic and copies ran while one was open for 5% of the time, Pallas kernels for 0%

commit v1 on v0

v1 whole, which is shorter than its diff:
```python
import functools
import math

import jax
import jax.numpy as jnp
from jax import lax
from jax.experimental import pallas as pl
from jax.experimental.pallas import tpu as pltpu
from jax.sharding import PartitionSpec as P

D = 4096
HEAD_SIZE = 128


first_decay = 0.9
second_decay = 0.95
weight_decay = 0.1
inner_rate = 0.05
outer_rate = 0.7
momentum_keep = 0.9
epsilon = 1e-08

BF = jnp.bfloat16
F32 = jnp.float32
VMEM = pl.BlockSpec(memory_space=pltpu.VMEM)
PARAMS = pltpu.CompilerParams(vmem_limit_bytes=48 * 1024 * 1024)


def cost(flops, nbytes):
    return pl.CostEstimate(flops=flops, bytes_accessed=nbytes, transcendentals=0)


def dot(a, b, dims=((1,), (0,))):
    return lax.dot_general(a, b, (dims, ((), ())), preferred_element_type=F32)


def attention_kernel(groups, per_group, queries, keys, targets, g_hi, g_lo, cross):
    seq = queries.shape[0]
    wide = per_group * seq
    source = lax.broadcasted_iota(jnp.int32, (seq, wide), 0)
    reader = lax.rem(lax.broadcasted_iota(jnp.int32, (seq, wide), 1), seq)
    causal = source <= reader
    for g in range(groups):
        cols = slice(g * HEAD_SIZE, (g + 1) * HEAD_SIZE)
        heads = [
            slice((g * per_group + h) * HEAD_SIZE, (g * per_group + h + 1) * HEAD_SIZE)
            for h in range(per_group)
        ]
        query = jnp.concatenate([queries[:, h] for h in heads], axis=0)
        target = jnp.concatenate([targets[:, h] for h in heads], axis=0)
        scores = dot(keys[:, cols], query, ((1,), (1,))) * (1.0 / math.sqrt(HEAD_SIZE))
        scores = jnp.where(causal, scores, -jnp.inf)
        expo = jnp.exp(scores - jnp.max(scores, axis=0, keepdims=True))
        probs = (expo / jnp.sum(expo, axis=0, keepdims=True)).astype(BF)
        gram = dot(probs, probs, ((1,), (1,)))
        high = gram.astype(BF)
        g_hi[:, cols] = high
        g_lo[:, cols] = (gram - high.astype(F32)).astype(BF)
        cross[:, cols] = dot(probs, target)


def own_kernel(tokens, weights, compact, own):
    compact[...] = weights[...].astype(BF)
    own[...] = dot(tokens[...], compact[...])


def partial_kernel(n, *refs):
    blocks, compact, outs = refs[:n], refs[n], refs[n + 1 :]
    for block, out in zip(blocks, outs):
        out[...] = dot(block[...], compact[...]).astype(BF)


def transpose_kernel(n, *refs):
    blocks, out = refs[:n], refs[n]
    seq = blocks[0].shape[0]
    for k, block in enumerate(blocks):
        out[:, k * seq : (k + 1) * seq] = block[...].T


def value_grad_kernel(n, scale, *refs):
    own, parts = refs[0], refs[1:n]
    g_hi, g_lo, cross, out = refs[n:]
    total = own[...]
    for part in parts:
        total = total + part[...].astype(F32)
    value = (total * (1.0 / math.sqrt(D))).astype(BF)
    for g in range(out.shape[1] // HEAD_SIZE):
        cols = slice(g * HEAD_SIZE, (g + 1) * HEAD_SIZE)
        acc = dot(g_hi[:, cols], value[:, cols]) + dot(g_lo[:, cols], value[:, cols])
        out[:, cols] = ((acc - cross[:, cols]) * scale).astype(BF)


def direction_kernel(n, start, features, *refs):
    grads = refs[:n]
    first, second, weights, out, stacked = refs[n:]
    seq = grads[0].shape[0]

    @pl.when(pl.program_id(0) == 0)
    def _():
        for k, grad in enumerate(grads):
            stacked[k * seq : (k + 1) * seq, :] = grad[...]

    gradient = dot(features[...], stacked[...]) * (1.0 / math.sqrt(D))
    first_new = first_decay * first[0] + (1.0 - first_decay) * gradient
    second_new = second_decay * second[0] + (1.0 - second_decay) * gradient * gradient
    direction = first_new / (jnp.sqrt(second_new) + epsilon) + weight_decay * weights[...]
    out[...] = direction.astype(out.dtype)


def direction_half(start, count, block, features, grads, first, second, weights, dtype):
    n = len(grads)
    width = weights.shape[1]
    seqs = features.shape[1]
    full = pl.BlockSpec((grads[0].shape[0], width), lambda i, s: (0, 0))
    moment = pl.BlockSpec((1, block, width), lambda i, s: (0, s[0] + i, 0))
    rows = count * block
    return pl.pallas_call(
        functools.partial(direction_kernel, n),
        grid_spec=pltpu.PrefetchScalarGridSpec(
            num_scalar_prefetch=1,
            grid=(count,),
            in_specs=[pl.BlockSpec((block, seqs), lambda i, s: (s[0] + i, 0))]
            + [full] * n
            + [moment, moment, pl.BlockSpec((block, width), lambda i, s: (s[0] + i, 0))],
            out_specs=pl.BlockSpec((block, width), lambda i, s: (i, 0)),
            scratch_shapes=[pltpu.VMEM((seqs, width), BF)],
        ),
        out_shape=jax.ShapeDtypeStruct((rows, width), dtype),
        compiler_params=PARAMS,
        cost_estimate=cost(2 * rows * seqs * width, rows * width * 16),
        name="direction",
    )(start, features, *grads, first, second, weights)


def split_kernel(n, where, mine, theirs, own, *outs):
    rows = own.shape[0]
    for k in range(n):
        at = pl.ds(pl.multiple_of((where[0] ^ k) * rows, rows), rows)
        total = mine[at, :] + theirs[at, :].astype(F32)
        if k == 0:
            own[...] = total
        else:
            outs[k - 1][...] = total.astype(BF)


def mean_kernel(inv, own, *refs):
    parts, out = refs[:-1], refs[-1]
    total = own[...]
    for part in parts:
        total = total + part[...].astype(F32)
    out[...] = (total * inv).astype(BF)


def outer_kernel(mean, momentum, weights, new_weights, new_momentum):
    mean_direction = mean[...].astype(F32)
    kept = momentum_keep * momentum[...] + mean_direction
    new_momentum[...] = kept
    new_weights[...] = weights[...] - outer_rate * inner_rate * (
        mean_direction + momentum_keep * kept
    )


def partner(i, k, n):
    return i ^ k if n & (n - 1) == 0 else (i + k) % n


def exchange(x, axis, k):
    n = lax.axis_size(axis)
    return lax.ppermute(x, axis, [(i, partner(i, k, n)) for i in range(n)])


def per_device(
    tokens, queries, rotated_key_rows, targets, value_weights, momentum, first_moment, second_moment
):
    seq_len = tokens.shape[0]
    rows, width = value_weights.shape
    n_seq = lax.axis_size("fsdp")
    n_rep = lax.axis_size("rep")
    groups = rotated_key_rows.shape[1] // HEAD_SIZE
    heads_per_group = queries.shape[1] // rotated_key_rows.shape[1]
    cot_scale = math.sqrt(D / (seq_len * n_seq))
    me = lax.axis_index("fsdp")
    hops = range(1, n_seq)
    power = n_seq & (n_seq - 1) == 0

    def columns(k):
        at = me ^ k if power else lax.rem(me + k, n_seq)
        return lax.dynamic_slice(tokens, (0, at * rows), (seq_len, rows))

    def sender(k):
        return k if power or k == 0 else n_seq - k

    own_block = columns(0)
    blocks = [exchange(columns(k), "fsdp", k) for k in hops]

    block_shape = jax.ShapeDtypeStruct((seq_len, width), BF)
    wide_shape = jax.ShapeDtypeStruct((seq_len, width), F32)
    g_hi, g_lo, cross = pl.pallas_call(
        functools.partial(attention_kernel, groups, heads_per_group),
        out_shape=(block_shape, block_shape, wide_shape),
        in_specs=[VMEM] * 3,
        out_specs=(VMEM,) * 3,
        compiler_params=PARAMS,
        cost_estimate=cost(6 * seq_len * seq_len * queries.shape[1], 4 * queries.size),
        name="attention",
    )(queries, rotated_key_rows, targets)
    compact, own_value = pl.pallas_call(
        own_kernel,
        out_shape=(jax.ShapeDtypeStruct((rows, width), BF), wide_shape),
        in_specs=[VMEM] * 2,
        out_specs=(VMEM,) * 2,
        compiler_params=PARAMS,
        cost_estimate=cost(2 * seq_len * rows * width, 6 * rows * width),
        name="own_value",
    )(own_block, value_weights)

    products = pl.pallas_call(
        functools.partial(partial_kernel, n_seq - 1),
        out_shape=(block_shape,) * (n_seq - 1),
        in_specs=[VMEM] * n_seq,
        out_specs=(VMEM,) * (n_seq - 1),
        compiler_params=PARAMS,
        cost_estimate=cost(2 * seq_len * rows * width * (n_seq - 1), 2 * rows * width),
        name="partial_values",
    )(*blocks, compact)
    parts = [exchange(products[k - 1], "fsdp", sender(k)) for k in hops]
    features = pl.pallas_call(
        functools.partial(transpose_kernel, n_seq),
        out_shape=jax.ShapeDtypeStruct((rows, n_seq * seq_len), BF),
        in_specs=[VMEM] * n_seq,
        out_specs=VMEM,
        compiler_params=PARAMS,
        cost_estimate=cost(0, 4 * rows * n_seq * seq_len),
        name="transpose_tokens",
    )(own_block, *blocks)
    value_grad = pl.pallas_call(
        functools.partial(value_grad_kernel, n_seq, cot_scale),
        out_shape=block_shape,
        in_specs=[VMEM] * (n_seq + 3),
        out_specs=VMEM,
        compiler_params=PARAMS,
        cost_estimate=cost(4 * seq_len * seq_len * width, 20 * seq_len * width),
        name="value_grad",
    )(own_value, *parts, g_hi, g_lo, cross)
    grads = [value_grad] + [exchange(value_grad, "fsdp", k) for k in hops]

    here = lax.axis_index("rep")
    if n_rep == 8 and rows % 64 == 0:
        core = lax.rem(here, 2)
        chip = here // 2
        half = rows // 2
        piece = rows // 8
        count = 2
        block = half // count
        args = (features, grads, first_moment, second_moment, value_weights)
        theirs = direction_half(jnp.reshape((1 - core) * count, (1,)), count, block, *args, BF)
        arrived = exchange(theirs, "rep", 1)
        mine = direction_half(jnp.reshape(core * count, (1,)), count, block, *args, F32)
        small = jax.ShapeDtypeStruct((piece, width), BF)
        own, *sends = pl.pallas_call(
            functools.partial(split_kernel, 4),
            out_shape=(jax.ShapeDtypeStruct((piece, width), F32),) + (small,) * 3,
            in_specs=[pl.BlockSpec(memory_space=pltpu.SMEM), VMEM, VMEM],
            out_specs=(VMEM,) * 4,
            compiler_params=PARAMS,
            cost_estimate=cost(0, 10 * half * width),
            name="chip_sum",
        )(jnp.reshape(chip, (1,)), mine, arrived)
        got = [exchange(s, "rep", 2 * k) for k, s in zip((1, 2, 3), sends)]
        mean = pl.pallas_call(
            functools.partial(mean_kernel, 1.0 / n_rep),
            out_shape=small,
            in_specs=[VMEM] * 4,
            out_specs=VMEM,
            compiler_params=PARAMS,
            cost_estimate=cost(0, 10 * piece * width),
            name="mean_direction",
        )(own, *got)
        pieces = [mean] + [exchange(mean, "rep", 2 * k) for k in (1, 2, 3)]
        ordered = jnp.zeros((4, piece, width), BF)
        for k, p in enumerate(pieces):
            ordered = lax.dynamic_update_slice(ordered, p[None], (chip ^ k, 0, 0))
        ordered = ordered.reshape(half, width)
        other = exchange(ordered, "rep", 1)
        low = jnp.where(core == 0, ordered, other)
        high = jnp.where(core == 0, other, ordered)
        mean_direction = jnp.concatenate([low, high], axis=0)
    else:
        direction = direction_half(
            jnp.zeros((1,), jnp.int32), 2, rows // 2, features, grads, first_moment, second_moment,
            value_weights, F32,
        )
        mean_direction = lax.psum(direction, "rep") / n_rep

    count = 4
    blocked = pl.BlockSpec((rows // count, width), lambda i: (i, 0))
    full_shape = jax.ShapeDtypeStruct((rows, width), F32)
    new_weights, new_momentum = pl.pallas_call(
        outer_kernel,
        grid=(count,),
        out_shape=(full_shape, full_shape),
        in_specs=[blocked] * 3,
        out_specs=(blocked, blocked),
        compiler_params=PARAMS,
        cost_estimate=cost(0, 18 * rows * width),
        name="outer_step",
    )(mean_direction, momentum, value_weights)
    return (new_weights, new_momentum)


def solution(mesh):
    in_specs = (
        P(("rep", "fsdp"), None),
        P(("rep", "fsdp"), None),
        P(("rep", "fsdp"), None),
        P(("rep", "fsdp"), None),
        P("fsdp", None),
        P("fsdp", None),
        P("rep", "fsdp", None),
        P("rep", "fsdp", None),
    )
    out_specs = (P("fsdp", None), P("fsdp", None))
    return jax.shard_map(
        per_device, mesh=mesh, in_specs=in_specs, out_specs=out_specs, check_vma=False
    )
```

time: 260 us -> 86.5 us (0.33)
  waiting for transfers between devices: 208 us -> 45.7 us
  starting transfers between devices: 0.12 us -> 22.4 us
  other arithmetic: 13.3 us -> 0.17 us
  between operations: 13.9 us -> 0.86 us
  Pallas kernels: 0 us -> 12.5 us
  local copies, waits for them, and re-layouts: 16.3 us -> 4.54 us
  matrix products: 7.96 us -> 0 us
    all_gather x1 -> x0, waiting for transfers between devices: 81.5 us -> none  [per_device(): lax.all_gather(compact, 'fsdp', axis=0, tiled=True)]
    reduce_scatter x1 -> x0, waiting for transfers between devices: 67.5 us -> none  [per_device(): lax.psum_scatter(jnp.einsum('si,sc->ic', feature_cols, value_grad, prefer...]
    psum x1 -> x0, waiting for transfers between devices: 59.2 us -> none  [per_device(): mean_direction = lax.psum(direction, 'rep') / lax.axis_size('rep')]
    ppermute x0 -> x17, waiting for transfers between devices: none -> 45.7 us  [exchange(): return lax.ppermute(x, axis, [(i, partner(i, k, n)) for i in range(n)])]
    ppermute x0 -> x17, starting transfers between devices: none -> 22.4 us  [exchange(): return lax.ppermute(x, axis, [(i, partner(i, k, n)) for i in range(n)])]
    unnamed x18 -> x26, local copies, waits for them, and re-layouts: 15.6 us -> 3.03 us
    pallas_call x0 -> x10, Pallas kernels: none -> 12.5 us  [the longest x2 5.9 us: direction_half(): pl.pallas_call(functools.partial(direction_kernel, n), grid_spec=pltpu.Pr...]
    add x2 -> x0, other arithmetic: 10.5 us -> none  [the longest x1 5.28 us: per_device(): first_new / (jnp.sqrt(second_new) + epsilon) + weight_decay * value_weights]
  transfers between devices with their start and end apart: 3 -> 17, of which waited for: 3 -> 11; matrix products, arithmetic and copies ran while one was open for 5% -> 0% of each run, Pallas kernels for 0% -> 5%
where the time goes in v1:
time: 86.5 us; the launch traced here: 86.2 us
  waiting for transfers between devices  45.7 us (53%)
  starting transfers between devices  22.4 us (26%)
  Pallas kernels  12.5 us (14%)
  local copies, waits for them, and re-layouts  4.54 us (5%)
    ppermute x17, waiting for transfers between devices, exchange(): return lax.ppermute(x, axis, [(i, partner(i, k, n)) for i in range(n)])  45.7 us
    ppermute x17, starting transfers between devices, exchange(): return lax.ppermute(x, axis, [(i, partner(i, k, n)) for i in range(n)])  22.4 us
    pallas_call x2, Pallas kernels, direction_half(): pl.pallas_call(functools.partial(direction_kernel, n), grid_spec=pltpu.Pr...  5.9 us
    unnamed x26, local copies, waits for them, and re-layouts  3.03 us
    pallas_call x1, Pallas kernels, per_device(): pl.pallas_call(outer_kernel, grid=(count,), out_shape=(full_shape, full_s...  2.43 us
  transfers between devices with their start and end apart: 17, of which 11 were waited for; matrix products, arithmetic and copies ran while one was open for 0% of the time, Pallas kernels for 5%

profile of v1, /device:TPU:0, one launch (start us, length us, event | category | flops | bytes accessed | tf_op | source)
XLA Modules:
  0.0 86.2 jit_solution(9874112722045235312)
XLA Ops:
  0.6 0.0 copy-start
  0.7 1.4 %constant_dynamic-slice_fusion = (bf16[128,1024]{1,0:T(8,128)(2,1)S(1)}, bf16[128,1024]{1,0:T(8,128)(2,1)S(1)}, bf16[128,1024]{1,0:T(8,128)(2,1)S(1)}, bf16[128,1024]{1,0:T(8,128)(2,1)S(1)}) fusion(bf16[128,4096]{1,0:T(8,128)(2,1)} %param.8, s32[]{:T(128)S(6)} %select_n.46, s32[]{:T(128)S(6)} %select_n.44, s32[]{:T(128)S(6)} %select_n.43, s32[]{:T(128)S(6)} %select_n.45), kind=kLoop, calls=%fused_computation.7 | loop fusion | bytes 2097168 | tf_op jit(solution)/shard_map/dynamic_slice | solution.py:188
  2.1 5.1 %collective-permute-start.2 = (bf16[128,1024]{1,0:T(8,128)(2,1)S(1)}, bf16[128,1024]{1,0:T(8,128)(2,1)S(1)}, u32[]{:S(2)}, u32[]{:S(2)}) collective-permute-start(bf16[128,1024]{1,0:T(8,128)(2,1)S(1)} %get-tuple-element.28), channel_id=1, source_target_pairs={{0,3},{1,2},{2,1},{3,0},{4,7},{5,6},{6,5},{7,4},{8,11},{9,10},{10,... | collective-permute-start | bytes 786440 | tf_op jit(solution)/shard_map/ppermute | solution.py:169
  7.2 0.6 collective-permute-start.1
  7.8 0.4 own_value.1
  8.2 6.2 %collective-permute-done.2.refs_3_.refs_2_ = bf16[128,1024]{1,0:T(8,128)(2,1)S(1)} collective-permute-done((bf16[128,1024]{1,0:T(8,128)(2,1)S(1)}, bf16[128,1024]{1,0:T(8,128)(2,1)S(1)}, u32[]{:S(2)}, u32[]{:S(2)}) %collective-permute-start.2) | collective-permute-done | bytes 262176 | tf_op jit(solution)/shard_map/ppermute | solution.py:169
  14.4 5.8 %collective-permute-done.refs_1_.refs_0_ = bf16[128,1024]{1,0:T(8,128)(2,1)S(1)} collective-permute-done((bf16[128,1024]{1,0:T(8,128)(2,1)S(1)}, bf16[128,1024]{1,0:T(8,128)(2,1)S(1)}, u32[]{:S(2)}, u32[]{:S(2)}) %collective-permute-start) | collective-permute-done | bytes 262176 | tf_op jit(solution)/shard_map/ppermute | solution.py:169
  20.3 9.2 %collective-permute-done.1.refs_2_.refs_1_ = bf16[128,1024]{1,0:T(8,128)(2,1)S(1)} collective-permute-done((bf16[128,1024]{1,0:T(8,128)(2,1)S(1)}, bf16[128,1024]{1,0:T(8,128)(2,1)S(1)}, u32[]{:S(2)}, u32[]{:S(2)}) %collective-permute-start.1) | collective-permute-done | bytes 262176 | tf_op jit(solution)/shard_map/ppermute | solution.py:169
  29.5 0.6 partial_values.1
  30.1 0.1 collective-permute-start.3
  30.2 3.0 %collective-permute-start.4 = (bf16[128,512]{1,0:T(8,128)(2,1)S(1)}, bf16[128,512]{1,0:T(8,128)(2,1)S(1)}, u32[]{:S(2)}, u32[]{:S(2)}) collective-permute-start(bf16[128,512]{1,0:T(8,128)(2,1)S(1)} %get-tuple-element.17), channel_id=1, source_target_pairs={{0,2},{1,3},{2,0},{3,1},{4,6},{5,7},{6,4},{7,5},{8,10},{9,11},{10,... | collective-permute-start | bytes 393224 | tf_op jit(solution)/shard_map/ppermute | solution.py:169
  33.2 1.4 %collective-permute-start.5 = (bf16[128,512]{1,0:T(8,128)(2,1)S(1)}, bf16[128,512]{1,0:T(8,128)(2,1)S(1)}, u32[]{:S(2)}, u32[]{:S(2)}) collective-permute-start(bf16[128,512]{1,0:T(8,128)(2,1)S(1)} %get-tuple-element.18), channel_id=1, source_target_pairs={{0,3},{1,2},{2,1},{3,0},{4,7},{5,6},{6,5},{7,4},{8,11},{9,10},{10,... | collective-permute-start | bytes 393224 | tf_op jit(solution)/shard_map/ppermute | solution.py:169
  34.6 1.4 %attention.1 = (bf16[128,512]{1,0:T(8,128)(2,1)S(1)}, bf16[128,512]{1,0:T(8,128)(2,1)S(1)}, f32[128,512]{1,0:T(8,128)S(1)}) custom-call(bf16[128,2048]{1,0:T(8,128)(2,1)S(1)} %copy-done.10, bf16[128,512]{1,0:T(8,128)(2,1)S(1)} %copy-done.12, bf16[128,2048]{1,0:T(8,128)(2,1)S(1)} %copy-done.11), custom_call_target="tpu_custom_call" | custom-call | flops 201326592 | bytes 1048576 | tf_op jit(solution)/shard_map/attention/pallas_call | solution.py:198
  36.1 0.4 collective-permute-done.3.refs_1_
  36.5 6.2 %collective-permute-done.4.refs_2_ = bf16[128,512]{1,0:T(8,128)(2,1)S(1)} collective-permute-done((bf16[128,512]{1,0:T(8,128)(2,1)S(1)}, bf16[128,512]{1,0:T(8,128)(2,1)S(1)}, u32[]{:S(2)}, u32[]{:S(2)}) %collective-permute-start.4) | collective-permute-done | bytes 131104 | tf_op jit(solution)/shard_map/ppermute | solution.py:169
  42.8 0.0 collective-permute-done.5.refs_3_
  42.8 0.2 value_grad.1.refs_0_
  43.0 2.4 %collective-permute-start.8 = (bf16[128,512]{1,0:T(8,128)(2,1)S(1)}, bf16[128,512]{1,0:T(8,128)(2,1)}, u32[]{:S(2)}, u32[]{:S(2)}) collective-permute-start(bf16[128,512]{1,0:T(8,128)(2,1)S(1)} %value_grad.1.refs_0_), channel_id=1, source_target_pairs={{0,3},{1,2},{2,1},{3,0},{4,7},{5,6},{6,5},{7,4},{8,11},{9,10},{10,... | collective-permute-start | bytes 393224 | tf_op jit(solution)/shard_map/ppermute | solution.py:169
  45.4 2.6 %collective-permute-start.7 = (bf16[128,512]{1,0:T(8,128)(2,1)S(1)}, bf16[128,512]{1,0:T(8,128)(2,1)}, u32[]{:S(2)}, u32[]{:S(2)}) collective-permute-start(bf16[128,512]{1,0:T(8,128)(2,1)S(1)} %value_grad.1.refs_0_), channel_id=1, source_target_pairs={{0,2},{1,3},{2,0},{3,1},{4,6},{5,7},{6,4},{7,5},{8,10},{9,11},{10,... | collective-permute-start | bytes 393224 | tf_op jit(solution)/shard_map/ppermute | solution.py:169
  47.9 0.1 collective-permute-start.6
  48.0 0.9 %copy-done.5 = bf16[128,1024]{1,0:T(8,128)(2,1)S(1)} copy-done((bf16[128,1024]{1,0:T(8,128)(2,1)S(1)}, bf16[128,1024]{1,0:T(8,128)(2,1)}, u32[]{:S(2)}) %copy-start.5) | copy-done | bytes 262168
  49.0 0.9 %copy-done.7 = bf16[128,1024]{1,0:T(8,128)(2,1)S(1)} copy-done((bf16[128,1024]{1,0:T(8,128)(2,1)S(1)}, bf16[128,1024]{1,0:T(8,128)(2,1)}, u32[]{:S(2)}) %copy-start.7) | copy-done | bytes 262168
  49.9 0.9 %copy-done.9 = bf16[128,1024]{1,0:T(8,128)(2,1)S(1)} copy-done((bf16[128,1024]{1,0:T(8,128)(2,1)S(1)}, bf16[128,1024]{1,0:T(8,128)(2,1)}, u32[]{:S(2)}) %copy-start.9) | copy-done | bytes 262168
  50.9 0.3 transpose_tokens.1.features
  51.2 0.2 collective-permute-done.8.refs_3_
  51.4 4.1 %collective-permute-done.7.refs_2_ = bf16[128,512]{1,0:T(8,128)(2,1)} collective-permute-done((bf16[128,512]{1,0:T(8,128)(2,1)S(1)}, bf16[128,512]{1,0:T(8,128)(2,1)}, u32[]{:S(2)}, u32[]{:S(2)}) %collective-permute-start.7) | collective-permute-done | bytes 131104 | tf_op jit(solution)/shard_map/ppermute | solution.py:169
  55.5 3.3 %direction.3 = bf16[512,512]{1,0:T(8,128)(2,1)} custom-call(s32[1]{0:T(128)} %bitcast.2.start, bf16[1024,512]{1,0:T(8,128)(2,1)S(1)} %transpose_tokens.1.features, bf16[128,512]{1,0:T(8,128)(2,1)S(1)} %value_grad.1.refs_0_, bf16[128,512]{1,0:T(8,128)(2,1)} %collective-permute-done.6.refs_1_, bf16[128,512]{1,0:T(8,128)(2,1)} %collective-permute-done.7.refs_2_, ...), custom_call_target="tpu_custom_call" | custom-call | flops 268435456 | bytes 4194304 | tf_op jit(solution)/shard_map/direction/pallas_call | solution.py:117
  58.8 0.0 collective-permute-start.9
  58.8 2.6 %direction.2.mine = f32[512,512]{1,0:T(8,128)S(1)} custom-call(s32[1]{0:T(128)} %bitcast.1.start, bf16[1024,512]{1,0:T(8,128)(2,1)S(1)} %transpose_tokens.1.features, bf16[128,512]{1,0:T(8,128)(2,1)S(1)} %value_grad.1.refs_0_, bf16[128,512]{1,0:T(8,128)(2,1)} %collective-permute-done.6.refs_1_, bf16[128,512]{1,0:T(8,128)(2,1)} %collective-permute-done.7.refs_2_, ...), custom_call_target="tpu_custom_call" | custom-call | flops 268435456 | bytes 4194304 | tf_op jit(solution)/shard_map/direction/pallas_call | solution.py:117
  61.4 1.1 %chip_sum.1 = (f32[128,512]{1,0:T(8,128)S(1)}, bf16[128,512]{1,0:T(8,128)(2,1)S(1)}, bf16[128,512]{1,0:T(8,128)(2,1)S(1)}, bf16[128,512]{1,0:T(8,128)(2,1)S(1)}) custom-call(s32[1]{0:T(128)} %bitcast.where, f32[512,512]{1,0:T(8,128)S(1)} %direction.2.mine, bf16[512,512]{1,0:T(8,128)(2,1)} %collective-permute-done.9.theirs), custom_call_target="tpu_custom_call" | custom-call | bytes 2621440 | tf_op jit(solution)/shard_map/chip_sum/pallas_call | solution.py:260
  62.6 1.6 %collective-permute-start.10 = (bf16[128,512]{1,0:T(8,128)(2,1)S(1)}, bf16[128,512]{1,0:T(8,128)(2,1)S(1)}, u32[]{:S(2)}, u32[]{:S(2)}) collective-permute-start(bf16[128,512]{1,0:T(8,128)(2,1)S(1)} %get-tuple-element.23), channel_id=1, source_target_pairs={{0,8},{4,12},{8,0},{12,4},{16,24},{20,28},{24,16},{28,20},{1,9},{5... | collective-permute-start | bytes 393224 | tf_op jit(solution)/shard_map/ppermute | solution.py:169
  64.1 1.5 %collective-permute-start.11 = (bf16[128,512]{1,0:T(8,128)(2,1)S(1)}, bf16[128,512]{1,0:T(8,128)(2,1)S(1)}, u32[]{:S(2)}, u32[]{:S(2)}) collective-permute-start(bf16[128,512]{1,0:T(8,128)(2,1)S(1)} %get-tuple-element.24), channel_id=1, source_target_pairs={{0,16},{4,20},{8,24},{12,28},{16,0},{20,4},{24,8},{28,12},{1,17},{... | collective-permute-start | bytes 393224 | tf_op jit(solution)/shard_map/ppermute | solution.py:169
  65.6 0.5 collective-permute-start.12
  66.1 2.8 %collective-permute-done.10.refs_0_ = bf16[128,512]{1,0:T(8,128)(2,1)S(1)} collective-permute-done((bf16[128,512]{1,0:T(8,128)(2,1)S(1)}, bf16[128,512]{1,0:T(8,128)(2,1)S(1)}, u32[]{:S(2)}, u32[]{:S(2)}) %collective-permute-start.10) | collective-permute-done | bytes 131104 | tf_op jit(solution)/shard_map/ppermute | solution.py:169
  68.9 3.6 %collective-permute-done.11.refs_1_ = bf16[128,512]{1,0:T(8,128)(2,1)S(1)} collective-permute-done((bf16[128,512]{1,0:T(8,128)(2,1)S(1)}, bf16[128,512]{1,0:T(8,128)(2,1)S(1)}, u32[]{:S(2)}, u32[]{:S(2)}) %collective-permute-start.11) | collective-permute-done | bytes 131104 | tf_op jit(solution)/shard_map/ppermute | solution.py:169
  72.6 0.1 mean_direction.1
  72.6 1.6 %collective-permute-start.15 = (bf16[128,512]{1,0:T(8,128)(2,1)S(1)}, bf16[128,512]{1,0:T(8,128)(2,1)S(1)}, u32[]{:S(2)}, u32[]{:S(2)}) collective-permute-start(bf16[128,512]{1,0:T(8,128)(2,1)S(1)} %mean_direction.1), channel_id=1, source_target_pairs={{0,24},{4,28},{8,16},{12,20},{16,8},{20,12},{24,0},{28,4},{1,25},{... | collective-permute-start | bytes 393224 | tf_op jit(solution)/shard_map/ppermute | solution.py:169
  74.2 1.2 %collective-permute-start.14 = (bf16[128,512]{1,0:T(8,128)(2,1)S(1)}, bf16[128,512]{1,0:T(8,128)(2,1)S(1)}, u32[]{:S(2)}, u32[]{:S(2)}) collective-permute-start(bf16[128,512]{1,0:T(8,128)(2,1)S(1)} %mean_direction.1), channel_id=1, source_target_pairs={{0,16},{4,20},{8,24},{12,28},{16,0},{20,4},{24,8},{28,12},{1,17},{... | collective-permute-start | bytes 393224 | tf_op jit(solution)/shard_map/ppermute | solution.py:169
  75.4 0.8 collective-permute-start.13
  76.3 5.1 %collective-permute-done.13 = bf16[128,512]{1,0:T(8,128)(2,1)S(1)} collective-permute-done((bf16[128,512]{1,0:T(8,128)(2,1)S(1)}, bf16[128,512]{1,0:T(8,128)(2,1)S(1)}, u32[]{:S(2)}, u32[]{:S(2)}) %collective-permute-start.13) | collective-permute-done | bytes 131104 | tf_op jit(solution)/shard_map/ppermute | solution.py:169
  81.4 0.1 collective-permute-start.16
  81.5 0.0 copy-start.1
  81.5 0.0 copy-start.3
  81.5 1.9 %collective-permute-done.16 = bf16[512,512]{1,0:T(8,128)(2,1)S(1)} collective-permute-done((bf16[512,512]{1,0:T(8,128)(2,1)S(1)}, bf16[512,512]{1,0:T(8,128)(2,1)S(1)}, u32[]{:S(2)}, u32[]{:S(2)}) %collective-permute-start.16) | collective-permute-done | bytes 524320 | tf_op jit(solution)/shard_map/ppermute | solution.py:169
  83.4 0.1 broadcast_select_fusion.1
  83.5 0.1 pad_maximum_fusion.mean
  83.6 0.1 copy-done.3
  83.7 2.4 %outer_step.1 = (f32[1024,512]{1,0:T(8,128)}, f32[1024,512]{1,0:T(8,128)}) custom-call(bf16[1024,512]{1,0:T(8,128)(2,1)S(1)} %pad_maximum_fusion.mean, f32[1024,512]{1,0:T(8,128)S(1)} %copy-done.3, f32[1024,512]{1,0:T(8,128)S(1)} %copy-done.1), custom_call_target="tpu_custom_call" | custom-call | bytes 9437184 | tf_op jit(solution)/shard_map/outer_step/pallas_call | solution.py:298
  (30 shorter events, 0.1 us)
Async XLA Ops:
  0.6 7.2 %copy-start = (f32[1024,512]{1,0:T(8,128)S(1)}, f32[1024,512]{1,0:T(8,128)}, u32[]{:S(2)}) copy-start(f32[1024,512]{1,0:T(8,128)} %weights.3) | copy-start | bytes 6291460
  2.1 12.3 %collective-permute-start.2 = (bf16[128,1024]{1,0:T(8,128)(2,1)S(1)}, bf16[128,1024]{1,0:T(8,128)(2,1)S(1)}, u32[]{:S(2)}, u32[]{:S(2)}) collective-permute-start(bf16[128,1024]{1,0:T(8,128)(2,1)S(1)} %get-tuple-element.28), channel_id=1, source_target_pairs={{0,3},{1,2},{2,1},{3,0},{4,7},{5,6},{6,5},{7,4},{8,11},{9,10},{10,... | collective-permute-start | bytes 786440 | tf_op jit(solution)/shard_map/ppermute | solution.py:169
  7.2 13.1 %collective-permute-start = (bf16[128,1024]{1,0:T(8,128)(2,1)S(1)}, bf16[128,1024]{1,0:T(8,128)(2,1)S(1)}, u32[]{:S(2)}, u32[]{:S(2)}) collective-permute-start(bf16[128,1024]{1,0:T(8,128)(2,1)S(1)} %get-tuple-element.29), channel_id=1, source_target_pairs={{0,1},{1,0},{2,3},{3,2},{4,5},{5,4},{6,7},{7,6},{8,9},{9,8},{10,11... | collective-permute-start | bytes 786440 | tf_op jit(solution)/shard_map/ppermute | solution.py:169
  7.2 22.3 %collective-permute-start.1 = (bf16[128,1024]{1,0:T(8,128)(2,1)S(1)}, bf16[128,1024]{1,0:T(8,128)(2,1)S(1)}, u32[]{:S(2)}, u32[]{:S(2)}) collective-permute-start(bf16[128,1024]{1,0:T(8,128)(2,1)S(1)} %get-tuple-element.31), channel_id=1, source_target_pairs={{0,2},{1,3},{2,0},{3,1},{4,6},{5,7},{6,4},{7,5},{8,10},{9,11},{10,... | collective-permute-start | bytes 786440 | tf_op jit(solution)/shard_map/ppermute | solution.py:169
  7.8 26.8 %copy-start.10 = (bf16[128,2048]{1,0:T(8,128)(2,1)S(1)}, bf16[128,2048]{1,0:T(8,128)(2,1)}, u32[]{:S(2)}) copy-start(bf16[128,2048]{1,0:T(8,128)(2,1)} %queries.1) | copy-start | bytes 1572868
  7.8 26.8 %copy-start.11 = (bf16[128,2048]{1,0:T(8,128)(2,1)S(1)}, bf16[128,2048]{1,0:T(8,128)(2,1)}, u32[]{:S(2)}) copy-start(bf16[128,2048]{1,0:T(8,128)(2,1)} %targets.1) | copy-start | bytes 1572868
  7.8 26.8 %copy-start.12 = (bf16[128,512]{1,0:T(8,128)(2,1)S(1)}, bf16[128,512]{1,0:T(8,128)(2,1)}, u32[]{:S(2)}) copy-start(bf16[128,512]{1,0:T(8,128)(2,1)} %keys.1) | copy-start | bytes 393220
  14.4 18.8 %copy-start.4 = (bf16[128,1024]{1,0:T(8,128)(2,1)}, bf16[128,1024]{1,0:T(8,128)(2,1)S(1)}, u32[]{:S(2)}) copy-start(bf16[128,1024]{1,0:T(8,128)(2,1)S(1)} %collective-permute-done.2.refs_3_.refs_2_) | copy-start | bytes 786436
  20.3 12.9 %copy-start.6 = (bf16[128,1024]{1,0:T(8,128)(2,1)}, bf16[128,1024]{1,0:T(8,128)(2,1)S(1)}, u32[]{:S(2)}) copy-start(bf16[128,1024]{1,0:T(8,128)(2,1)S(1)} %collective-permute-done.refs_1_.refs_0_) | copy-start | bytes 786436
  29.5 3.7 %copy-start.8 = (bf16[128,1024]{1,0:T(8,128)(2,1)}, bf16[128,1024]{1,0:T(8,128)(2,1)S(1)}, u32[]{:S(2)}) copy-start(bf16[128,1024]{1,0:T(8,128)(2,1)S(1)} %collective-permute-done.1.refs_2_.refs_1_) | copy-start | bytes 786436
  30.1 6.4 %collective-permute-start.3 = (bf16[128,512]{1,0:T(8,128)(2,1)S(1)}, bf16[128,512]{1,0:T(8,128)(2,1)S(1)}, u32[]{:S(2)}, u32[]{:S(2)}) collective-permute-start(bf16[128,512]{1,0:T(8,128)(2,1)S(1)} %get-tuple-element.16), channel_id=1, source_target_pairs={{0,1},{1,0},{2,3},{3,2},{4,5},{5,4},{6,7},{7,6},{8,9},{9,8},{10,11... | collective-permute-start | bytes 393224 | tf_op jit(solution)/shard_map/ppermute | solution.py:169
  30.2 12.6 %collective-permute-start.4 = (bf16[128,512]{1,0:T(8,128)(2,1)S(1)}, bf16[128,512]{1,0:T(8,128)(2,1)S(1)}, u32[]{:S(2)}, u32[]{:S(2)}) collective-permute-start(bf16[128,512]{1,0:T(8,128)(2,1)S(1)} %get-tuple-element.17), channel_id=1, source_target_pairs={{0,2},{1,3},{2,0},{3,1},{4,6},{5,7},{6,4},{7,5},{8,10},{9,11},{10,... | collective-permute-start | bytes 393224 | tf_op jit(solution)/shard_map/ppermute | solution.py:169
  33.2 22.3 %copy-start.2 = (f32[1,1024,512]{2,1,0:T(8,128)S(1)}, f32[1,1024,512]{2,1,0:T(8,128)}, u32[]{:S(2)}) copy-start(f32[1,1024,512]{2,1,0:T(8,128)} %refs_4_.3) | copy-start | bytes 6291460
  33.2 9.5 %collective-permute-start.5 = (bf16[128,512]{1,0:T(8,128)(2,1)S(1)}, bf16[128,512]{1,0:T(8,128)(2,1)S(1)}, u32[]{:S(2)}, u32[]{:S(2)}) collective-permute-start(bf16[128,512]{1,0:T(8,128)(2,1)S(1)} %get-tuple-element.18), channel_id=1, source_target_pairs={{0,3},{1,2},{2,1},{3,0},{4,7},{5,6},{6,5},{7,4},{8,11},{9,10},{10,... | collective-permute-start | bytes 393224 | tf_op jit(solution)/shard_map/ppermute | solution.py:169
  43.0 8.4 %collective-permute-start.8 = (bf16[128,512]{1,0:T(8,128)(2,1)S(1)}, bf16[128,512]{1,0:T(8,128)(2,1)}, u32[]{:S(2)}, u32[]{:S(2)}) collective-permute-start(bf16[128,512]{1,0:T(8,128)(2,1)S(1)} %value_grad.1.refs_0_), channel_id=1, source_target_pairs={{0,3},{1,2},{2,1},{3,0},{4,7},{5,6},{6,5},{7,4},{8,11},{9,10},{10,... | collective-permute-start | bytes 393224 | tf_op jit(solution)/shard_map/ppermute | solution.py:169
  45.4 10.1 %collective-permute-start.7 = (bf16[128,512]{1,0:T(8,128)(2,1)S(1)}, bf16[128,512]{1,0:T(8,128)(2,1)}, u32[]{:S(2)}, u32[]{:S(2)}) collective-permute-start(bf16[128,512]{1,0:T(8,128)(2,1)S(1)} %value_grad.1.refs_0_), channel_id=1, source_target_pairs={{0,2},{1,3},{2,0},{3,1},{4,6},{5,7},{6,4},{7,5},{8,10},{9,11},{10,... | collective-permute-start | bytes 393224 | tf_op jit(solution)/shard_map/ppermute | solution.py:169
  47.9 7.6 %collective-permute-start.6 = (bf16[128,512]{1,0:T(8,128)(2,1)S(1)}, bf16[128,512]{1,0:T(8,128)(2,1)}, u32[]{:S(2)}, u32[]{:S(2)}) collective-permute-start(bf16[128,512]{1,0:T(8,128)(2,1)S(1)} %value_grad.1.refs_0_), channel_id=1, source_target_pairs={{0,1},{1,0},{2,3},{3,2},{4,5},{5,4},{6,7},{7,6},{8,9},{9,8},{10,11... | collective-permute-start | bytes 393224 | tf_op jit(solution)/shard_map/ppermute | solution.py:169
  48.0 0.9 %copy-start.5 = (bf16[128,1024]{1,0:T(8,128)(2,1)S(1)}, bf16[128,1024]{1,0:T(8,128)(2,1)}, u32[]{:S(2)}) copy-start(bf16[128,1024]{1,0:T(8,128)(2,1)} %copy-done.4) | copy-start | bytes 786436
  49.0 0.9 %copy-start.7 = (bf16[128,1024]{1,0:T(8,128)(2,1)S(1)}, bf16[128,1024]{1,0:T(8,128)(2,1)}, u32[]{:S(2)}) copy-start(bf16[128,1024]{1,0:T(8,128)(2,1)} %copy-done.6) | copy-start | bytes 786436
  49.9 0.9 %copy-start.9 = (bf16[128,1024]{1,0:T(8,128)(2,1)S(1)}, bf16[128,1024]{1,0:T(8,128)(2,1)}, u32[]{:S(2)}) copy-start(bf16[128,1024]{1,0:T(8,128)(2,1)} %copy-done.8) | copy-start | bytes 786436
  58.8 2.6 %collective-permute-start.9 = (bf16[512,512]{1,0:T(8,128)(2,1)}, bf16[512,512]{1,0:T(8,128)(2,1)}, u32[]{:S(2)}, u32[]{:S(2)}) collective-permute-start(bf16[512,512]{1,0:T(8,128)(2,1)} %direction.3), channel_id=1, source_target_pairs={{0,4},{4,0},{8,12},{12,8},{16,20},{20,16},{24,28},{28,24},{1,5},{5... | collective-permute-start | bytes 1572872 | tf_op jit(solution)/shard_map/ppermute | solution.py:169
  62.6 6.4 %collective-permute-start.10 = (bf16[128,512]{1,0:T(8,128)(2,1)S(1)}, bf16[128,512]{1,0:T(8,128)(2,1)S(1)}, u32[]{:S(2)}, u32[]{:S(2)}) collective-permute-start(bf16[128,512]{1,0:T(8,128)(2,1)S(1)} %get-tuple-element.23), channel_id=1, source_target_pairs={{0,8},{4,12},{8,0},{12,4},{16,24},{20,28},{24,16},{28,20},{1,9},{5... | collective-permute-start | bytes 393224 | tf_op jit(solution)/shard_map/ppermute | solution.py:169
  64.1 8.4 %collective-permute-start.11 = (bf16[128,512]{1,0:T(8,128)(2,1)S(1)}, bf16[128,512]{1,0:T(8,128)(2,1)S(1)}, u32[]{:S(2)}, u32[]{:S(2)}) collective-permute-start(bf16[128,512]{1,0:T(8,128)(2,1)S(1)} %get-tuple-element.24), channel_id=1, source_target_pairs={{0,16},{4,20},{8,24},{12,28},{16,0},{20,4},{24,8},{28,12},{1,17},{... | collective-permute-start | bytes 393224 | tf_op jit(solution)/shard_map/ppermute | solution.py:169
  65.6 6.9 %collective-permute-start.12 = (bf16[128,512]{1,0:T(8,128)(2,1)S(1)}, bf16[128,512]{1,0:T(8,128)(2,1)S(1)}, u32[]{:S(2)}, u32[]{:S(2)}) collective-permute-start(bf16[128,512]{1,0:T(8,128)(2,1)S(1)} %get-tuple-element.25), channel_id=1, source_target_pairs={{0,24},{4,28},{8,16},{12,20},{16,8},{20,12},{24,0},{28,4},{1,25},{... | collective-permute-start | bytes 393224 | tf_op jit(solution)/shard_map/ppermute | solution.py:169
  72.6 8.8 %collective-permute-start.15 = (bf16[128,512]{1,0:T(8,128)(2,1)S(1)}, bf16[128,512]{1,0:T(8,128)(2,1)S(1)}, u32[]{:S(2)}, u32[]{:S(2)}) collective-permute-start(bf16[128,512]{1,0:T(8,128)(2,1)S(1)} %mean_direction.1), channel_id=1, source_target_pairs={{0,24},{4,28},{8,16},{12,20},{16,8},{20,12},{24,0},{28,4},{1,25},{... | collective-permute-start | bytes 393224 | tf_op jit(solution)/shard_map/ppermute | solution.py:169
  74.2 7.2 %collective-permute-start.14 = (bf16[128,512]{1,0:T(8,128)(2,1)S(1)}, bf16[128,512]{1,0:T(8,128)(2,1)S(1)}, u32[]{:S(2)}, u32[]{:S(2)}) collective-permute-start(bf16[128,512]{1,0:T(8,128)(2,1)S(1)} %mean_direction.1), channel_id=1, source_target_pairs={{0,16},{4,20},{8,24},{12,28},{16,0},{20,4},{24,8},{28,12},{1,17},{... | collective-permute-start | bytes 393224 | tf_op jit(solution)/shard_map/ppermute | solution.py:169
  75.4 6.0 %collective-permute-start.13 = (bf16[128,512]{1,0:T(8,128)(2,1)S(1)}, bf16[128,512]{1,0:T(8,128)(2,1)S(1)}, u32[]{:S(2)}, u32[]{:S(2)}) collective-permute-start(bf16[128,512]{1,0:T(8,128)(2,1)S(1)} %mean_direction.1), channel_id=1, source_target_pairs={{0,8},{4,12},{8,0},{12,4},{16,24},{20,28},{24,16},{28,20},{1,9},{5... | collective-permute-start | bytes 393224 | tf_op jit(solution)/shard_map/ppermute | solution.py:169
  81.4 2.0 %collective-permute-start.16 = (bf16[512,512]{1,0:T(8,128)(2,1)S(1)}, bf16[512,512]{1,0:T(8,128)(2,1)S(1)}, u32[]{:S(2)}, u32[]{:S(2)}) collective-permute-start(bf16[512,512]{1,0:T(8,128)(2,1)S(1)} %bitcast.14), channel_id=1, source_target_pairs={{0,4},{4,0},{8,12},{12,8},{16,20},{20,16},{24,28},{28,24},{1,5},{5... | collective-permute-start | bytes 1572872 | tf_op jit(solution)/shard_map/ppermute | solution.py:169
  81.5 2.1 %copy-start.1 = (f32[1024,512]{1,0:T(8,128)S(1)}, f32[1024,512]{1,0:T(8,128)}, u32[]{:S(2)}) copy-start(f32[1024,512]{1,0:T(8,128)} %weights.3) | copy-start | bytes 6291460
  81.5 2.2 %copy-start.3 = (f32[1024,512]{1,0:T(8,128)S(1)}, f32[1024,512]{1,0:T(8,128)}, u32[]{:S(2)}) copy-start(f32[1024,512]{1,0:T(8,128)} %momentum.1) | copy-start | bytes 6291460

commit v2 on v1

--- a/solution.py
+++ b/solution.py
@@ -23,7 +23,9 @@
 BF = jnp.bfloat16
 F32 = jnp.float32
 VMEM = pl.BlockSpec(memory_space=pltpu.VMEM)
-PARAMS = pltpu.CompilerParams(vmem_limit_bytes=48 * 1024 * 1024)
+ANY = pl.BlockSpec(memory_space=pl.ANY)
+SMEM = pl.BlockSpec(memory_space=pltpu.SMEM)
+PARAMS = pltpu.CompilerParams(vmem_limit_bytes=12 * 1024 * 1024)
 
 
 def cost(flops, nbytes):
@@ -77,6 +79,28 @@
         out[:, k * seq : (k + 1) * seq] = block[...].T
 
 
+def local(kernel, shapes, *args, flops=0, name):
+    specs = [SMEM if a.dtype == jnp.int32 else VMEM for a in args]
+    nbytes = sum(a.size * a.dtype.itemsize for a in (*args, *shapes))
+    return pl.pallas_call(
+        kernel,
+        out_shape=tuple(shapes),
+        in_specs=specs,
+        out_specs=(VMEM,) * len(shapes),
+        compiler_params=PARAMS,
+        cost_estimate=cost(flops, nbytes),
+        name=name,
+    )(*args)
+
+
+def after(values, *first):
+    return lax.optimization_barrier((values, first))[0]
+
+
+def to_chips(sends):
+    return [exchange(s, "rep", 2 * k) for k, s in zip((1, 2, 3), sends)]
+
+
 def value_grad_kernel(n, scale, *refs):
     own, parts = refs[0], refs[1:n]
     g_hi, g_lo, cross, out = refs[n:]
@@ -90,57 +114,49 @@
         out[:, cols] = ((acc - cross[:, cols]) * scale).astype(BF)
 
 
-def direction_kernel(n, start, features, *refs):
+def direction_of(features, stacked, first, second, weights, at):
+    summed = dot(features[at, :], stacked)
+    first_new = first_decay * first[0, at, :] + (1.0 - first_decay) / math.sqrt(D) * summed
+    second_new = second_decay * second[0, at, :] + (1.0 - second_decay) / D * summed * summed
+    return first_new / (jnp.sqrt(second_new) + epsilon) + weight_decay * weights[at, :]
+
+
+def rows_at(start, count):
+    return pl.ds(pl.multiple_of(start, count), count)
+
+
+def first_row(ids, other, offset, half):
+    core = lax.rem(ids[1], 2)
+    return (1 - core if other else core) * half + offset
+
+
+def half_kernel(n, rows, other, ids, features, *refs):
     grads = refs[:n]
-    first, second, weights, out, stacked = refs[n:]
-    seq = grads[0].shape[0]
-
-    @pl.when(pl.program_id(0) == 0)
-    def _():
-        for k, grad in enumerate(grads):
-            stacked[k * seq : (k + 1) * seq, :] = grad[...]
-
-    gradient = dot(features[...], stacked[...]) * (1.0 / math.sqrt(D))
-    first_new = first_decay * first[0] + (1.0 - first_decay) * gradient
-    second_new = second_decay * second[0] + (1.0 - second_decay) * gradient * gradient
-    direction = first_new / (jnp.sqrt(second_new) + epsilon) + weight_decay * weights[...]
-    out[...] = direction.astype(out.dtype)
-
-
-def direction_half(start, count, block, features, grads, first, second, weights, dtype):
-    n = len(grads)
-    width = weights.shape[1]
-    seqs = features.shape[1]
-    full = pl.BlockSpec((grads[0].shape[0], width), lambda i, s: (0, 0))
-    moment = pl.BlockSpec((1, block, width), lambda i, s: (0, s[0] + i, 0))
-    rows = count * block
-    return pl.pallas_call(
-        functools.partial(direction_kernel, n),
-        grid_spec=pltpu.PrefetchScalarGridSpec(
-            num_scalar_prefetch=1,
-            grid=(count,),
-            in_specs=[pl.BlockSpec((block, seqs), lambda i, s: (s[0] + i, 0))]
-            + [full] * n
-            + [moment, moment, pl.BlockSpec((block, width), lambda i, s: (s[0] + i, 0))],
-            out_specs=pl.BlockSpec((block, width), lambda i, s: (i, 0)),
-            scratch_shapes=[pltpu.VMEM((seqs, width), BF)],
-        ),
-        out_shape=jax.ShapeDtypeStruct((rows, width), dtype),
-        compiler_params=PARAMS,
-        cost_estimate=cost(2 * rows * seqs * width, rows * width * 16),
-        name="direction",
-    )(start, features, *grads, first, second, weights)
-
-
-def split_kernel(n, where, mine, theirs, own, *outs):
+    first, second, weights, out = refs[n:]
+    stacked = jnp.concatenate([g[...] for g in grads], axis=0)
+    start = first_row(ids, other, 0, weights.shape[0] // 2)
+    for i in range(0, out.shape[0], rows):
+        at = rows_at(start + i, rows)
+        total = direction_of(features, stacked, first, second, weights, at)
+        out[i : i + rows, :] = total.astype(out.dtype)
+
+
+def split_kernel(ids, mine, theirs, own, *outs):
     rows = own.shape[0]
-    for k in range(n):
-        at = pl.ds(pl.multiple_of((where[0] ^ k) * rows, rows), rows)
+    for k in range(len(outs) + 1):
+        at = rows_at((ids[1] // 2 ^ k) * rows, rows)
         total = mine[at, :] + theirs[at, :].astype(F32)
         if k == 0:
             own[...] = total
         else:
             outs[k - 1][...] = total.astype(BF)
+
+
+def direction_kernel(n, features, *refs):
+    grads = refs[:n]
+    first, second, weights, out = refs[n:]
+    stacked = jnp.concatenate([g[...] for g in grads], axis=0)
+    out[...] = direction_of(features, stacked, first, second, weights, slice(None))
 
 
 def mean_kernel(inv, own, *refs):
@@ -158,6 +174,51 @@
     new_weights[...] = weights[...] - outer_rate * inner_rate * (
         mean_direction + momentum_keep * kept
     )
+
+
+def stack_kernel(*refs):
+    pieces, out = refs[:-1], refs[-1]
+    rows = pieces[0].shape[0]
+    for k, piece in enumerate(pieces):
+        out[k * rows : (k + 1) * rows, :] = piece[...]
+
+
+def piece_kernel(n, other, offset, ids, *refs):
+    means = refs[:n]
+    momentum, weights = refs[n : n + 2]
+    new_weights, new_momentum, w_out, m_out, sems = refs[-5:]
+    rows = w_out.shape[1]
+    start = first_row(ids, other, offset, weights.shape[0] // 2)
+    copies = []
+    for k in range(4):
+        mean = means[k] if n == 4 else means[0].at[k * rows : (k + 1) * rows, :]
+        at = rows_at(start + (ids[1] // 2 ^ k) * rows, rows)
+        outer_kernel(mean, momentum.at[at, :], weights.at[at, :], w_out.at[k], m_out.at[k])
+        for i, (src, dst) in enumerate(((w_out, new_weights), (m_out, new_momentum))):
+            copy = pltpu.make_async_copy(src.at[k], dst.at[at, :], sems.at[i, k])
+            copy.start()
+            copies.append(copy)
+    for copy in copies:
+        copy.wait()
+
+
+def outer_piece(ids, other, offset, means, momentum, weights, outs):
+    n = len(means)
+    width = weights.shape[1]
+    piece = means[0].shape[0] * n // 4
+    full_shape = jax.ShapeDtypeStruct(weights.shape, F32)
+    return pl.pallas_call(
+        functools.partial(piece_kernel, n, other, offset),
+        out_shape=(full_shape, full_shape),
+        in_specs=[SMEM] + [VMEM] * (n + 2) + [ANY] * len(outs),
+        out_specs=(ANY, ANY),
+        scratch_shapes=[pltpu.VMEM((4, piece, width), F32)] * 2
+        + [pltpu.SemaphoreType.DMA((2, 4))],
+        input_output_aliases={n + 3 + i: i for i in range(len(outs))},
+        compiler_params=PARAMS,
+        cost_estimate=cost(0, 72 * piece * width),
+        name="outer_step",
+    )(ids, *means, momentum, weights, *outs)
 
 
 def partner(i, k, n):
@@ -179,16 +240,17 @@
     groups = rotated_key_rows.shape[1] // HEAD_SIZE
     heads_per_group = queries.shape[1] // rotated_key_rows.shape[1]
     cot_scale = math.sqrt(D / (seq_len * n_seq))
-    me = lax.axis_index("fsdp")
-    hops = range(1, n_seq)
+    ids = jnp.stack([lax.axis_index("fsdp"), lax.axis_index("rep")]).astype(jnp.int32)
+    ids, tokens = lax.optimization_barrier((ids, tokens))
+    hops = tuple(range(n_seq - 1, 0, -1))
     power = n_seq & (n_seq - 1) == 0
-
-    def columns(k):
-        at = me ^ k if power else lax.rem(me + k, n_seq)
-        return lax.dynamic_slice(tokens, (0, at * rows), (seq_len, rows))
 
     def sender(k):
         return k if power or k == 0 else n_seq - k
+
+    def columns(k):
+        block = ids[0] ^ k if power else lax.rem(ids[0] + k, n_seq)
+        return lax.dynamic_slice(tokens, (0, block * rows), (seq_len, rows))
 
     own_block = columns(0)
     blocks = [exchange(columns(k), "fsdp", k) for k in hops]
@@ -223,7 +285,7 @@
         cost_estimate=cost(2 * seq_len * rows * width * (n_seq - 1), 2 * rows * width),
         name="partial_values",
     )(*blocks, compact)
-    parts = [exchange(products[k - 1], "fsdp", sender(k)) for k in hops]
+    parts = [exchange(p, "fsdp", sender(k)) for k, p in zip(hops, products)]
     features = pl.pallas_call(
         functools.partial(transpose_kernel, n_seq),
         out_shape=jax.ShapeDtypeStruct((rows, n_seq * seq_len), BF),
@@ -244,68 +306,57 @@
     )(own_value, *parts, g_hi, g_lo, cross)
     grads = [value_grad] + [exchange(value_grad, "fsdp", k) for k in hops]
 
-    here = lax.axis_index("rep")
-    if n_rep == 8 and rows % 64 == 0:
-        core = lax.rem(here, 2)
-        chip = here // 2
-        half = rows // 2
-        piece = rows // 8
-        count = 2
-        block = half // count
-        args = (features, grads, first_moment, second_moment, value_weights)
-        theirs = direction_half(jnp.reshape((1 - core) * count, (1,)), count, block, *args, BF)
-        arrived = exchange(theirs, "rep", 1)
-        mine = direction_half(jnp.reshape(core * count, (1,)), count, block, *args, F32)
-        small = jax.ShapeDtypeStruct((piece, width), BF)
-        own, *sends = pl.pallas_call(
-            functools.partial(split_kernel, 4),
-            out_shape=(jax.ShapeDtypeStruct((piece, width), F32),) + (small,) * 3,
-            in_specs=[pl.BlockSpec(memory_space=pltpu.SMEM), VMEM, VMEM],
-            out_specs=(VMEM,) * 4,
-            compiler_params=PARAMS,
-            cost_estimate=cost(0, 10 * half * width),
-            name="chip_sum",
-        )(jnp.reshape(chip, (1,)), mine, arrived)
-        got = [exchange(s, "rep", 2 * k) for k, s in zip((1, 2, 3), sends)]
-        mean = pl.pallas_call(
-            functools.partial(mean_kernel, 1.0 / n_rep),
-            out_shape=small,
-            in_specs=[VMEM] * 4,
+    moments = (first_moment, second_moment, value_weights)
+    n = n_seq
+    if n_rep != 8 or rows % 128:
+        direction = pl.pallas_call(
+            functools.partial(direction_kernel, n),
+            out_shape=jax.ShapeDtypeStruct((rows, width), F32),
+            in_specs=[VMEM] * (n + 4),
             out_specs=VMEM,
             compiler_params=PARAMS,
-            cost_estimate=cost(0, 10 * piece * width),
-            name="mean_direction",
-        )(own, *got)
-        pieces = [mean] + [exchange(mean, "rep", 2 * k) for k in (1, 2, 3)]
-        ordered = jnp.zeros((4, piece, width), BF)
-        for k, p in enumerate(pieces):
-            ordered = lax.dynamic_update_slice(ordered, p[None], (chip ^ k, 0, 0))
-        ordered = ordered.reshape(half, width)
-        other = exchange(ordered, "rep", 1)
-        low = jnp.where(core == 0, ordered, other)
-        high = jnp.where(core == 0, other, ordered)
-        mean_direction = jnp.concatenate([low, high], axis=0)
-    else:
-        direction = direction_half(
-            jnp.zeros((1,), jnp.int32), 2, rows // 2, features, grads, first_moment, second_moment,
-            value_weights, F32,
-        )
-        mean_direction = lax.psum(direction, "rep") / n_rep
-
-    count = 4
-    blocked = pl.BlockSpec((rows // count, width), lambda i: (i, 0))
-    full_shape = jax.ShapeDtypeStruct((rows, width), F32)
-    new_weights, new_momentum = pl.pallas_call(
-        outer_kernel,
-        grid=(count,),
-        out_shape=(full_shape, full_shape),
-        in_specs=[blocked] * 3,
-        out_specs=(blocked, blocked),
-        compiler_params=PARAMS,
-        cost_estimate=cost(0, 18 * rows * width),
-        name="outer_step",
-    )(mean_direction, momentum, value_weights)
-    return (new_weights, new_momentum)
+            name="direction",
+        )(features, *grads, *moments)
+        full_shape = jax.ShapeDtypeStruct((rows, width), F32)
+        return pl.pallas_call(
+            outer_kernel,
+            out_shape=(full_shape, full_shape),
+            in_specs=[VMEM] * 3,
+            out_specs=(VMEM, VMEM),
+            compiler_params=PARAMS,
+            name="outer_step",
+        )(lax.psum(direction, "rep") / n_rep, momentum, value_weights)
+
+    half = rows // 2
+    piece = half // 4
+    small = jax.ShapeDtypeStruct((piece, width), BF)
+
+    def half_direction(other, dtype):
+        return local(
+            functools.partial(half_kernel, n, min(half, 128), other),
+            (jax.ShapeDtypeStruct((half, width), dtype),),
+            ids, features, *grads, *moments,
+            flops=2 * half * width * features.shape[1],
+            name="direction",
+        )[0]
+
+    theirs = half_direction(True, BF)
+    arrived = exchange(theirs, "rep", 1)
+    mine = half_direction(False, F32)
+    own, *sends = local(
+        split_kernel, (jax.ShapeDtypeStruct((piece, width), F32),) + (small,) * 3,
+        ids, mine, arrived, name="chip_sum",
+    )
+    got = to_chips(sends)
+    mean = local(
+        functools.partial(mean_kernel, 1.0 / n_rep), (small,), own, *got, name="mean_direction"
+    )[0]
+    means = [mean] + to_chips([mean] * 3)
+    stack = local(stack_kernel, (jax.ShapeDtypeStruct((half, width), BF),), *means, name="stack")[0]
+    other = exchange(stack, "rep", 1)
+    outs = outer_piece(ids, False, 0, means, momentum, value_weights, ())
+    outs = outer_piece(ids, True, 0, [other], momentum, value_weights, outs)
+    return tuple(outs)
 
 
 def solution(mesh):

time: 86.5 us -> 81.9 us (0.947)
  local copies, waits for them, and re-layouts: 4.54 us -> 1.45 us
  starting transfers between devices: 22.4 us -> 25.2 us
  waiting for transfers between devices: 45.7 us -> 43.3 us
  Pallas kernels: 12.5 us -> 10.7 us
    unnamed x26 -> x14, local copies, waits for them, and re-layouts: 3.03 us -> 0.03 us
    ppermute x17, starting transfers between devices: 22.4 us -> 25.2 us  [exchange(): return lax.ppermute(x, axis, [(i, partner(i, k, n)) for i in range(n)])]
    ppermute x17, waiting for transfers between devices: 45.7 us -> 43.3 us  [exchange(): return lax.ppermute(x, axis, [(i, partner(i, k, n)) for i in range(n)])]
    pallas_call x5 -> x7, Pallas kernels: 9.54 us -> 7.7 us  [the longest x2 4.01 us: outer_piece(): pl.pallas_call(functools.partial(piece_kernel, n, other, offset), out_sha...]
  transfers between devices with their start and end apart: 17 -> 17, of which waited for: 11 -> 11; matrix products, arithmetic and copies ran while one was open for 0% -> 0% of each run, Pallas kernels for 5% -> 7%
where the time goes in v2:
time: 81.9 us; the launch traced here: 81.7 us
  waiting for transfers between devices  43.3 us (53%)
  starting transfers between devices  25.2 us (31%)
  Pallas kernels  10.7 us (13%)
  local copies, waits for them, and re-layouts  1.45 us (2%)
  between operations  0.98 us (1%)
    ppermute x17, waiting for transfers between devices, exchange(): return lax.ppermute(x, axis, [(i, partner(i, k, n)) for i in range(n)])  43.3 us
    ppermute x17, starting transfers between devices, exchange(): return lax.ppermute(x, axis, [(i, partner(i, k, n)) for i in range(n)])  25.2 us
    pallas_call x2, Pallas kernels, outer_piece(): pl.pallas_call(functools.partial(piece_kernel, n, other, offset), out_sha...  4.01 us
    pallas_call x5, Pallas kernels, local(): pl.pallas_call(kernel, out_shape=tuple(shapes), in_specs=specs, out_specs...  3.69 us
  transfers between devices with their start and end apart: 17, of which 11 were waited for; matrix products, arithmetic and copies ran while one was open for 0% of the time, Pallas kernels for 7%

profile of v2, /device:TPU:0, one launch (start us, length us, event | category | flops | bytes accessed | tf_op | source)
XLA Modules:
  0.0 81.7 jit_solution(111053126727013941)
XLA Ops:
  0.6 0.1 pad_add_fusion.ids
  0.9 1.4 %constant_dynamic-slice_fusion = (bf16[128,1024]{1,0:T(8,128)(2,1)S(1)}, bf16[128,1024]{1,0:T(8,128)(2,1)S(1)}, bf16[128,1024]{1,0:T(8,128)(2,1)S(1)}, bf16[128,1024]{1,0:T(8,128)(2,1)S(1)}) fusion(bf16[128,4096]{1,0:T(8,128)(2,1)} %param.8, s32[]{:T(128)S(6)} %select_n.15, s32[]{:T(128)S(6)} %select_n.14, s32[]{:T(128)S(6)} %select_n.13, s32[]{:T(128)S(6)} %select_n.12), kind=kLoop, calls=%fused_computation | loop fusion | bytes 2097168 | tf_op jit(solution)/shard_map/dynamic_slice | solution.py:253
  2.3 3.1 %collective-permute-start.2 = (bf16[128,1024]{1,0:T(8,128)(2,1)S(1)}, bf16[128,1024]{1,0:T(8,128)(2,1)S(1)}, u32[]{:S(2)}, u32[]{:S(2)}) collective-permute-start(bf16[128,1024]{1,0:T(8,128)(2,1)S(1)} %get-tuple-element.34), channel_id=1, source_target_pairs={{0,1},{1,0},{2,3},{3,2},{4,5},{5,4},{6,7},{7,6},{8,9},{9,8},{10,11... | collective-permute-start | bytes 786440 | tf_op jit(solution)/shard_map/ppermute | solution.py:230
  5.4 2.6 %collective-permute-start.1 = (bf16[128,1024]{1,0:T(8,128)(2,1)S(1)}, bf16[128,1024]{1,0:T(8,128)(2,1)S(1)}, u32[]{:S(2)}, u32[]{:S(2)}) collective-permute-start(bf16[128,1024]{1,0:T(8,128)(2,1)S(1)} %get-tuple-element.35), channel_id=1, source_target_pairs={{0,2},{1,3},{2,0},{3,1},{4,6},{5,7},{6,4},{7,5},{8,10},{9,11},{10,... | collective-permute-start | bytes 786440 | tf_op jit(solution)/shard_map/ppermute | solution.py:230
  8.0 0.0 collective-permute-start
  8.0 0.0 copy-start.6
  8.0 0.4 own_value.1
  8.4 8.2 %collective-permute-done.2.refs_3_.refs_2_ = bf16[128,1024]{1,0:T(8,128)(2,1)S(1)} collective-permute-done((bf16[128,1024]{1,0:T(8,128)(2,1)S(1)}, bf16[128,1024]{1,0:T(8,128)(2,1)S(1)}, u32[]{:S(2)}, u32[]{:S(2)}) %collective-permute-start.2) | collective-permute-done | bytes 262176 | tf_op jit(solution)/shard_map/ppermute | solution.py:230
  16.6 10.2 %collective-permute-done.1.refs_2_.refs_1_ = bf16[128,1024]{1,0:T(8,128)(2,1)S(1)} collective-permute-done((bf16[128,1024]{1,0:T(8,128)(2,1)S(1)}, bf16[128,1024]{1,0:T(8,128)(2,1)S(1)}, u32[]{:S(2)}, u32[]{:S(2)}) %collective-permute-start.1) | collective-permute-done | bytes 262176 | tf_op jit(solution)/shard_map/ppermute | solution.py:230
  26.8 0.0 collective-permute-done.refs_1_.refs_0_
  26.8 0.6 partial_values.1
  27.4 2.5 %collective-permute-start.3 = (bf16[128,512]{1,0:T(8,128)(2,1)S(1)}, bf16[128,512]{1,0:T(8,128)(2,1)S(1)}, u32[]{:S(2)}, u32[]{:S(2)}) collective-permute-start(bf16[128,512]{1,0:T(8,128)(2,1)S(1)} %get-tuple-element.22), channel_id=1, source_target_pairs={{0,3},{1,2},{2,1},{3,0},{4,7},{5,6},{6,5},{7,4},{8,11},{9,10},{10,... | collective-permute-start | bytes 393224 | tf_op jit(solution)/shard_map/ppermute | solution.py:230
  29.9 5.2 %collective-permute-start.4 = (bf16[128,512]{1,0:T(8,128)(2,1)S(1)}, bf16[128,512]{1,0:T(8,128)(2,1)S(1)}, u32[]{:S(2)}, u32[]{:S(2)}) collective-permute-start(bf16[128,512]{1,0:T(8,128)(2,1)S(1)} %get-tuple-element.23), channel_id=1, source_target_pairs={{0,2},{1,3},{2,0},{3,1},{4,6},{5,7},{6,4},{7,5},{8,10},{9,11},{10,... | collective-permute-start | bytes 393224 | tf_op jit(solution)/shard_map/ppermute | solution.py:230
  35.1 0.1 collective-permute-start.5
  35.2 1.4 %attention.1 = (bf16[128,512]{1,0:T(8,128)(2,1)S(1)}, bf16[128,512]{1,0:T(8,128)(2,1)S(1)}, f32[128,512]{1,0:T(8,128)S(1)}) custom-call(bf16[128,2048]{1,0:T(8,128)(2,1)S(1)} %copy-done.4, bf16[128,512]{1,0:T(8,128)(2,1)S(1)} %copy-done.6, bf16[128,2048]{1,0:T(8,128)(2,1)S(1)} %copy-done.5), custom_call_target="tpu_custom_call" | custom-call | flops 201326592 | bytes 1048576 | tf_op jit(solution)/shard_map/attention/pallas_call | solution.py:260
  36.6 0.0 collective-permute-done.3.refs_1_
  36.7 6.1 %collective-permute-done.4.refs_2_ = bf16[128,512]{1,0:T(8,128)(2,1)S(1)} collective-permute-done((bf16[128,512]{1,0:T(8,128)(2,1)S(1)}, bf16[128,512]{1,0:T(8,128)(2,1)S(1)}, u32[]{:S(2)}, u32[]{:S(2)}) %collective-permute-start.4) | collective-permute-done | bytes 131104 | tf_op jit(solution)/shard_map/ppermute | solution.py:230
  42.8 0.0 collective-permute-done.5.refs_3_
  42.8 0.2 value_grad.1.refs_0_
  43.0 0.1 collective-permute-start.8
  43.1 3.0 %collective-permute-start.7 = (bf16[128,512]{1,0:T(8,128)(2,1)S(1)}, bf16[128,512]{1,0:T(8,128)(2,1)S(1)}, u32[]{:S(2)}, u32[]{:S(2)}) collective-permute-start(bf16[128,512]{1,0:T(8,128)(2,1)S(1)} %value_grad.1.refs_0_), channel_id=1, source_target_pairs={{0,2},{1,3},{2,0},{3,1},{4,6},{5,7},{6,4},{7,5},{8,10},{9,11},{10,... | collective-permute-start | bytes 393224 | tf_op jit(solution)/shard_map/ppermute | solution.py:230
  46.1 1.4 %collective-permute-start.6 = (bf16[128,512]{1,0:T(8,128)(2,1)S(1)}, bf16[128,512]{1,0:T(8,128)(2,1)S(1)}, u32[]{:S(2)}, u32[]{:S(2)}) collective-permute-start(bf16[128,512]{1,0:T(8,128)(2,1)S(1)} %value_grad.1.refs_0_), channel_id=1, source_target_pairs={{0,3},{1,2},{2,1},{3,0},{4,7},{5,6},{6,5},{7,4},{8,11},{9,10},{10,... | collective-permute-start | bytes 393224 | tf_op jit(solution)/shard_map/ppermute | solution.py:230
  47.5 0.3 transpose_tokens.1.features
  47.8 0.7 collective-permute-done.8.refs_3_
  48.6 6.8 %collective-permute-done.7.refs_2_ = bf16[128,512]{1,0:T(8,128)(2,1)S(1)} collective-permute-done((bf16[128,512]{1,0:T(8,128)(2,1)S(1)}, bf16[128,512]{1,0:T(8,128)(2,1)S(1)}, u32[]{:S(2)}, u32[]{:S(2)}) %collective-permute-start.7) | collective-permute-done | bytes 131104 | tf_op jit(solution)/shard_map/ppermute | solution.py:230
  55.4 0.0 collective-permute-done.6.refs_1_
  55.4 1.5 %direction.3 = bf16[512,512]{1,0:T(8,128)(2,1)S(1)} custom-call(s32[2]{0:T(128)S(1)} %pad_add_fusion.ids, bf16[1024,512]{1,0:T(8,128)(2,1)S(1)} %transpose_tokens.1.features, bf16[128,512]{1,0:T(8,128)(2,1)S(1)} %value_grad.1.refs_0_, bf16[128,512]{1,0:T(8,128)(2,1)S(1)} %collective-permute-done.6.refs_1_, ...), custom_call_target="tpu_custom_call" | custom-call | flops 268435456 | bytes 8388616 | tf_op jit(solution)/shard_map/direction/pallas_call | solution.py:85
  56.9 0.1 collective-permute-start.9
  57.0 1.5 %direction.2.mine = f32[512,512]{1,0:T(8,128)S(1)} custom-call(s32[2]{0:T(128)S(1)} %pad_add_fusion.ids, bf16[1024,512]{1,0:T(8,128)(2,1)S(1)} %transpose_tokens.1.features, bf16[128,512]{1,0:T(8,128)(2,1)S(1)} %value_grad.1.refs_0_, bf16[128,512]{1,0:T(8,128)(2,1)S(1)} %collective-permute-done.6.refs_1_, ...), custom_call_target="tpu_custom_call" | custom-call | flops 268435456 | bytes 8912904 | tf_op jit(solution)/shard_map/direction/pallas_call | solution.py:85
  58.4 0.0 copy-start.1
  58.4 0.4 collective-permute-done.9.theirs
  58.9 0.6 chip_sum.1
  59.5 1.6 %collective-permute-start.10 = (bf16[128,512]{1,0:T(8,128)(2,1)S(1)}, bf16[128,512]{1,0:T(8,128)(2,1)S(1)}, u32[]{:S(2)}, u32[]{:S(2)}) collective-permute-start(bf16[128,512]{1,0:T(8,128)(2,1)S(1)} %get-tuple-element.29), channel_id=1, source_target_pairs={{0,8},{4,12},{8,0},{12,4},{16,24},{20,28},{24,16},{28,20},{1,9},{5... | collective-permute-start | bytes 393224 | tf_op jit(solution)/shard_map/ppermute | solution.py:230
  61.1 1.5 %collective-permute-start.11 = (bf16[128,512]{1,0:T(8,128)(2,1)S(1)}, bf16[128,512]{1,0:T(8,128)(2,1)S(1)}, u32[]{:S(2)}, u32[]{:S(2)}) collective-permute-start(bf16[128,512]{1,0:T(8,128)(2,1)S(1)} %get-tuple-element.30), channel_id=1, source_target_pairs={{0,16},{4,20},{8,24},{12,28},{16,0},{20,4},{24,8},{28,12},{1,17},{... | collective-permute-start | bytes 393224 | tf_op jit(solution)/shard_map/ppermute | solution.py:230
  62.6 0.5 collective-permute-start.12
  63.1 2.4 %collective-permute-done.10.refs_0_ = bf16[128,512]{1,0:T(8,128)(2,1)S(1)} collective-permute-done((bf16[128,512]{1,0:T(8,128)(2,1)S(1)}, bf16[128,512]{1,0:T(8,128)(2,1)S(1)}, u32[]{:S(2)}, u32[]{:S(2)}) %collective-permute-start.10) | collective-permute-done | bytes 131104 | tf_op jit(solution)/shard_map/ppermute | solution.py:230
  65.5 3.7 %collective-permute-done.11.refs_1_ = bf16[128,512]{1,0:T(8,128)(2,1)S(1)} collective-permute-done((bf16[128,512]{1,0:T(8,128)(2,1)S(1)}, bf16[128,512]{1,0:T(8,128)(2,1)S(1)}, u32[]{:S(2)}, u32[]{:S(2)}) %collective-permute-start.11) | collective-permute-done | bytes 131104 | tf_op jit(solution)/shard_map/ppermute | solution.py:230
  69.1 0.0 collective-permute-done.12.refs_2_
  69.1 0.1 mean_direction.1.refs_0_
  69.2 1.6 %collective-permute-start.15 = (bf16[128,512]{1,0:T(8,128)(2,1)S(1)}, bf16[128,512]{1,0:T(8,128)(2,1)S(1)}, u32[]{:S(2)}, u32[]{:S(2)}) collective-permute-start(bf16[128,512]{1,0:T(8,128)(2,1)S(1)} %mean_direction.1.refs_0_), channel_id=1, source_target_pairs={{0,24},{4,28},{8,16},{12,20},{16,8},{20,12},{24,0},{28,4},{1,25},{... | collective-permute-start | bytes 393224 | tf_op jit(solution)/shard_map/ppermute | solution.py:230
  70.8 1.2 %collective-permute-start.14 = (bf16[128,512]{1,0:T(8,128)(2,1)S(1)}, bf16[128,512]{1,0:T(8,128)(2,1)S(1)}, u32[]{:S(2)}, u32[]{:S(2)}) collective-permute-start(bf16[128,512]{1,0:T(8,128)(2,1)S(1)} %mean_direction.1.refs_0_), channel_id=1, source_target_pairs={{0,16},{4,20},{8,24},{12,28},{16,0},{20,4},{24,8},{28,12},{1,17},{... | collective-permute-start | bytes 393224 | tf_op jit(solution)/shard_map/ppermute | solution.py:230
  72.0 0.8 collective-permute-start.13
  72.8 3.4 %collective-permute-done.15.refs_3_ = bf16[128,512]{1,0:T(8,128)(2,1)S(1)} collective-permute-done((bf16[128,512]{1,0:T(8,128)(2,1)S(1)}, bf16[128,512]{1,0:T(8,128)(2,1)S(1)}, u32[]{:S(2)}, u32[]{:S(2)}) %collective-permute-start.15) | collective-permute-done | bytes 131104 | tf_op jit(solution)/shard_map/ppermute | solution.py:230
  76.1 1.1 %collective-permute-done.14.refs_2_ = bf16[128,512]{1,0:T(8,128)(2,1)S(1)} collective-permute-done((bf16[128,512]{1,0:T(8,128)(2,1)S(1)}, bf16[128,512]{1,0:T(8,128)(2,1)S(1)}, u32[]{:S(2)}, u32[]{:S(2)}) %collective-permute-start.14) | collective-permute-done | bytes 131104 | tf_op jit(solution)/shard_map/ppermute | solution.py:230
  77.3 0.3 collective-permute-done.13.refs_1_
  77.6 0.1 collective-permute-start.16
  77.7 2.0 %outer_step.2 = (f32[1024,512]{1,0:T(8,128)}, f32[1024,512]{1,0:T(8,128)}) custom-call(s32[2]{0:T(128)S(1)} %pad_add_fusion.ids, bf16[128,512]{1,0:T(8,128)(2,1)S(1)} %mean_direction.1.refs_0_, bf16[128,512]{1,0:T(8,128)(2,1)S(1)} %collective-permute-done.13.refs_1_, bf16[128,512]{1,0:T(8,128)(2,1)S(1)} %collective-permute-done.14.refs_2_, ...), custom_call_target="tpu_custom_call" | custom-call | bytes 4718592 | tf_op jit(solution)/shard_map/outer_step/pallas_call | solution.py:210
  79.7 2.0 %outer_step.3 = (f32[1024,512]{1,0:T(8,128)}, f32[1024,512]{1,0:T(8,128)}) custom-call(s32[2]{0:T(128)S(1)} %pad_add_fusion.ids, bf16[512,512]{1,0:T(8,128)(2,1)S(1)} %collective-permute-done.16.refs_0_, f32[1024,512]{1,0:T(8,128)S(1)} %copy-done.1, f32[1024,512]{1,0:T(8,128)S(1)} %copy-done, ...), custom_call_target="tpu_custom_call", output_to_operand_aliasing={{0}: (4, {}), {1}: (5, {})} | custom-call | bytes 4718592 | tf_op jit(solution)/shard_map/outer_step/pallas_call | solution.py:210
  (14 shorter events, 0.1 us)
Async XLA Ops:
  0.6 7.4 %copy-start = (f32[1024,512]{1,0:T(8,128)S(1)}, f32[1024,512]{1,0:T(8,128)}, u32[]{:S(2)}) copy-start(f32[1024,512]{1,0:T(8,128)} %refs_2_.1) | copy-start | bytes 6291460
  2.3 14.2 %collective-permute-start.2 = (bf16[128,1024]{1,0:T(8,128)(2,1)S(1)}, bf16[128,1024]{1,0:T(8,128)(2,1)S(1)}, u32[]{:S(2)}, u32[]{:S(2)}) collective-permute-start(bf16[128,1024]{1,0:T(8,128)(2,1)S(1)} %get-tuple-element.34), channel_id=1, source_target_pairs={{0,1},{1,0},{2,3},{3,2},{4,5},{5,4},{6,7},{7,6},{8,9},{9,8},{10,11... | collective-permute-start | bytes 786440 | tf_op jit(solution)/shard_map/ppermute | solution.py:230
  5.4 21.4 %collective-permute-start.1 = (bf16[128,1024]{1,0:T(8,128)(2,1)S(1)}, bf16[128,1024]{1,0:T(8,128)(2,1)S(1)}, u32[]{:S(2)}, u32[]{:S(2)}) collective-permute-start(bf16[128,1024]{1,0:T(8,128)(2,1)S(1)} %get-tuple-element.35), channel_id=1, source_target_pairs={{0,2},{1,3},{2,0},{3,1},{4,6},{5,7},{6,4},{7,5},{8,10},{9,11},{10,... | collective-permute-start | bytes 786440 | tf_op jit(solution)/shard_map/ppermute | solution.py:230
  8.0 18.8 %collective-permute-start = (bf16[128,1024]{1,0:T(8,128)(2,1)S(1)}, bf16[128,1024]{1,0:T(8,128)(2,1)S(1)}, u32[]{:S(2)}, u32[]{:S(2)}) collective-permute-start(bf16[128,1024]{1,0:T(8,128)(2,1)S(1)} %get-tuple-element.36), channel_id=1, source_target_pairs={{0,3},{1,2},{2,1},{3,0},{4,7},{5,6},{6,5},{7,4},{8,11},{9,10},{10,... | collective-permute-start | bytes 786440 | tf_op jit(solution)/shard_map/ppermute | solution.py:230
  8.0 27.2 %copy-start.4 = (bf16[128,2048]{1,0:T(8,128)(2,1)S(1)}, bf16[128,2048]{1,0:T(8,128)(2,1)}, u32[]{:S(2)}) copy-start(bf16[128,2048]{1,0:T(8,128)(2,1)} %queries.1) | copy-start | bytes 1572868
  8.0 27.2 %copy-start.5 = (bf16[128,2048]{1,0:T(8,128)(2,1)S(1)}, bf16[128,2048]{1,0:T(8,128)(2,1)}, u32[]{:S(2)}) copy-start(bf16[128,2048]{1,0:T(8,128)(2,1)} %targets.1) | copy-start | bytes 1572868
  8.0 27.2 %copy-start.6 = (bf16[128,512]{1,0:T(8,128)(2,1)S(1)}, bf16[128,512]{1,0:T(8,128)(2,1)}, u32[]{:S(2)}) copy-start(bf16[128,512]{1,0:T(8,128)(2,1)} %keys.1) | copy-start | bytes 393220
  27.4 9.3 %collective-permute-start.3 = (bf16[128,512]{1,0:T(8,128)(2,1)S(1)}, bf16[128,512]{1,0:T(8,128)(2,1)S(1)}, u32[]{:S(2)}, u32[]{:S(2)}) collective-permute-start(bf16[128,512]{1,0:T(8,128)(2,1)S(1)} %get-tuple-element.22), channel_id=1, source_target_pairs={{0,3},{1,2},{2,1},{3,0},{4,7},{5,6},{6,5},{7,4},{8,11},{9,10},{10,... | collective-permute-start | bytes 393224 | tf_op jit(solution)/shard_map/ppermute | solution.py:230
  29.9 12.9 %collective-permute-start.4 = (bf16[128,512]{1,0:T(8,128)(2,1)S(1)}, bf16[128,512]{1,0:T(8,128)(2,1)S(1)}, u32[]{:S(2)}, u32[]{:S(2)}) collective-permute-start(bf16[128,512]{1,0:T(8,128)(2,1)S(1)} %get-tuple-element.23), channel_id=1, source_target_pairs={{0,2},{1,3},{2,0},{3,1},{4,6},{5,7},{6,4},{7,5},{8,10},{9,11},{10,... | collective-permute-start | bytes 393224 | tf_op jit(solution)/shard_map/ppermute | solution.py:230
  35.1 20.3 %copy-start.2 = (f32[1,1024,512]{2,1,0:T(8,128)S(1)}, f32[1,1024,512]{2,1,0:T(8,128)}, u32[]{:S(2)}) copy-start(f32[1,1024,512]{2,1,0:T(8,128)} %refs_4_.4) | copy-start | bytes 6291460
  35.1 20.3 %copy-start.3 = (f32[1,1024,512]{2,1,0:T(8,128)S(1)}, f32[1,1024,512]{2,1,0:T(8,128)}, u32[]{:S(2)}) copy-start(f32[1,1024,512]{2,1,0:T(8,128)} %refs_5_.4) | copy-start | bytes 6291460
  35.1 7.7 %collective-permute-start.5 = (bf16[128,512]{1,0:T(8,128)(2,1)S(1)}, bf16[128,512]{1,0:T(8,128)(2,1)S(1)}, u32[]{:S(2)}, u32[]{:S(2)}) collective-permute-start(bf16[128,512]{1,0:T(8,128)(2,1)S(1)} %get-tuple-element.24), channel_id=1, source_target_pairs={{0,1},{1,0},{2,3},{3,2},{4,5},{5,4},{6,7},{7,6},{8,9},{9,8},{10,11... | collective-permute-start | bytes 393224 | tf_op jit(solution)/shard_map/ppermute | solution.py:230
  43.0 5.5 %collective-permute-start.8 = (bf16[128,512]{1,0:T(8,128)(2,1)S(1)}, bf16[128,512]{1,0:T(8,128)(2,1)S(1)}, u32[]{:S(2)}, u32[]{:S(2)}) collective-permute-start(bf16[128,512]{1,0:T(8,128)(2,1)S(1)} %value_grad.1.refs_0_), channel_id=1, source_target_pairs={{0,1},{1,0},{2,3},{3,2},{4,5},{5,4},{6,7},{7,6},{8,9},{9,8},{10,11... | collective-permute-start | bytes 393224 | tf_op jit(solution)/shard_map/ppermute | solution.py:230
  43.1 12.3 %collective-permute-start.7 = (bf16[128,512]{1,0:T(8,128)(2,1)S(1)}, bf16[128,512]{1,0:T(8,128)(2,1)S(1)}, u32[]{:S(2)}, u32[]{:S(2)}) collective-permute-start(bf16[128,512]{1,0:T(8,128)(2,1)S(1)} %value_grad.1.refs_0_), channel_id=1, source_target_pairs={{0,2},{1,3},{2,0},{3,1},{4,6},{5,7},{6,4},{7,5},{8,10},{9,11},{10,... | collective-permute-start | bytes 393224 | tf_op jit(solution)/shard_map/ppermute | solution.py:230
  46.1 9.3 %collective-permute-start.6 = (bf16[128,512]{1,0:T(8,128)(2,1)S(1)}, bf16[128,512]{1,0:T(8,128)(2,1)S(1)}, u32[]{:S(2)}, u32[]{:S(2)}) collective-permute-start(bf16[128,512]{1,0:T(8,128)(2,1)S(1)} %value_grad.1.refs_0_), channel_id=1, source_target_pairs={{0,3},{1,2},{2,1},{3,0},{4,7},{5,6},{6,5},{7,4},{8,11},{9,10},{10,... | collective-permute-start | bytes 393224 | tf_op jit(solution)/shard_map/ppermute | solution.py:230
  56.9 2.0 %collective-permute-start.9 = (bf16[512,512]{1,0:T(8,128)(2,1)S(1)}, bf16[512,512]{1,0:T(8,128)(2,1)S(1)}, u32[]{:S(2)}, u32[]{:S(2)}) collective-permute-start(bf16[512,512]{1,0:T(8,128)(2,1)S(1)} %direction.3), channel_id=1, source_target_pairs={{0,4},{4,0},{8,12},{12,8},{16,20},{20,16},{24,28},{28,24},{1,5},{5... | collective-permute-start | bytes 1572872 | tf_op jit(solution)/shard_map/ppermute | solution.py:230
  58.4 19.2 %copy-start.1 = (f32[1024,512]{1,0:T(8,128)S(1)}, f32[1024,512]{1,0:T(8,128)}, u32[]{:S(2)}) copy-start(f32[1024,512]{1,0:T(8,128)} %refs_1_.1) | copy-start | bytes 6291460
  59.5 5.9 %collective-permute-start.10 = (bf16[128,512]{1,0:T(8,128)(2,1)S(1)}, bf16[128,512]{1,0:T(8,128)(2,1)S(1)}, u32[]{:S(2)}, u32[]{:S(2)}) collective-permute-start(bf16[128,512]{1,0:T(8,128)(2,1)S(1)} %get-tuple-element.29), channel_id=1, source_target_pairs={{0,8},{4,12},{8,0},{12,4},{16,24},{20,28},{24,16},{28,20},{1,9},{5... | collective-permute-start | bytes 393224 | tf_op jit(solution)/shard_map/ppermute | solution.py:230
  61.1 8.1 %collective-permute-start.11 = (bf16[128,512]{1,0:T(8,128)(2,1)S(1)}, bf16[128,512]{1,0:T(8,128)(2,1)S(1)}, u32[]{:S(2)}, u32[]{:S(2)}) collective-permute-start(bf16[128,512]{1,0:T(8,128)(2,1)S(1)} %get-tuple-element.30), channel_id=1, source_target_pairs={{0,16},{4,20},{8,24},{12,28},{16,0},{20,4},{24,8},{28,12},{1,17},{... | collective-permute-start | bytes 393224 | tf_op jit(solution)/shard_map/ppermute | solution.py:230
  62.6 6.5 %collective-permute-start.12 = (bf16[128,512]{1,0:T(8,128)(2,1)S(1)}, bf16[128,512]{1,0:T(8,128)(2,1)S(1)}, u32[]{:S(2)}, u32[]{:S(2)}) collective-permute-start(bf16[128,512]{1,0:T(8,128)(2,1)S(1)} %get-tuple-element.31), channel_id=1, source_target_pairs={{0,24},{4,28},{8,16},{12,20},{16,8},{20,12},{24,0},{28,4},{1,25},{... | collective-permute-start | bytes 393224 | tf_op jit(solution)/shard_map/ppermute | solution.py:230
  69.2 6.9 %collective-permute-start.15 = (bf16[128,512]{1,0:T(8,128)(2,1)S(1)}, bf16[128,512]{1,0:T(8,128)(2,1)S(1)}, u32[]{:S(2)}, u32[]{:S(2)}) collective-permute-start(bf16[128,512]{1,0:T(8,128)(2,1)S(1)} %mean_direction.1.refs_0_), channel_id=1, source_target_pairs={{0,24},{4,28},{8,16},{12,20},{16,8},{20,12},{24,0},{28,4},{1,25},{... | collective-permute-start | bytes 393224 | tf_op jit(solution)/shard_map/ppermute | solution.py:230
  70.8 6.5 %collective-permute-start.14 = (bf16[128,512]{1,0:T(8,128)(2,1)S(1)}, bf16[128,512]{1,0:T(8,128)(2,1)S(1)}, u32[]{:S(2)}, u32[]{:S(2)}) collective-permute-start(bf16[128,512]{1,0:T(8,128)(2,1)S(1)} %mean_direction.1.refs_0_), channel_id=1, source_target_pairs={{0,16},{4,20},{8,24},{12,28},{16,0},{20,4},{24,8},{28,12},{1,17},{... | collective-permute-start | bytes 393224 | tf_op jit(solution)/shard_map/ppermute | solution.py:230
  72.0 5.6 %collective-permute-start.13 = (bf16[128,512]{1,0:T(8,128)(2,1)S(1)}, bf16[128,512]{1,0:T(8,128)(2,1)S(1)}, u32[]{:S(2)}, u32[]{:S(2)}) collective-permute-start(bf16[128,512]{1,0:T(8,128)(2,1)S(1)} %mean_direction.1.refs_0_), channel_id=1, source_target_pairs={{0,8},{4,12},{8,0},{12,4},{16,24},{20,28},{24,16},{28,20},{1,9},{5... | collective-permute-start | bytes 393224 | tf_op jit(solution)/shard_map/ppermute | solution.py:230
  77.6 2.1 %collective-permute-start.16 = (bf16[512,512]{1,0:T(8,128)(2,1)S(1)}, bf16[512,512]{1,0:T(8,128)(2,1)S(1)}, u32[]{:S(2)}, u32[]{:S(2)}) collective-permute-start(bf16[512,512]{1,0:T(8,128)(2,1)S(1)} %stack.13), channel_id=1, source_target_pairs={{0,4},{4,0},{8,12},{12,8},{16,20},{20,16},{24,28},{28,24},{1,5},{5... | collective-permute-start | bytes 1572872 | tf_op jit(solution)/shard_map/ppermute | solution.py:230

commit v3 on v2

--- a/solution.py
+++ b/solution.py
@@ -24,7 +24,6 @@
 F32 = jnp.float32
 VMEM = pl.BlockSpec(memory_space=pltpu.VMEM)
 ANY = pl.BlockSpec(memory_space=pl.ANY)
-SMEM = pl.BlockSpec(memory_space=pltpu.SMEM)
 PARAMS = pltpu.CompilerParams(vmem_limit_bytes=12 * 1024 * 1024)
 
 
@@ -80,7 +79,7 @@
 
 
 def local(kernel, shapes, *args, flops=0, name):
-    specs = [SMEM if a.dtype == jnp.int32 else VMEM for a in args]
+    specs = [VMEM] * len(args)
     nbytes = sum(a.size * a.dtype.itemsize for a in (*args, *shapes))
     return pl.pallas_call(
         kernel,
@@ -125,26 +124,32 @@
     return pl.ds(pl.multiple_of(start, count), count)
 
 
-def first_row(ids, other, offset, half):
-    core = lax.rem(ids[1], 2)
-    return (1 - core if other else core) * half + offset
-
-
-def half_kernel(n, rows, other, ids, features, *refs):
+def position():
+    here = lax.axis_index("rep")
+    return lax.div(here, 2), lax.rem(here, 2)
+
+
+def first_row(other, half):
+    _, core = position()
+    return (1 - core if other else core) * half
+
+
+def half_kernel(n, rows, other, features, *refs):
     grads = refs[:n]
     first, second, weights, out = refs[n:]
     stacked = jnp.concatenate([g[...] for g in grads], axis=0)
-    start = first_row(ids, other, 0, weights.shape[0] // 2)
+    start = first_row(other, weights.shape[0] // 2)
     for i in range(0, out.shape[0], rows):
         at = rows_at(start + i, rows)
         total = direction_of(features, stacked, first, second, weights, at)
         out[i : i + rows, :] = total.astype(out.dtype)
 
 
-def split_kernel(ids, mine, theirs, own, *outs):
+def split_kernel(mine, theirs, own, *outs):
     rows = own.shape[0]
+    chip, _ = position()
     for k in range(len(outs) + 1):
-        at = rows_at((ids[1] // 2 ^ k) * rows, rows)
+        at = rows_at((chip ^ k) * rows, rows)
         total = mine[at, :] + theirs[at, :].astype(F32)
         if k == 0:
             own[...] = total
@@ -183,16 +188,17 @@
         out[k * rows : (k + 1) * rows, :] = piece[...]
 
 
-def piece_kernel(n, other, offset, ids, *refs):
+def piece_kernel(n, other, *refs):
     means = refs[:n]
     momentum, weights = refs[n : n + 2]
     new_weights, new_momentum, w_out, m_out, sems = refs[-5:]
     rows = w_out.shape[1]
-    start = first_row(ids, other, offset, weights.shape[0] // 2)
+    start = first_row(other, weights.shape[0] // 2)
+    chip, _ = position()
     copies = []
     for k in range(4):
         mean = means[k] if n == 4 else means[0].at[k * rows : (k + 1) * rows, :]
-        at = rows_at(start + (ids[1] // 2 ^ k) * rows, rows)
+        at = rows_at(start + (chip ^ k) * rows, rows)
         outer_kernel(mean, momentum.at[at, :], weights.at[at, :], w_out.at[k], m_out.at[k])
         for i, (src, dst) in enumerate(((w_out, new_weights), (m_out, new_momentum))):
             copy = pltpu.make_async_copy(src.at[k], dst.at[at, :], sems.at[i, k])
@@ -202,32 +208,44 @@
         copy.wait()
 
 
-def outer_piece(ids, other, offset, means, momentum, weights, outs):
+def outer_piece(other, means, momentum, weights, outs):
     n = len(means)
     width = weights.shape[1]
     piece = means[0].shape[0] * n // 4
     full_shape = jax.ShapeDtypeStruct(weights.shape, F32)
     return pl.pallas_call(
-        functools.partial(piece_kernel, n, other, offset),
+        functools.partial(piece_kernel, n, other),
         out_shape=(full_shape, full_shape),
-        in_specs=[SMEM] + [VMEM] * (n + 2) + [ANY] * len(outs),
+        in_specs=[VMEM] * (n + 2) + [ANY] * len(outs),
         out_specs=(ANY, ANY),
         scratch_shapes=[pltpu.VMEM((4, piece, width), F32)] * 2
         + [pltpu.SemaphoreType.DMA((2, 4))],
-        input_output_aliases={n + 3 + i: i for i in range(len(outs))},
+        input_output_aliases={n + 2 + i: i for i in range(len(outs))},
         compiler_params=PARAMS,
         cost_estimate=cost(0, 72 * piece * width),
         name="outer_step",
-    )(ids, *means, momentum, weights, *outs)
-
-
-def partner(i, k, n):
-    return i ^ k if n & (n - 1) == 0 else (i + k) % n
+    )(*means, momentum, weights, *outs)
 
 
 def exchange(x, axis, k):
     n = lax.axis_size(axis)
-    return lax.ppermute(x, axis, [(i, partner(i, k, n)) for i in range(n)])
+    return lax.ppermute(x, axis, [(i, i ^ k) for i in range(n)])
+
+
+def ring_hop(i, k, n):
+    if n & (n - 1):
+        return (i + k) % n
+    place, shift = i, 1
+    while shift < n:
+        place = place ^ (place >> shift)
+        shift *= 2
+    place = (place + k) % n
+    return place ^ (place >> 1)
+
+
+def turn(x, k):
+    n = lax.axis_size("fsdp")
+    return lax.ppermute(x, "fsdp", [(i, ring_hop(i, k, n)) for i in range(n)])
 
 
 def per_device(
@@ -240,20 +258,14 @@
     groups = rotated_key_rows.shape[1] // HEAD_SIZE
     heads_per_group = queries.shape[1] // rotated_key_rows.shape[1]
     cot_scale = math.sqrt(D / (seq_len * n_seq))
-    ids = jnp.stack([lax.axis_index("fsdp"), lax.axis_index("rep")]).astype(jnp.int32)
-    ids, tokens = lax.optimization_barrier((ids, tokens))
-    hops = tuple(range(n_seq - 1, 0, -1))
-    power = n_seq & (n_seq - 1) == 0
-
-    def sender(k):
-        return k if power or k == 0 else n_seq - k
-
+    me, tokens = lax.optimization_barrier((lax.axis_index("fsdp"), tokens))
+    hops = (n_seq // 2, *[k for k in range(n_seq - 1, 0, -1) if k != n_seq // 2])
     def columns(k):
-        block = ids[0] ^ k if power else lax.rem(ids[0] + k, n_seq)
+        block = ring_hop(me, k, n_seq)
         return lax.dynamic_slice(tokens, (0, block * rows), (seq_len, rows))
 
     own_block = columns(0)
-    blocks = [exchange(columns(k), "fsdp", k) for k in hops]
+    blocks = [turn(columns(k), k) for k in hops]
 
     block_shape = jax.ShapeDtypeStruct((seq_len, width), BF)
     wide_shape = jax.ShapeDtypeStruct((seq_len, width), F32)
@@ -285,7 +297,7 @@
         cost_estimate=cost(2 * seq_len * rows * width * (n_seq - 1), 2 * rows * width),
         name="partial_values",
     )(*blocks, compact)
-    parts = [exchange(p, "fsdp", sender(k)) for k, p in zip(hops, products)]
+    parts = [turn(p, n_seq - k) for k, p in zip(hops, products)]
     features = pl.pallas_call(
         functools.partial(transpose_kernel, n_seq),
         out_shape=jax.ShapeDtypeStruct((rows, n_seq * seq_len), BF),
@@ -304,7 +316,7 @@
         cost_estimate=cost(4 * seq_len * seq_len * width, 20 * seq_len * width),
         name="value_grad",
     )(own_value, *parts, g_hi, g_lo, cross)
-    grads = [value_grad] + [exchange(value_grad, "fsdp", k) for k in hops]
+    grads = [value_grad] + [turn(value_grad, k) for k in hops]
 
     moments = (first_moment, second_moment, value_weights)
     n = n_seq
@@ -335,7 +347,7 @@
         return local(
             functools.partial(half_kernel, n, min(half, 128), other),
             (jax.ShapeDtypeStruct((half, width), dtype),),
-            ids, features, *grads, *moments,
+            features, *grads, *moments,
             flops=2 * half * width * features.shape[1],
             name="direction",
         )[0]
@@ -345,7 +357,7 @@
     mine = half_direction(False, F32)
     own, *sends = local(
         split_kernel, (jax.ShapeDtypeStruct((piece, width), F32),) + (small,) * 3,
-        ids, mine, arrived, name="chip_sum",
+        mine, arrived, name="chip_sum",
     )
     got = to_chips(sends)
     mean = local(
@@ -354,8 +366,8 @@
     means = [mean] + to_chips([mean] * 3)
     stack = local(stack_kernel, (jax.ShapeDtypeStruct((half, width), BF),), *means, name="stack")[0]
     other = exchange(stack, "rep", 1)
-    outs = outer_piece(ids, False, 0, means, momentum, value_weights, ())
-    outs = outer_piece(ids, True, 0, [other], momentum, value_weights, outs)
+    outs = outer_piece(False, means, momentum, value_weights, ())
+    outs = outer_piece(True, [other], momentum, value_weights, outs)
     return tuple(outs)
 
 

time: 81.9 us -> 77.6 us (0.947)
  waiting for transfers between devices: 43.3 us -> 37.1 us
  starting transfers between devices: 25.2 us -> 30.1 us
  Pallas kernels: 10.7 us -> 7.87 us
    ppermute x17, waiting for transfers between devices: 43.3 us -> 37.1 us  [the longest x9 24.9 us: turn(): return lax.ppermute(x, 'fsdp', [(i, ring_hop(i, k, n)) for i in range(n)])]
    ppermute x17, starting transfers between devices: 25.2 us -> 30.1 us  [the longest x9 22.9 us: turn(): return lax.ppermute(x, 'fsdp', [(i, ring_hop(i, k, n)) for i in range(n)])]
    pallas_call x5, Pallas kernels: 3.69 us -> 2 us  [local(): pl.pallas_call(kernel, out_shape=tuple(shapes), in_specs=specs, out_specs...]
    pallas_call x2, Pallas kernels: 4.01 us -> 2.92 us  [outer_piece(): pl.pallas_call(functools.partial(piece_kernel, n, other), out_shape=(full...]
  transfers between devices with their start and end apart: 17 -> 17, of which waited for: 11 -> 14; matrix products, arithmetic and copies ran while one was open for 0% -> 0% of each run, Pallas kernels for 7% -> 6%
where the time goes in v3:
time: 77.6 us; the launch traced here: 77.4 us
  waiting for transfers between devices  37.1 us (48%)
  starting transfers between devices  30.1 us (39%)
  Pallas kernels  7.87 us (10%)
  local copies, waits for them, and re-layouts  1.43 us (2%)
  between operations  0.89 us (1%)
    ppermute x9, waiting for transfers between devices, turn(): return lax.ppermute(x, 'fsdp', [(i, ring_hop(i, k, n)) for i in range(n)])  24.9 us
    ppermute x9, starting transfers between devices, turn(): return lax.ppermute(x, 'fsdp', [(i, ring_hop(i, k, n)) for i in range(n)])  22.9 us
    ppermute x8, waiting for transfers between devices, exchange(): return lax.ppermute(x, axis, [(i, i ^ k) for i in range(n)])  12.2 us
    ppermute x8, starting transfers between devices, exchange(): return lax.ppermute(x, axis, [(i, i ^ k) for i in range(n)])  7.25 us
    pallas_call x2, Pallas kernels, outer_piece(): pl.pallas_call(functools.partial(piece_kernel, n, other), out_shape=(full...  2.92 us
    pallas_call x5, Pallas kernels, local(): pl.pallas_call(kernel, out_shape=tuple(shapes), in_specs=specs, out_specs...  2 us
  transfers between devices with their start and end apart: 17, of which 14 were waited for; matrix products, arithmetic and copies ran while one was open for 0% of the time, Pallas kernels for 6%

profile of v3, /device:TPU:0, one launch (start us, length us, event | category | flops | bytes accessed | tf_op | source)
XLA Modules:
  0.0 77.4 jit_solution(18184953889579453315)
XLA Ops:
  0.7 1.4 %constant_dynamic-slice_fusion = (bf16[128,1024]{1,0:T(8,128)(2,1)S(1)}, bf16[128,1024]{1,0:T(8,128)(2,1)S(1)}, bf16[128,1024]{1,0:T(8,128)(2,1)S(1)}, bf16[128,1024]{1,0:T(8,128)(2,1)S(1)}) fusion(bf16[128,4096]{1,0:T(8,128)(2,1)} %param.8, s32[]{:T(128)S(6)} %select_n.38, s32[]{:T(128)S(6)} %select_n.36, s32[]{:T(128)S(6)} %select_n.34, s32[]{:T(128)S(6)} %select_n.32), kind=kLoop, calls=%fused_computation | loop fusion | bytes 2097168 | tf_op jit(solution)/shard_map/dynamic_slice | solution.py:265
  2.1 3.1 %collective-permute-start.2 = (bf16[128,1024]{1,0:T(8,128)(2,1)S(1)}, bf16[128,1024]{1,0:T(8,128)(2,1)S(1)}, u32[]{:S(2)}, u32[]{:S(2)}) collective-permute-start(bf16[128,1024]{1,0:T(8,128)(2,1)S(1)} %get-tuple-element.34), channel_id=1, source_target_pairs={{0,1},{1,3},{2,0},{3,2},{4,5},{5,7},{6,4},{7,6},{8,9},{9,11},{10,8... | collective-permute-start | bytes 786440 | tf_op jit(solution)/shard_map/ppermute | solution.py:248
  5.2 1.1 %collective-permute-start.1 = (bf16[128,1024]{1,0:T(8,128)(2,1)S(1)}, bf16[128,1024]{1,0:T(8,128)(2,1)S(1)}, u32[]{:S(2)}, u32[]{:S(2)}) collective-permute-start(bf16[128,1024]{1,0:T(8,128)(2,1)S(1)} %get-tuple-element.35), channel_id=1, source_target_pairs={{0,2},{1,0},{2,3},{3,1},{4,6},{5,4},{6,7},{7,5},{8,10},{9,8},{10,1... | collective-permute-start | bytes 786440 | tf_op jit(solution)/shard_map/ppermute | solution.py:248
  6.3 3.9 %collective-permute-start = (bf16[128,1024]{1,0:T(8,128)(2,1)S(1)}, bf16[128,1024]{1,0:T(8,128)(2,1)S(1)}, u32[]{:S(2)}, u32[]{:S(2)}) collective-permute-start(bf16[128,1024]{1,0:T(8,128)(2,1)S(1)} %get-tuple-element.36), channel_id=1, source_target_pairs={{0,3},{1,2},{2,1},{3,0},{4,7},{5,6},{6,5},{7,4},{8,11},{9,10},{10,... | collective-permute-start | bytes 786440 | tf_op jit(solution)/shard_map/ppermute | solution.py:248
  10.2 0.4 own_value.1
  10.5 3.7 %collective-permute-done.2.refs_3_.refs_2_ = bf16[128,1024]{1,0:T(8,128)(2,1)S(1)} collective-permute-done((bf16[128,1024]{1,0:T(8,128)(2,1)S(1)}, bf16[128,1024]{1,0:T(8,128)(2,1)S(1)}, u32[]{:S(2)}, u32[]{:S(2)}) %collective-permute-start.2) | collective-permute-done | bytes 262176 | tf_op jit(solution)/shard_map/ppermute | solution.py:248
  14.2 3.9 %collective-permute-done.1.refs_2_.refs_1_ = bf16[128,1024]{1,0:T(8,128)(2,1)S(1)} collective-permute-done((bf16[128,1024]{1,0:T(8,128)(2,1)S(1)}, bf16[128,1024]{1,0:T(8,128)(2,1)S(1)}, u32[]{:S(2)}, u32[]{:S(2)}) %collective-permute-start.1) | collective-permute-done | bytes 262176 | tf_op jit(solution)/shard_map/ppermute | solution.py:248
  18.1 6.9 %collective-permute-done.refs_1_.refs_0_ = bf16[128,1024]{1,0:T(8,128)(2,1)S(1)} collective-permute-done((bf16[128,1024]{1,0:T(8,128)(2,1)S(1)}, bf16[128,1024]{1,0:T(8,128)(2,1)S(1)}, u32[]{:S(2)}, u32[]{:S(2)}) %collective-permute-start) | collective-permute-done | bytes 262176 | tf_op jit(solution)/shard_map/ppermute | solution.py:248
  25.0 0.6 partial_values.1
  25.6 3.6 %collective-permute-start.3 = (bf16[128,512]{1,0:T(8,128)(2,1)S(1)}, bf16[128,512]{1,0:T(8,128)(2,1)S(1)}, u32[]{:S(2)}, u32[]{:S(2)}) collective-permute-start(bf16[128,512]{1,0:T(8,128)(2,1)S(1)} %get-tuple-element.22), channel_id=1, source_target_pairs={{0,3},{1,2},{2,1},{3,0},{4,7},{5,6},{6,5},{7,4},{8,11},{9,10},{10,... | collective-permute-start | bytes 393224 | tf_op jit(solution)/shard_map/ppermute | solution.py:248
  29.2 5.6 %collective-permute-start.4 = (bf16[128,512]{1,0:T(8,128)(2,1)S(1)}, bf16[128,512]{1,0:T(8,128)(2,1)S(1)}, u32[]{:S(2)}, u32[]{:S(2)}) collective-permute-start(bf16[128,512]{1,0:T(8,128)(2,1)S(1)} %get-tuple-element.23), channel_id=1, source_target_pairs={{0,1},{1,3},{2,0},{3,2},{4,5},{5,7},{6,4},{7,6},{8,9},{9,11},{10,8... | collective-permute-start | bytes 393224 | tf_op jit(solution)/shard_map/ppermute | solution.py:248
  34.8 0.0 collective-permute-start.5
  34.8 1.4 %attention.1 = (bf16[128,512]{1,0:T(8,128)(2,1)S(1)}, bf16[128,512]{1,0:T(8,128)(2,1)S(1)}, f32[128,512]{1,0:T(8,128)S(1)}) custom-call(bf16[128,2048]{1,0:T(8,128)(2,1)S(1)} %copy-done.4, bf16[128,512]{1,0:T(8,128)(2,1)S(1)} %copy-done.6, bf16[128,2048]{1,0:T(8,128)(2,1)S(1)} %copy-done.5), custom_call_target="tpu_custom_call" | custom-call | flops 201326592 | bytes 1048576 | tf_op jit(solution)/shard_map/attention/pallas_call | solution.py:272
  36.3 0.0 collective-permute-done.3.refs_1_
  36.3 6.2 %collective-permute-done.4.refs_2_ = bf16[128,512]{1,0:T(8,128)(2,1)S(1)} collective-permute-done((bf16[128,512]{1,0:T(8,128)(2,1)S(1)}, bf16[128,512]{1,0:T(8,128)(2,1)S(1)}, u32[]{:S(2)}, u32[]{:S(2)}) %collective-permute-start.4) | collective-permute-done | bytes 131104 | tf_op jit(solution)/shard_map/ppermute | solution.py:248
  42.5 0.0 collective-permute-done.5.refs_3_
  42.5 0.2 value_grad.1.refs_0_
  42.8 0.1 collective-permute-start.8
  42.8 2.9 %collective-permute-start.7 = (bf16[128,512]{1,0:T(8,128)(2,1)S(1)}, bf16[128,512]{1,0:T(8,128)(2,1)S(1)}, u32[]{:S(2)}, u32[]{:S(2)}) collective-permute-start(bf16[128,512]{1,0:T(8,128)(2,1)S(1)} %value_grad.1.refs_0_), channel_id=1, source_target_pairs={{0,2},{1,0},{2,3},{3,1},{4,6},{5,4},{6,7},{7,5},{8,10},{9,8},{10,1... | collective-permute-start | bytes 393224 | tf_op jit(solution)/shard_map/ppermute | solution.py:248
  45.8 2.7 %collective-permute-start.6 = (bf16[128,512]{1,0:T(8,128)(2,1)S(1)}, bf16[128,512]{1,0:T(8,128)(2,1)S(1)}, u32[]{:S(2)}, u32[]{:S(2)}) collective-permute-start(bf16[128,512]{1,0:T(8,128)(2,1)S(1)} %value_grad.1.refs_0_), channel_id=1, source_target_pairs={{0,3},{1,2},{2,1},{3,0},{4,7},{5,6},{6,5},{7,4},{8,11},{9,10},{10,... | collective-permute-start | bytes 393224 | tf_op jit(solution)/shard_map/ppermute | solution.py:248
  48.5 0.3 transpose_tokens.1.features
  48.8 1.3 %collective-permute-done.8.refs_3_ = bf16[128,512]{1,0:T(8,128)(2,1)S(1)} collective-permute-done((bf16[128,512]{1,0:T(8,128)(2,1)S(1)}, bf16[128,512]{1,0:T(8,128)(2,1)S(1)}, u32[]{:S(2)}, u32[]{:S(2)}) %collective-permute-start.8) | collective-permute-done | bytes 131104 | tf_op jit(solution)/shard_map/ppermute | solution.py:248
  50.1 0.8 %collective-permute-done.7.refs_2_ = bf16[128,512]{1,0:T(8,128)(2,1)S(1)} collective-permute-done((bf16[128,512]{1,0:T(8,128)(2,1)S(1)}, bf16[128,512]{1,0:T(8,128)(2,1)S(1)}, u32[]{:S(2)}, u32[]{:S(2)}) %collective-permute-start.7) | collective-permute-done | bytes 131104 | tf_op jit(solution)/shard_map/ppermute | solution.py:248
  50.9 2.0 %collective-permute-done.6.refs_1_ = bf16[128,512]{1,0:T(8,128)(2,1)S(1)} collective-permute-done((bf16[128,512]{1,0:T(8,128)(2,1)S(1)}, bf16[128,512]{1,0:T(8,128)(2,1)S(1)}, u32[]{:S(2)}, u32[]{:S(2)}) %collective-permute-start.6) | collective-permute-done | bytes 131104 | tf_op jit(solution)/shard_map/ppermute | solution.py:248
  52.9 0.0 copy-done.2
  52.9 0.9 %direction.3 = bf16[512,512]{1,0:T(8,128)(2,1)S(1)} custom-call(bf16[1024,512]{1,0:T(8,128)(2,1)S(1)} %transpose_tokens.1.features, bf16[128,512]{1,0:T(8,128)(2,1)S(1)} %value_grad.1.refs_0_, bf16[128,512]{1,0:T(8,128)(2,1)S(1)} %collective-permute-done.6.refs_1_, bf16[128,512]{1,0:T(8,128)(2,1)S(1)} %collective-permute-done.7.refs_2_, ...), custom_call_target="tpu_custom_call" | custom-call | flops 268435456 | bytes 8388608 | tf_op jit(solution)/shard_map/direction/pallas_call | solution.py:84
  53.8 0.1 collective-permute-start.9
  53.9 0.9 %direction.2.mine = f32[512,512]{1,0:T(8,128)S(1)} custom-call(bf16[1024,512]{1,0:T(8,128)(2,1)S(1)} %transpose_tokens.1.features, bf16[128,512]{1,0:T(8,128)(2,1)S(1)} %value_grad.1.refs_0_, bf16[128,512]{1,0:T(8,128)(2,1)S(1)} %collective-permute-done.6.refs_1_, bf16[128,512]{1,0:T(8,128)(2,1)S(1)} %collective-permute-done.7.refs_2_, ...), custom_call_target="tpu_custom_call" | custom-call | flops 268435456 | bytes 8912896 | tf_op jit(solution)/shard_map/direction/pallas_call | solution.py:84
  54.8 0.0 copy-start.1
  54.8 1.0 %collective-permute-done.9.theirs = bf16[512,512]{1,0:T(8,128)(2,1)S(1)} collective-permute-done((bf16[512,512]{1,0:T(8,128)(2,1)S(1)}, bf16[512,512]{1,0:T(8,128)(2,1)S(1)}, u32[]{:S(2)}, u32[]{:S(2)}) %collective-permute-start.9) | collective-permute-done | bytes 524320 | tf_op jit(solution)/shard_map/ppermute | solution.py:232
  55.8 0.1 chip_sum.1
  55.9 1.6 %collective-permute-start.10 = (bf16[128,512]{1,0:T(8,128)(2,1)S(1)}, bf16[128,512]{1,0:T(8,128)(2,1)S(1)}, u32[]{:S(2)}, u32[]{:S(2)}) collective-permute-start(bf16[128,512]{1,0:T(8,128)(2,1)S(1)} %get-tuple-element.29), channel_id=1, source_target_pairs={{0,8},{4,12},{8,0},{12,4},{16,24},{20,28},{24,16},{28,20},{1,9},{5... | collective-permute-start | bytes 393224 | tf_op jit(solution)/shard_map/ppermute | solution.py:232
  57.5 1.5 %collective-permute-start.11 = (bf16[128,512]{1,0:T(8,128)(2,1)S(1)}, bf16[128,512]{1,0:T(8,128)(2,1)S(1)}, u32[]{:S(2)}, u32[]{:S(2)}) collective-permute-start(bf16[128,512]{1,0:T(8,128)(2,1)S(1)} %get-tuple-element.30), channel_id=1, source_target_pairs={{0,16},{4,20},{8,24},{12,28},{16,0},{20,4},{24,8},{28,12},{1,17},{... | collective-permute-start | bytes 393224 | tf_op jit(solution)/shard_map/ppermute | solution.py:232
  59.0 0.5 collective-permute-start.12
  59.5 2.4 %collective-permute-done.10.refs_0_ = bf16[128,512]{1,0:T(8,128)(2,1)S(1)} collective-permute-done((bf16[128,512]{1,0:T(8,128)(2,1)S(1)}, bf16[128,512]{1,0:T(8,128)(2,1)S(1)}, u32[]{:S(2)}, u32[]{:S(2)}) %collective-permute-start.10) | collective-permute-done | bytes 131104 | tf_op jit(solution)/shard_map/ppermute | solution.py:232
  61.9 3.7 %collective-permute-done.11.refs_1_ = bf16[128,512]{1,0:T(8,128)(2,1)S(1)} collective-permute-done((bf16[128,512]{1,0:T(8,128)(2,1)S(1)}, bf16[128,512]{1,0:T(8,128)(2,1)S(1)}, u32[]{:S(2)}, u32[]{:S(2)}) %collective-permute-start.11) | collective-permute-done | bytes 131104 | tf_op jit(solution)/shard_map/ppermute | solution.py:232
  65.5 0.0 collective-permute-done.12.refs_2_
  65.5 0.1 mean_direction.1.refs_0_
  65.6 1.6 %collective-permute-start.15 = (bf16[128,512]{1,0:T(8,128)(2,1)S(1)}, bf16[128,512]{1,0:T(8,128)(2,1)S(1)}, u32[]{:S(2)}, u32[]{:S(2)}) collective-permute-start(bf16[128,512]{1,0:T(8,128)(2,1)S(1)} %mean_direction.1.refs_0_), channel_id=1, source_target_pairs={{0,24},{4,28},{8,16},{12,20},{16,8},{20,12},{24,0},{28,4},{1,25},{... | collective-permute-start | bytes 393224 | tf_op jit(solution)/shard_map/ppermute | solution.py:232
  67.2 1.2 %collective-permute-start.14 = (bf16[128,512]{1,0:T(8,128)(2,1)S(1)}, bf16[128,512]{1,0:T(8,128)(2,1)S(1)}, u32[]{:S(2)}, u32[]{:S(2)}) collective-permute-start(bf16[128,512]{1,0:T(8,128)(2,1)S(1)} %mean_direction.1.refs_0_), channel_id=1, source_target_pairs={{0,16},{4,20},{8,24},{12,28},{16,0},{20,4},{24,8},{28,12},{1,17},{... | collective-permute-start | bytes 393224 | tf_op jit(solution)/shard_map/ppermute | solution.py:232
  68.4 0.8 %collective-permute-start.13 = (bf16[128,512]{1,0:T(8,128)(2,1)S(1)}, bf16[128,512]{1,0:T(8,128)(2,1)S(1)}, u32[]{:S(2)}, u32[]{:S(2)}) collective-permute-start(bf16[128,512]{1,0:T(8,128)(2,1)S(1)} %mean_direction.1.refs_0_), channel_id=1, source_target_pairs={{0,8},{4,12},{8,0},{12,4},{16,24},{20,28},{24,16},{28,20},{1,9},{5... | collective-permute-start | bytes 393224 | tf_op jit(solution)/shard_map/ppermute | solution.py:232
  69.2 3.4 %collective-permute-done.15.refs_3_ = bf16[128,512]{1,0:T(8,128)(2,1)S(1)} collective-permute-done((bf16[128,512]{1,0:T(8,128)(2,1)S(1)}, bf16[128,512]{1,0:T(8,128)(2,1)S(1)}, u32[]{:S(2)}, u32[]{:S(2)}) %collective-permute-start.15) | collective-permute-done | bytes 131104 | tf_op jit(solution)/shard_map/ppermute | solution.py:232
  72.5 1.1 %collective-permute-done.14.refs_2_ = bf16[128,512]{1,0:T(8,128)(2,1)S(1)} collective-permute-done((bf16[128,512]{1,0:T(8,128)(2,1)S(1)}, bf16[128,512]{1,0:T(8,128)(2,1)S(1)}, u32[]{:S(2)}, u32[]{:S(2)}) %collective-permute-start.14) | collective-permute-done | bytes 131104 | tf_op jit(solution)/shard_map/ppermute | solution.py:232
  73.7 0.3 collective-permute-done.13.refs_1_
  74.0 0.1 collective-permute-start.16
  74.1 1.5 %outer_step.2 = (f32[1024,512]{1,0:T(8,128)}, f32[1024,512]{1,0:T(8,128)}) custom-call(bf16[128,512]{1,0:T(8,128)(2,1)S(1)} %mean_direction.1.refs_0_, bf16[128,512]{1,0:T(8,128)(2,1)S(1)} %collective-permute-done.13.refs_1_, bf16[128,512]{1,0:T(8,128)(2,1)S(1)} %collective-permute-done.14.refs_2_, bf16[128,512]{1,0:T(8,128)(2,1)S(1)} %collective-permute-done.15.refs_3_, ...), custom_call_target="tpu_custom_call" | custom-call | bytes 4718592 | tf_op jit(solution)/shard_map/outer_step/pallas_call | solution.py:216
  75.5 0.4 collective-permute-done.16.refs_0_
  75.9 1.5 %outer_step.3 = (f32[1024,512]{1,0:T(8,128)}, f32[1024,512]{1,0:T(8,128)}) custom-call(bf16[512,512]{1,0:T(8,128)(2,1)S(1)} %collective-permute-done.16.refs_0_, f32[1024,512]{1,0:T(8,128)S(1)} %copy-done.1, f32[1024,512]{1,0:T(8,128)S(1)} %copy-done, f32[1024,512]{1,0:T(8,128)} %get-tuple-element.32.refs_3_, ...), custom_call_target="tpu_custom_call", output_to_operand_aliasing={{0}: (3, {}), {1}: (4, {})} | custom-call | bytes 4718592 | tf_op jit(solution)/shard_map/outer_step/pallas_call | solution.py:216
  (13 shorter events, 0.1 us)
Async XLA Ops:
  0.6 9.5 %copy-start = (f32[1024,512]{1,0:T(8,128)S(1)}, f32[1024,512]{1,0:T(8,128)}, u32[]{:S(2)}) copy-start(f32[1024,512]{1,0:T(8,128)} %refs_2_.1) | copy-start | bytes 6291460
  2.1 12.1 %collective-permute-start.2 = (bf16[128,1024]{1,0:T(8,128)(2,1)S(1)}, bf16[128,1024]{1,0:T(8,128)(2,1)S(1)}, u32[]{:S(2)}, u32[]{:S(2)}) collective-permute-start(bf16[128,1024]{1,0:T(8,128)(2,1)S(1)} %get-tuple-element.34), channel_id=1, source_target_pairs={{0,1},{1,3},{2,0},{3,2},{4,5},{5,7},{6,4},{7,6},{8,9},{9,11},{10,8... | collective-permute-start | bytes 786440 | tf_op jit(solution)/shard_map/ppermute | solution.py:248
  5.2 12.9 %collective-permute-start.1 = (bf16[128,1024]{1,0:T(8,128)(2,1)S(1)}, bf16[128,1024]{1,0:T(8,128)(2,1)S(1)}, u32[]{:S(2)}, u32[]{:S(2)}) collective-permute-start(bf16[128,1024]{1,0:T(8,128)(2,1)S(1)} %get-tuple-element.35), channel_id=1, source_target_pairs={{0,2},{1,0},{2,3},{3,1},{4,6},{5,4},{6,7},{7,5},{8,10},{9,8},{10,1... | collective-permute-start | bytes 786440 | tf_op jit(solution)/shard_map/ppermute | solution.py:248
  6.3 18.8 %collective-permute-start = (bf16[128,1024]{1,0:T(8,128)(2,1)S(1)}, bf16[128,1024]{1,0:T(8,128)(2,1)S(1)}, u32[]{:S(2)}, u32[]{:S(2)}) collective-permute-start(bf16[128,1024]{1,0:T(8,128)(2,1)S(1)} %get-tuple-element.36), channel_id=1, source_target_pairs={{0,3},{1,2},{2,1},{3,0},{4,7},{5,6},{6,5},{7,4},{8,11},{9,10},{10,... | collective-permute-start | bytes 786440 | tf_op jit(solution)/shard_map/ppermute | solution.py:248
  10.2 24.6 %copy-start.4 = (bf16[128,2048]{1,0:T(8,128)(2,1)S(1)}, bf16[128,2048]{1,0:T(8,128)(2,1)}, u32[]{:S(2)}) copy-start(bf16[128,2048]{1,0:T(8,128)(2,1)} %queries.1) | copy-start | bytes 1572868
  10.2 24.7 %copy-start.5 = (bf16[128,2048]{1,0:T(8,128)(2,1)S(1)}, bf16[128,2048]{1,0:T(8,128)(2,1)}, u32[]{:S(2)}) copy-start(bf16[128,2048]{1,0:T(8,128)(2,1)} %targets.1) | copy-start | bytes 1572868
  10.2 24.7 %copy-start.6 = (bf16[128,512]{1,0:T(8,128)(2,1)S(1)}, bf16[128,512]{1,0:T(8,128)(2,1)}, u32[]{:S(2)}) copy-start(bf16[128,512]{1,0:T(8,128)(2,1)} %keys.1) | copy-start | bytes 393220
  25.6 10.7 %collective-permute-start.3 = (bf16[128,512]{1,0:T(8,128)(2,1)S(1)}, bf16[128,512]{1,0:T(8,128)(2,1)S(1)}, u32[]{:S(2)}, u32[]{:S(2)}) collective-permute-start(bf16[128,512]{1,0:T(8,128)(2,1)S(1)} %get-tuple-element.22), channel_id=1, source_target_pairs={{0,3},{1,2},{2,1},{3,0},{4,7},{5,6},{6,5},{7,4},{8,11},{9,10},{10,... | collective-permute-start | bytes 393224 | tf_op jit(solution)/shard_map/ppermute | solution.py:248
  29.2 13.3 %collective-permute-start.4 = (bf16[128,512]{1,0:T(8,128)(2,1)S(1)}, bf16[128,512]{1,0:T(8,128)(2,1)S(1)}, u32[]{:S(2)}, u32[]{:S(2)}) collective-permute-start(bf16[128,512]{1,0:T(8,128)(2,1)S(1)} %get-tuple-element.23), channel_id=1, source_target_pairs={{0,1},{1,3},{2,0},{3,2},{4,5},{5,7},{6,4},{7,6},{8,9},{9,11},{10,8... | collective-permute-start | bytes 393224 | tf_op jit(solution)/shard_map/ppermute | solution.py:248
  34.8 18.1 %copy-start.2 = (f32[1,1024,512]{2,1,0:T(8,128)S(1)}, f32[1,1024,512]{2,1,0:T(8,128)}, u32[]{:S(2)}) copy-start(f32[1,1024,512]{2,1,0:T(8,128)} %refs_4_.4) | copy-start | bytes 6291460
  34.8 18.1 %copy-start.3 = (f32[1,1024,512]{2,1,0:T(8,128)S(1)}, f32[1,1024,512]{2,1,0:T(8,128)}, u32[]{:S(2)}) copy-start(f32[1,1024,512]{2,1,0:T(8,128)} %refs_5_.4) | copy-start | bytes 6291460
  34.8 7.7 %collective-permute-start.5 = (bf16[128,512]{1,0:T(8,128)(2,1)S(1)}, bf16[128,512]{1,0:T(8,128)(2,1)S(1)}, u32[]{:S(2)}, u32[]{:S(2)}) collective-permute-start(bf16[128,512]{1,0:T(8,128)(2,1)S(1)} %get-tuple-element.24), channel_id=1, source_target_pairs={{0,2},{1,0},{2,3},{3,1},{4,6},{5,4},{6,7},{7,5},{8,10},{9,8},{10,1... | collective-permute-start | bytes 393224 | tf_op jit(solution)/shard_map/ppermute | solution.py:248
  42.8 7.3 %collective-permute-start.8 = (bf16[128,512]{1,0:T(8,128)(2,1)S(1)}, bf16[128,512]{1,0:T(8,128)(2,1)S(1)}, u32[]{:S(2)}, u32[]{:S(2)}) collective-permute-start(bf16[128,512]{1,0:T(8,128)(2,1)S(1)} %value_grad.1.refs_0_), channel_id=1, source_target_pairs={{0,1},{1,3},{2,0},{3,2},{4,5},{5,7},{6,4},{7,6},{8,9},{9,11},{10,8... | collective-permute-start | bytes 393224 | tf_op jit(solution)/shard_map/ppermute | solution.py:248
  42.8 8.1 %collective-permute-start.7 = (bf16[128,512]{1,0:T(8,128)(2,1)S(1)}, bf16[128,512]{1,0:T(8,128)(2,1)S(1)}, u32[]{:S(2)}, u32[]{:S(2)}) collective-permute-start(bf16[128,512]{1,0:T(8,128)(2,1)S(1)} %value_grad.1.refs_0_), channel_id=1, source_target_pairs={{0,2},{1,0},{2,3},{3,1},{4,6},{5,4},{6,7},{7,5},{8,10},{9,8},{10,1... | collective-permute-start | bytes 393224 | tf_op jit(solution)/shard_map/ppermute | solution.py:248
  45.8 7.2 %collective-permute-start.6 = (bf16[128,512]{1,0:T(8,128)(2,1)S(1)}, bf16[128,512]{1,0:T(8,128)(2,1)S(1)}, u32[]{:S(2)}, u32[]{:S(2)}) collective-permute-start(bf16[128,512]{1,0:T(8,128)(2,1)S(1)} %value_grad.1.refs_0_), channel_id=1, source_target_pairs={{0,3},{1,2},{2,1},{3,0},{4,7},{5,6},{6,5},{7,4},{8,11},{9,10},{10,... | collective-permute-start | bytes 393224 | tf_op jit(solution)/shard_map/ppermute | solution.py:248
  53.8 2.0 %collective-permute-start.9 = (bf16[512,512]{1,0:T(8,128)(2,1)S(1)}, bf16[512,512]{1,0:T(8,128)(2,1)S(1)}, u32[]{:S(2)}, u32[]{:S(2)}) collective-permute-start(bf16[512,512]{1,0:T(8,128)(2,1)S(1)} %direction.3), channel_id=1, source_target_pairs={{0,4},{4,0},{8,12},{12,8},{16,20},{20,16},{24,28},{28,24},{1,5},{5... | collective-permute-start | bytes 1572872 | tf_op jit(solution)/shard_map/ppermute | solution.py:232
  54.8 19.2 %copy-start.1 = (f32[1024,512]{1,0:T(8,128)S(1)}, f32[1024,512]{1,0:T(8,128)}, u32[]{:S(2)}) copy-start(f32[1024,512]{1,0:T(8,128)} %refs_1_.1) | copy-start | bytes 6291460
  55.9 5.9 %collective-permute-start.10 = (bf16[128,512]{1,0:T(8,128)(2,1)S(1)}, bf16[128,512]{1,0:T(8,128)(2,1)S(1)}, u32[]{:S(2)}, u32[]{:S(2)}) collective-permute-start(bf16[128,512]{1,0:T(8,128)(2,1)S(1)} %get-tuple-element.29), channel_id=1, source_target_pairs={{0,8},{4,12},{8,0},{12,4},{16,24},{20,28},{24,16},{28,20},{1,9},{5... | collective-permute-start | bytes 393224 | tf_op jit(solution)/shard_map/ppermute | solution.py:232
  57.5 8.1 %collective-permute-start.11 = (bf16[128,512]{1,0:T(8,128)(2,1)S(1)}, bf16[128,512]{1,0:T(8,128)(2,1)S(1)}, u32[]{:S(2)}, u32[]{:S(2)}) collective-permute-start(bf16[128,512]{1,0:T(8,128)(2,1)S(1)} %get-tuple-element.30), channel_id=1, source_target_pairs={{0,16},{4,20},{8,24},{12,28},{16,0},{20,4},{24,8},{28,12},{1,17},{... | collective-permute-start | bytes 393224 | tf_op jit(solution)/shard_map/ppermute | solution.py:232
  59.0 6.5 %collective-permute-start.12 = (bf16[128,512]{1,0:T(8,128)(2,1)S(1)}, bf16[128,512]{1,0:T(8,128)(2,1)S(1)}, u32[]{:S(2)}, u32[]{:S(2)}) collective-permute-start(bf16[128,512]{1,0:T(8,128)(2,1)S(1)} %get-tuple-element.31), channel_id=1, source_target_pairs={{0,24},{4,28},{8,16},{12,20},{16,8},{20,12},{24,0},{28,4},{1,25},{... | collective-permute-start | bytes 393224 | tf_op jit(solution)/shard_map/ppermute | solution.py:232
  65.6 6.9 %collective-permute-start.15 = (bf16[128,512]{1,0:T(8,128)(2,1)S(1)}, bf16[128,512]{1,0:T(8,128)(2,1)S(1)}, u32[]{:S(2)}, u32[]{:S(2)}) collective-permute-start(bf16[128,512]{1,0:T(8,128)(2,1)S(1)} %mean_direction.1.refs_0_), channel_id=1, source_target_pairs={{0,24},{4,28},{8,16},{12,20},{16,8},{20,12},{24,0},{28,4},{1,25},{... | collective-permute-start | bytes 393224 | tf_op jit(solution)/shard_map/ppermute | solution.py:232
  67.2 6.5 %collective-permute-start.14 = (bf16[128,512]{1,0:T(8,128)(2,1)S(1)}, bf16[128,512]{1,0:T(8,128)(2,1)S(1)}, u32[]{:S(2)}, u32[]{:S(2)}) collective-permute-start(bf16[128,512]{1,0:T(8,128)(2,1)S(1)} %mean_direction.1.refs_0_), channel_id=1, source_target_pairs={{0,16},{4,20},{8,24},{12,28},{16,0},{20,4},{24,8},{28,12},{1,17},{... | collective-permute-start | bytes 393224 | tf_op jit(solution)/shard_map/ppermute | solution.py:232
  68.4 5.6 %collective-permute-start.13 = (bf16[128,512]{1,0:T(8,128)(2,1)S(1)}, bf16[128,512]{1,0:T(8,128)(2,1)S(1)}, u32[]{:S(2)}, u32[]{:S(2)}) collective-permute-start(bf16[128,512]{1,0:T(8,128)(2,1)S(1)} %mean_direction.1.refs_0_), channel_id=1, source_target_pairs={{0,8},{4,12},{8,0},{12,4},{16,24},{20,28},{24,16},{28,20},{1,9},{5... | collective-permute-start | bytes 393224 | tf_op jit(solution)/shard_map/ppermute | solution.py:232
  74.0 2.0 %collective-permute-start.16 = (bf16[512,512]{1,0:T(8,128)(2,1)S(1)}, bf16[512,512]{1,0:T(8,128)(2,1)S(1)}, u32[]{:S(2)}, u32[]{:S(2)}) collective-permute-start(bf16[512,512]{1,0:T(8,128)(2,1)S(1)} %stack.1), channel_id=1, source_target_pairs={{0,4},{4,0},{8,12},{12,8},{16,20},{20,16},{24,28},{28,24},{1,5},{5... | collective-permute-start | bytes 1572872 | tf_op jit(solution)/shard_map/ppermute | solution.py:232

commit v4 on v3

--- a/solution.py
+++ b/solution.py
@@ -68,7 +68,11 @@
 def partial_kernel(n, *refs):
     blocks, compact, outs = refs[:n], refs[n], refs[n + 1 :]
     for block, out in zip(blocks, outs):
-        out[...] = dot(block[...], compact[...]).astype(BF)
+        out[...] = dot(block[...], compact[...]).astype(out.dtype)
+
+
+def add_kernel(one, two, out):
+    out[...] = (one[...] + two[...].astype(F32)).astype(out.dtype)
 
 
 def transpose_kernel(n, *refs):
@@ -181,48 +185,38 @@
     )
 
 
-def stack_kernel(*refs):
-    pieces, out = refs[:-1], refs[-1]
-    rows = pieces[0].shape[0]
-    for k, piece in enumerate(pieces):
-        out[k * rows : (k + 1) * rows, :] = piece[...]
-
-
-def piece_kernel(n, other, *refs):
-    means = refs[:n]
-    momentum, weights = refs[n : n + 2]
+def piece_kernel(places, *refs):
+    n = len(places)
+    means, (momentum, weights) = refs[:n], refs[n : n + 2]
     new_weights, new_momentum, w_out, m_out, sems = refs[-5:]
     rows = w_out.shape[1]
-    start = first_row(other, weights.shape[0] // 2)
     chip, _ = position()
     copies = []
-    for k in range(4):
-        mean = means[k] if n == 4 else means[0].at[k * rows : (k + 1) * rows, :]
-        at = rows_at(start + (chip ^ k) * rows, rows)
-        outer_kernel(mean, momentum.at[at, :], weights.at[at, :], w_out.at[k], m_out.at[k])
+    for j, (k, other) in enumerate(places):
+        at = rows_at(first_row(other, weights.shape[0] // 2) + (chip ^ k) * rows, rows)
+        outer_kernel(means[j], momentum.at[at, :], weights.at[at, :], w_out.at[j], m_out.at[j])
         for i, (src, dst) in enumerate(((w_out, new_weights), (m_out, new_momentum))):
-            copy = pltpu.make_async_copy(src.at[k], dst.at[at, :], sems.at[i, k])
+            copy = pltpu.make_async_copy(src.at[j], dst.at[at, :], sems.at[i, j])
             copy.start()
             copies.append(copy)
     for copy in copies:
         copy.wait()
 
 
-def outer_piece(other, means, momentum, weights, outs):
-    n = len(means)
-    width = weights.shape[1]
-    piece = means[0].shape[0] * n // 4
+def outer_pieces(places, means, momentum, weights, outs):
+    n = len(places)
+    piece, width = means[0].shape
     full_shape = jax.ShapeDtypeStruct(weights.shape, F32)
     return pl.pallas_call(
-        functools.partial(piece_kernel, n, other),
+        functools.partial(piece_kernel, places),
         out_shape=(full_shape, full_shape),
         in_specs=[VMEM] * (n + 2) + [ANY] * len(outs),
         out_specs=(ANY, ANY),
-        scratch_shapes=[pltpu.VMEM((4, piece, width), F32)] * 2
-        + [pltpu.SemaphoreType.DMA((2, 4))],
+        scratch_shapes=[pltpu.VMEM((n, piece, width), F32)] * 2
+        + [pltpu.SemaphoreType.DMA((2, n))],
         input_output_aliases={n + 2 + i: i for i in range(len(outs))},
         compiler_params=PARAMS,
-        cost_estimate=cost(0, 72 * piece * width),
+        cost_estimate=cost(0, 18 * n * piece * width),
         name="outer_step",
     )(*means, momentum, weights, *outs)
 
@@ -264,8 +258,11 @@
         block = ring_hop(me, k, n_seq)
         return lax.dynamic_slice(tokens, (0, block * rows), (seq_len, rows))
 
-    own_block = columns(0)
-    blocks = [turn(columns(k), k) for k in hops]
+    cut = {hops[0]: columns(hops[0])}
+    tokens, cut[hops[0]] = lax.optimization_barrier((tokens, cut[hops[0]]))
+    cut.update({k: columns(k) for k in (0, *hops[1:])})
+    own_block = cut[0]
+    blocks = [turn(cut[k], k) for k in hops]
 
     block_shape = jax.ShapeDtypeStruct((seq_len, width), BF)
     wide_shape = jax.ShapeDtypeStruct((seq_len, width), F32)
@@ -288,16 +285,21 @@
         name="own_value",
     )(own_block, value_weights)
 
-    products = pl.pallas_call(
-        functools.partial(partial_kernel, n_seq - 1),
-        out_shape=(block_shape,) * (n_seq - 1),
-        in_specs=[VMEM] * n_seq,
-        out_specs=(VMEM,) * (n_seq - 1),
-        compiler_params=PARAMS,
-        cost_estimate=cost(2 * seq_len * rows * width * (n_seq - 1), 2 * rows * width),
-        name="partial_values",
-    )(*blocks, compact)
-    parts = [turn(p, n_seq - k) for k, p in zip(hops, products)]
+    def product(k, dtype):
+        return local(
+            functools.partial(partial_kernel, 1), (jax.ShapeDtypeStruct((seq_len, width), dtype),),
+            blocks[hops.index(k)], compact,
+            flops=2 * seq_len * rows * width, name="partial_value",
+        )[0]
+
+    if n_seq == 4:
+        passed = turn(product(2, BF), 1)
+        back = turn(product(1, BF), 3)
+        joined = local(add_kernel, (block_shape,), product(3, F32), passed, name="joined_value")[0]
+        parts = [turn(joined, 1), back]
+    else:
+        parts = [turn(product(k, BF), n_seq - k) for k in hops]
+    gathered = (hops[0], *hops[:0:-1])
     features = pl.pallas_call(
         functools.partial(transpose_kernel, n_seq),
         out_shape=jax.ShapeDtypeStruct((rows, n_seq * seq_len), BF),
@@ -306,17 +308,17 @@
         compiler_params=PARAMS,
         cost_estimate=cost(0, 4 * rows * n_seq * seq_len),
         name="transpose_tokens",
-    )(own_block, *blocks)
+    )(own_block, *[blocks[hops.index(k)] for k in gathered])
     value_grad = pl.pallas_call(
-        functools.partial(value_grad_kernel, n_seq, cot_scale),
+        functools.partial(value_grad_kernel, 1 + len(parts), cot_scale),
         out_shape=block_shape,
-        in_specs=[VMEM] * (n_seq + 3),
+        in_specs=[VMEM] * (len(parts) + 4),
         out_specs=VMEM,
         compiler_params=PARAMS,
         cost_estimate=cost(4 * seq_len * seq_len * width, 20 * seq_len * width),
         name="value_grad",
     )(own_value, *parts, g_hi, g_lo, cross)
-    grads = [value_grad] + [turn(value_grad, k) for k in hops]
+    grads = [value_grad] + [turn(value_grad, k) for k in gathered]
 
     moments = (first_moment, second_moment, value_weights)
     n = n_seq
@@ -363,12 +365,14 @@
     mean = local(
         functools.partial(mean_kernel, 1.0 / n_rep), (small,), own, *got, name="mean_direction"
     )[0]
-    means = [mean] + to_chips([mean] * 3)
-    stack = local(stack_kernel, (jax.ShapeDtypeStruct((half, width), BF),), *means, name="stack")[0]
-    other = exchange(stack, "rep", 1)
-    outs = outer_piece(False, means, momentum, value_weights, ())
-    outs = outer_piece(True, [other], momentum, value_weights, outs)
-    return tuple(outs)
+    got = to_chips([mean] * 3)
+    theirs = [exchange(g, "rep", 1) for g in (mean, *got)]
+    outs = outer_pieces(
+        tuple((k, False) for k in range(4)), [mean, *got], momentum, value_weights, ()
+    )
+    return tuple(
+        outer_pieces(tuple((k, True) for k in range(4)), theirs, momentum, value_weights, outs)
+    )
 
 
 def solution(mesh):

time: 77.6 us -> 74.6 us (0.961)
  starting transfers between devices: 30.1 us -> 26.6 us
  local copies, waits for them, and re-layouts: 1.43 us -> 2.32 us
    ppermute x9, starting transfers between devices: 22.9 us -> 19.2 us  [turn(): return lax.ppermute(x, 'fsdp', [(i, ring_hop(i, k, n)) for i in range(n)])]
    pallas_call x5 -> x8, Pallas kernels: 2 us -> 2.93 us  [local(): pl.pallas_call(kernel, out_shape=tuple(shapes), in_specs=specs, out_specs...]
    dynamic_slice x1 -> x2, local copies, waits for them, and re-layouts: 1.4 us -> 2.28 us  [columns(): return lax.dynamic_slice(tokens, (0, block * rows), (seq_len, rows))]
    pallas_call x4 -> x3, Pallas kernels: 3.74 us -> 3.15 us  [the longest x2 2.92 us: outer_pieces(): pl.pallas_call(functools.partial(piece_kernel, places), out_shape=(full_s...]
    ppermute x8 -> x11, waiting for transfers between devices: 12.2 us -> 11.8 us  [exchange(): return lax.ppermute(x, axis, [(i, i ^ k) for i in range(n)])]
    ppermute x8 -> x11, starting transfers between devices: 7.25 us -> 7.42 us  [exchange(): return lax.ppermute(x, axis, [(i, i ^ k) for i in range(n)])]
  transfers between devices with their start and end apart: 17 -> 20, of which waited for: 14 -> 13; matrix products, arithmetic and copies ran while one was open for 0% -> 2% of each run, Pallas kernels for 6% -> 7%
where the time goes in v4:
time: 74.6 us; the launch traced here: 74.4 us
  waiting for transfers between devices  36.4 us (49%)
  starting transfers between devices  26.6 us (36%)
  Pallas kernels  8.2 us (11%)
  local copies, waits for them, and re-layouts  2.32 us (3%)
  between operations  0.92 us (1%)
    ppermute x9, waiting for transfers between devices, turn(): return lax.ppermute(x, 'fsdp', [(i, ring_hop(i, k, n)) for i in range(n)])  24.6 us
    ppermute x9, starting transfers between devices, turn(): return lax.ppermute(x, 'fsdp', [(i, ring_hop(i, k, n)) for i in range(n)])  19.2 us
    ppermute x11, waiting for transfers between devices, exchange(): return lax.ppermute(x, axis, [(i, i ^ k) for i in range(n)])  11.8 us
    ppermute x11, starting transfers between devices, exchange(): return lax.ppermute(x, axis, [(i, i ^ k) for i in range(n)])  7.42 us
    pallas_call x8, Pallas kernels, local(): pl.pallas_call(kernel, out_shape=tuple(shapes), in_specs=specs, out_specs...  2.93 us
    pallas_call x2, Pallas kernels, outer_pieces(): pl.pallas_call(functools.partial(piece_kernel, places), out_shape=(full_s...  2.92 us
    dynamic_slice x2, local copies, waits for them, and re-layouts, columns(): return lax.dynamic_slice(tokens, (0, block * rows), (seq_len, rows))  2.28 us
  transfers between devices with their start and end apart: 20, of which 13 were waited for; matrix products, arithmetic and copies ran while one was open for 2% of the time, Pallas kernels for 7%

profile of v4, /device:TPU:0, one launch (start us, length us, event | category | flops | bytes accessed | tf_op | source)
XLA Modules:
  0.0 74.4 jit_solution(3616262070974245135)
XLA Ops:
  0.7 1.1 %constant_dynamic-slice_fusion.3 = bf16[128,1024]{1,0:T(8,128)(2,1)S(1)} fusion(bf16[128,4096]{1,0:T(8,128)(2,1)} %param.8, s32[]{:T(128)S(6)} %select_n.32), kind=kLoop, calls=%fused_computation.3 | loop fusion | bytes 524292 | tf_op jit(solution)/shard_map/dynamic_slice | solution.py:259
  1.8 5.1 %collective-permute-start = (bf16[128,1024]{1,0:T(8,128)(2,1)S(1)}, bf16[128,1024]{1,0:T(8,128)(2,1)S(1)}, u32[]{:S(2)}, u32[]{:S(2)}) collective-permute-start(bf16[128,1024]{1,0:T(8,128)(2,1)S(1)} %constant_dynamic-slice_fusion.3), channel_id=1, source_target_pairs={{0,3},{1,2},{2,1},{3,0},{4,7},{5,6},{6,5},{7,4},{8,11},{9,10},{10,... | collective-permute-start | bytes 786440 | tf_op jit(solution)/shard_map/ppermute | solution.py:242
  6.9 1.2 %constant_dynamic-slice_fusion = (bf16[128,1024]{1,0:T(8,128)(2,1)S(1)}, bf16[128,1024]{1,0:T(8,128)(2,1)S(1)}, bf16[128,1024]{1,0:T(8,128)(2,1)S(1)}) fusion(bf16[128,4096]{1,0:T(8,128)(2,1)} %param.8, s32[]{:T(128)S(6)} %select_n.38, s32[]{:T(128)S(6)} %select_n.36, s32[]{:T(128)S(6)} %select_n.34), kind=kLoop, calls=%fused_computation | loop fusion | bytes 1572876 | tf_op jit(solution)/shard_map/dynamic_slice | solution.py:259
  8.1 0.1 collective-permute-start.1
  8.1 2.9 %collective-permute-start.2 = (bf16[128,1024]{1,0:T(8,128)(2,1)S(1)}, bf16[128,1024]{1,0:T(8,128)(2,1)S(1)}, u32[]{:S(2)}, u32[]{:S(2)}) collective-permute-start(bf16[128,1024]{1,0:T(8,128)(2,1)S(1)} %get-tuple-element.32), channel_id=1, source_target_pairs={{0,2},{1,0},{2,3},{3,1},{4,6},{5,4},{6,7},{7,5},{8,10},{9,8},{10,1... | collective-permute-start | bytes 786440 | tf_op jit(solution)/shard_map/ppermute | solution.py:242
  11.0 0.4 own_value.1
  11.4 2.7 %collective-permute-done.refs_1_.refs_0_ = bf16[128,1024]{1,0:T(8,128)(2,1)S(1)} collective-permute-done((bf16[128,1024]{1,0:T(8,128)(2,1)S(1)}, bf16[128,1024]{1,0:T(8,128)(2,1)S(1)}, u32[]{:S(2)}, u32[]{:S(2)}) %collective-permute-start) | collective-permute-done | bytes 262176 | tf_op jit(solution)/shard_map/ppermute | solution.py:242
  14.1 0.3 partial_value.4
  14.4 0.0 copy-start.4
  14.4 0.0 copy-start.5
  14.4 6.3 %collective-permute-start.3 = (bf16[128,512]{1,0:T(8,128)(2,1)S(1)}, bf16[128,512]{1,0:T(8,128)(2,1)S(1)}, u32[]{:S(2)}, u32[]{:S(2)}) collective-permute-start(bf16[128,512]{1,0:T(8,128)(2,1)S(1)} %partial_value.4), channel_id=1, source_target_pairs={{0,1},{1,3},{2,0},{3,2},{4,5},{5,7},{6,4},{7,6},{8,9},{9,11},{10,8... | collective-permute-start | bytes 393224 | tf_op jit(solution)/shard_map/ppermute | solution.py:242
  20.7 9.4 %collective-permute-done.1.refs_2_.refs_0_ = bf16[128,1024]{1,0:T(8,128)(2,1)S(1)} collective-permute-done((bf16[128,1024]{1,0:T(8,128)(2,1)S(1)}, bf16[128,1024]{1,0:T(8,128)(2,1)S(1)}, u32[]{:S(2)}, u32[]{:S(2)}) %collective-permute-start.1) | collective-permute-done | bytes 262176 | tf_op jit(solution)/shard_map/ppermute | solution.py:242
  30.2 0.3 partial_value.5
  30.5 0.1 collective-permute-start.5
  30.6 0.3 partial_value.3.one
  30.9 2.5 %collective-permute-done.3.two = bf16[128,512]{1,0:T(8,128)(2,1)S(1)} collective-permute-done((bf16[128,512]{1,0:T(8,128)(2,1)S(1)}, bf16[128,512]{1,0:T(8,128)(2,1)S(1)}, u32[]{:S(2)}, u32[]{:S(2)}) %collective-permute-start.3) | collective-permute-done | bytes 131104 | tf_op jit(solution)/shard_map/ppermute | solution.py:242
  33.5 0.0 copy-start.3
  33.5 0.1 collective-permute-start.4
  33.6 1.5 %attention.1 = (bf16[128,512]{1,0:T(8,128)(2,1)S(1)}, bf16[128,512]{1,0:T(8,128)(2,1)S(1)}, f32[128,512]{1,0:T(8,128)S(1)}) custom-call(bf16[128,2048]{1,0:T(8,128)(2,1)S(1)} %copy-done.4, bf16[128,512]{1,0:T(8,128)(2,1)S(1)} %copy-done.6, bf16[128,2048]{1,0:T(8,128)(2,1)S(1)} %copy-done.5), custom_call_target="tpu_custom_call" | custom-call | flops 201326592 | bytes 1048576 | tf_op jit(solution)/shard_map/attention/pallas_call | solution.py:269
  35.0 1.2 %collective-permute-done.5.refs_2_ = bf16[128,512]{1,0:T(8,128)(2,1)S(1)} collective-permute-done((bf16[128,512]{1,0:T(8,128)(2,1)S(1)}, bf16[128,512]{1,0:T(8,128)(2,1)S(1)}, u32[]{:S(2)}, u32[]{:S(2)}) %collective-permute-start.5) | collective-permute-done | bytes 131104 | tf_op jit(solution)/shard_map/ppermute | solution.py:242
  36.2 3.1 %collective-permute-done.4.refs_1_ = bf16[128,512]{1,0:T(8,128)(2,1)S(1)} collective-permute-done((bf16[128,512]{1,0:T(8,128)(2,1)S(1)}, bf16[128,512]{1,0:T(8,128)(2,1)S(1)}, u32[]{:S(2)}, u32[]{:S(2)}) %collective-permute-start.4) | collective-permute-done | bytes 131104 | tf_op jit(solution)/shard_map/ppermute | solution.py:242
  39.4 0.2 value_grad.1.refs_0_
  39.6 0.3 collective-permute-start.8
  39.9 1.8 %collective-permute-start.7 = (bf16[128,512]{1,0:T(8,128)(2,1)S(1)}, bf16[128,512]{1,0:T(8,128)(2,1)S(1)}, u32[]{:S(2)}, u32[]{:S(2)}) collective-permute-start(bf16[128,512]{1,0:T(8,128)(2,1)S(1)} %value_grad.1.refs_0_), channel_id=1, source_target_pairs={{0,1},{1,3},{2,0},{3,2},{4,5},{5,7},{6,4},{7,6},{8,9},{9,11},{10,8... | collective-permute-start | bytes 393224 | tf_op jit(solution)/shard_map/ppermute | solution.py:242
  41.7 2.6 %collective-permute-start.6 = (bf16[128,512]{1,0:T(8,128)(2,1)S(1)}, bf16[128,512]{1,0:T(8,128)(2,1)S(1)}, u32[]{:S(2)}, u32[]{:S(2)}) collective-permute-start(bf16[128,512]{1,0:T(8,128)(2,1)S(1)} %value_grad.1.refs_0_), channel_id=1, source_target_pairs={{0,3},{1,2},{2,1},{3,0},{4,7},{5,6},{6,5},{7,4},{8,11},{9,10},{10,... | collective-permute-start | bytes 393224 | tf_op jit(solution)/shard_map/ppermute | solution.py:242
  44.3 0.3 transpose_tokens.1.features
  44.6 1.3 %collective-permute-done.8.refs_3_ = bf16[128,512]{1,0:T(8,128)(2,1)S(1)} collective-permute-done((bf16[128,512]{1,0:T(8,128)(2,1)S(1)}, bf16[128,512]{1,0:T(8,128)(2,1)S(1)}, u32[]{:S(2)}, u32[]{:S(2)}) %collective-permute-start.8) | collective-permute-done | bytes 131104 | tf_op jit(solution)/shard_map/ppermute | solution.py:242
  45.9 4.2 %collective-permute-done.7.refs_2_ = bf16[128,512]{1,0:T(8,128)(2,1)S(1)} collective-permute-done((bf16[128,512]{1,0:T(8,128)(2,1)S(1)}, bf16[128,512]{1,0:T(8,128)(2,1)S(1)}, u32[]{:S(2)}, u32[]{:S(2)}) %collective-permute-start.7) | collective-permute-done | bytes 131104 | tf_op jit(solution)/shard_map/ppermute | solution.py:242
  50.2 0.9 %direction.3 = bf16[512,512]{1,0:T(8,128)(2,1)S(1)} custom-call(bf16[1024,512]{1,0:T(8,128)(2,1)S(1)} %transpose_tokens.1.features, bf16[128,512]{1,0:T(8,128)(2,1)S(1)} %value_grad.1.refs_0_, bf16[128,512]{1,0:T(8,128)(2,1)S(1)} %collective-permute-done.6.refs_1_, bf16[128,512]{1,0:T(8,128)(2,1)S(1)} %collective-permute-done.7.refs_2_, ...), custom_call_target="tpu_custom_call" | custom-call | flops 268435456 | bytes 8388608 | tf_op jit(solution)/shard_map/direction/pallas_call | solution.py:88
  51.1 0.1 collective-permute-start.9
  51.2 0.9 %direction.2.mine = f32[512,512]{1,0:T(8,128)S(1)} custom-call(bf16[1024,512]{1,0:T(8,128)(2,1)S(1)} %transpose_tokens.1.features, bf16[128,512]{1,0:T(8,128)(2,1)S(1)} %value_grad.1.refs_0_, bf16[128,512]{1,0:T(8,128)(2,1)S(1)} %collective-permute-done.6.refs_1_, bf16[128,512]{1,0:T(8,128)(2,1)S(1)} %collective-permute-done.7.refs_2_, ...), custom_call_target="tpu_custom_call" | custom-call | flops 268435456 | bytes 8912896 | tf_op jit(solution)/shard_map/direction/pallas_call | solution.py:88
  52.1 1.0 %collective-permute-done.9.theirs = bf16[512,512]{1,0:T(8,128)(2,1)S(1)} collective-permute-done((bf16[512,512]{1,0:T(8,128)(2,1)S(1)}, bf16[512,512]{1,0:T(8,128)(2,1)S(1)}, u32[]{:S(2)}, u32[]{:S(2)}) %collective-permute-start.9) | collective-permute-done | bytes 524320 | tf_op jit(solution)/shard_map/ppermute | solution.py:226
  53.1 0.1 chip_sum.1
  53.2 1.6 %collective-permute-start.10 = (bf16[128,512]{1,0:T(8,128)(2,1)S(1)}, bf16[128,512]{1,0:T(8,128)(2,1)S(1)}, u32[]{:S(2)}, u32[]{:S(2)}) collective-permute-start(bf16[128,512]{1,0:T(8,128)(2,1)S(1)} %get-tuple-element.27), channel_id=1, source_target_pairs={{0,8},{4,12},{8,0},{12,4},{16,24},{20,28},{24,16},{28,20},{1,9},{5... | collective-permute-start | bytes 393224 | tf_op jit(solution)/shard_map/ppermute | solution.py:226
  54.7 1.5 %collective-permute-start.11 = (bf16[128,512]{1,0:T(8,128)(2,1)S(1)}, bf16[128,512]{1,0:T(8,128)(2,1)S(1)}, u32[]{:S(2)}, u32[]{:S(2)}) collective-permute-start(bf16[128,512]{1,0:T(8,128)(2,1)S(1)} %get-tuple-element.28), channel_id=1, source_target_pairs={{0,16},{4,20},{8,24},{12,28},{16,0},{20,4},{24,8},{28,12},{1,17},{... | collective-permute-start | bytes 393224 | tf_op jit(solution)/shard_map/ppermute | solution.py:226
  56.3 0.5 collective-permute-start.12
  56.7 2.4 %collective-permute-done.10.refs_0_ = bf16[128,512]{1,0:T(8,128)(2,1)S(1)} collective-permute-done((bf16[128,512]{1,0:T(8,128)(2,1)S(1)}, bf16[128,512]{1,0:T(8,128)(2,1)S(1)}, u32[]{:S(2)}, u32[]{:S(2)}) %collective-permute-start.10) | collective-permute-done | bytes 131104 | tf_op jit(solution)/shard_map/ppermute | solution.py:226
  59.1 3.7 %collective-permute-done.11.refs_1_ = bf16[128,512]{1,0:T(8,128)(2,1)S(1)} collective-permute-done((bf16[128,512]{1,0:T(8,128)(2,1)S(1)}, bf16[128,512]{1,0:T(8,128)(2,1)S(1)}, u32[]{:S(2)}, u32[]{:S(2)}) %collective-permute-start.11) | collective-permute-done | bytes 131104 | tf_op jit(solution)/shard_map/ppermute | solution.py:226
  62.8 0.1 mean_direction.1.refs_0_
  62.9 1.6 %collective-permute-start.18 = (bf16[128,512]{1,0:T(8,128)(2,1)S(1)}, bf16[128,512]{1,0:T(8,128)(2,1)S(1)}, u32[]{:S(2)}, u32[]{:S(2)}) collective-permute-start(bf16[128,512]{1,0:T(8,128)(2,1)S(1)} %mean_direction.1.refs_0_), channel_id=1, source_target_pairs={{0,24},{4,28},{8,16},{12,20},{16,8},{20,12},{24,0},{28,4},{1,25},{... | collective-permute-start | bytes 393224 | tf_op jit(solution)/shard_map/ppermute | solution.py:226
  64.4 1.2 %collective-permute-start.16 = (bf16[128,512]{1,0:T(8,128)(2,1)S(1)}, bf16[128,512]{1,0:T(8,128)(2,1)S(1)}, u32[]{:S(2)}, u32[]{:S(2)}) collective-permute-start(bf16[128,512]{1,0:T(8,128)(2,1)S(1)} %mean_direction.1.refs_0_), channel_id=1, source_target_pairs={{0,16},{4,20},{8,24},{12,28},{16,0},{20,4},{24,8},{28,12},{1,17},{... | collective-permute-start | bytes 393224 | tf_op jit(solution)/shard_map/ppermute | solution.py:226
  65.6 0.8 %collective-permute-start.14 = (bf16[128,512]{1,0:T(8,128)(2,1)S(1)}, bf16[128,512]{1,0:T(8,128)(2,1)S(1)}, u32[]{:S(2)}, u32[]{:S(2)}) collective-permute-start(bf16[128,512]{1,0:T(8,128)(2,1)S(1)} %mean_direction.1.refs_0_), channel_id=1, source_target_pairs={{0,8},{4,12},{8,0},{12,4},{16,24},{20,28},{24,16},{28,20},{1,9},{5... | collective-permute-start | bytes 393224 | tf_op jit(solution)/shard_map/ppermute | solution.py:226
  66.4 3.4 %collective-permute-done.18.refs_3_ = bf16[128,512]{1,0:T(8,128)(2,1)S(1)} collective-permute-done((bf16[128,512]{1,0:T(8,128)(2,1)S(1)}, bf16[128,512]{1,0:T(8,128)(2,1)S(1)}, u32[]{:S(2)}, u32[]{:S(2)}) %collective-permute-start.18) | collective-permute-done | bytes 131104 | tf_op jit(solution)/shard_map/ppermute | solution.py:226
  69.8 1.1 %collective-permute-done.16.refs_2_ = bf16[128,512]{1,0:T(8,128)(2,1)S(1)} collective-permute-done((bf16[128,512]{1,0:T(8,128)(2,1)S(1)}, bf16[128,512]{1,0:T(8,128)(2,1)S(1)}, u32[]{:S(2)}, u32[]{:S(2)}) %collective-permute-start.16) | collective-permute-done | bytes 131104 | tf_op jit(solution)/shard_map/ppermute | solution.py:226
  70.9 0.3 collective-permute-done.14.refs_1_
  71.2 0.2 collective-permute-start.15
  71.4 1.5 %outer_step.2 = (f32[1024,512]{1,0:T(8,128)}, f32[1024,512]{1,0:T(8,128)}) custom-call(bf16[128,512]{1,0:T(8,128)(2,1)S(1)} %mean_direction.1.refs_0_, bf16[128,512]{1,0:T(8,128)(2,1)S(1)} %collective-permute-done.14.refs_1_, bf16[128,512]{1,0:T(8,128)(2,1)S(1)} %collective-permute-done.16.refs_2_, bf16[128,512]{1,0:T(8,128)(2,1)S(1)} %collective-permute-done.18.refs_3_, ...), custom_call_target="tpu_custom_call" | custom-call | bytes 4718592 | tf_op jit(solution)/shard_map/outer_step/pallas_call | solution.py:210
  72.9 1.5 %outer_step.3 = (f32[1024,512]{1,0:T(8,128)}, f32[1024,512]{1,0:T(8,128)}) custom-call(bf16[128,512]{1,0:T(8,128)(2,1)S(1)} %collective-permute-done.13.refs_0_, bf16[128,512]{1,0:T(8,128)(2,1)S(1)} %collective-permute-done.15.refs_1_, bf16[128,512]{1,0:T(8,128)(2,1)S(1)} %collective-permute-done.17.refs_2_, ...), custom_call_target="tpu_custom_call", output_to_operand_aliasing={{0}: (6, {}), {1}: (7, {})} | custom-call | bytes 4718592 | tf_op jit(solution)/shard_map/outer_step/pallas_call | solution.py:210
  (22 shorter events, 0.1 us)
Async XLA Ops:
  0.6 10.4 %copy-start = (f32[1024,512]{1,0:T(8,128)S(1)}, f32[1024,512]{1,0:T(8,128)}, u32[]{:S(2)}) copy-start(f32[1024,512]{1,0:T(8,128)} %refs_5_.7) | copy-start | bytes 6291460
  1.8 12.3 %collective-permute-start = (bf16[128,1024]{1,0:T(8,128)(2,1)S(1)}, bf16[128,1024]{1,0:T(8,128)(2,1)S(1)}, u32[]{:S(2)}, u32[]{:S(2)}) collective-permute-start(bf16[128,1024]{1,0:T(8,128)(2,1)S(1)} %constant_dynamic-slice_fusion.3), channel_id=1, source_target_pairs={{0,3},{1,2},{2,1},{3,0},{4,7},{5,6},{6,5},{7,4},{8,11},{9,10},{10,... | collective-permute-start | bytes 786440 | tf_op jit(solution)/shard_map/ppermute | solution.py:242
  8.1 22.1 %collective-permute-start.1 = (bf16[128,1024]{1,0:T(8,128)(2,1)S(1)}, bf16[128,1024]{1,0:T(8,128)(2,1)S(1)}, u32[]{:S(2)}, u32[]{:S(2)}) collective-permute-start(bf16[128,1024]{1,0:T(8,128)(2,1)S(1)} %get-tuple-element.33), channel_id=1, source_target_pairs={{0,1},{1,3},{2,0},{3,2},{4,5},{5,7},{6,4},{7,6},{8,9},{9,11},{10,8... | collective-permute-start | bytes 786440 | tf_op jit(solution)/shard_map/ppermute | solution.py:242
  8.1 22.4 %collective-permute-start.2 = (bf16[128,1024]{1,0:T(8,128)(2,1)S(1)}, bf16[128,1024]{1,0:T(8,128)(2,1)S(1)}, u32[]{:S(2)}, u32[]{:S(2)}) collective-permute-start(bf16[128,1024]{1,0:T(8,128)(2,1)S(1)} %get-tuple-element.32), channel_id=1, source_target_pairs={{0,2},{1,0},{2,3},{3,1},{4,6},{5,4},{6,7},{7,5},{8,10},{9,8},{10,1... | collective-permute-start | bytes 786440 | tf_op jit(solution)/shard_map/ppermute | solution.py:242
  14.4 19.1 %copy-start.4 = (bf16[128,2048]{1,0:T(8,128)(2,1)S(1)}, bf16[128,2048]{1,0:T(8,128)(2,1)}, u32[]{:S(2)}) copy-start(bf16[128,2048]{1,0:T(8,128)(2,1)} %queries.1) | copy-start | bytes 1572868
  14.4 19.1 %copy-start.5 = (bf16[128,2048]{1,0:T(8,128)(2,1)S(1)}, bf16[128,2048]{1,0:T(8,128)(2,1)}, u32[]{:S(2)}) copy-start(bf16[128,2048]{1,0:T(8,128)(2,1)} %targets.1) | copy-start | bytes 1572868
  14.4 19.1 %copy-start.6 = (bf16[128,512]{1,0:T(8,128)(2,1)S(1)}, bf16[128,512]{1,0:T(8,128)(2,1)}, u32[]{:S(2)}) copy-start(bf16[128,512]{1,0:T(8,128)(2,1)} %keys.1) | copy-start | bytes 393220
  14.4 19.0 %collective-permute-start.3 = (bf16[128,512]{1,0:T(8,128)(2,1)S(1)}, bf16[128,512]{1,0:T(8,128)(2,1)S(1)}, u32[]{:S(2)}, u32[]{:S(2)}) collective-permute-start(bf16[128,512]{1,0:T(8,128)(2,1)S(1)} %partial_value.4), channel_id=1, source_target_pairs={{0,1},{1,3},{2,0},{3,2},{4,5},{5,7},{6,4},{7,6},{8,9},{9,11},{10,8... | collective-permute-start | bytes 393224 | tf_op jit(solution)/shard_map/ppermute | solution.py:242
  30.5 5.8 %collective-permute-start.5 = (bf16[128,512]{1,0:T(8,128)(2,1)S(1)}, bf16[128,512]{1,0:T(8,128)(2,1)S(1)}, u32[]{:S(2)}, u32[]{:S(2)}) collective-permute-start(bf16[128,512]{1,0:T(8,128)(2,1)S(1)} %partial_value.5), channel_id=1, source_target_pairs={{0,2},{1,0},{2,3},{3,1},{4,6},{5,4},{6,7},{7,5},{8,10},{9,8},{10,1... | collective-permute-start | bytes 393224 | tf_op jit(solution)/shard_map/ppermute | solution.py:242
  33.5 16.7 %copy-start.2 = (f32[1,1024,512]{2,1,0:T(8,128)S(1)}, f32[1,1024,512]{2,1,0:T(8,128)}, u32[]{:S(2)}) copy-start(f32[1,1024,512]{2,1,0:T(8,128)} %refs_4_.5) | copy-start | bytes 6291460
  33.5 16.7 %copy-start.3 = (f32[1,1024,512]{2,1,0:T(8,128)S(1)}, f32[1,1024,512]{2,1,0:T(8,128)}, u32[]{:S(2)}) copy-start(f32[1,1024,512]{2,1,0:T(8,128)} %refs_5_.5) | copy-start | bytes 6291460
  33.5 5.9 %collective-permute-start.4 = (bf16[128,512]{1,0:T(8,128)(2,1)S(1)}, bf16[128,512]{1,0:T(8,128)(2,1)S(1)}, u32[]{:S(2)}, u32[]{:S(2)}) collective-permute-start(bf16[128,512]{1,0:T(8,128)(2,1)S(1)} %joined_value.1), channel_id=1, source_target_pairs={{0,1},{1,3},{2,0},{3,2},{4,5},{5,7},{6,4},{7,6},{8,9},{9,11},{10,8... | collective-permute-start | bytes 393224 | tf_op jit(solution)/shard_map/ppermute | solution.py:242
  39.6 6.3 %collective-permute-start.8 = (bf16[128,512]{1,0:T(8,128)(2,1)S(1)}, bf16[128,512]{1,0:T(8,128)(2,1)S(1)}, u32[]{:S(2)}, u32[]{:S(2)}) collective-permute-start(bf16[128,512]{1,0:T(8,128)(2,1)S(1)} %value_grad.1.refs_0_), channel_id=1, source_target_pairs={{0,2},{1,0},{2,3},{3,1},{4,6},{5,4},{6,7},{7,5},{8,10},{9,8},{10,1... | collective-permute-start | bytes 393224 | tf_op jit(solution)/shard_map/ppermute | solution.py:242
  39.9 10.3 %collective-permute-start.7 = (bf16[128,512]{1,0:T(8,128)(2,1)S(1)}, bf16[128,512]{1,0:T(8,128)(2,1)S(1)}, u32[]{:S(2)}, u32[]{:S(2)}) collective-permute-start(bf16[128,512]{1,0:T(8,128)(2,1)S(1)} %value_grad.1.refs_0_), channel_id=1, source_target_pairs={{0,1},{1,3},{2,0},{3,2},{4,5},{5,7},{6,4},{7,6},{8,9},{9,11},{10,8... | collective-permute-start | bytes 393224 | tf_op jit(solution)/shard_map/ppermute | solution.py:242
  41.7 8.5 %collective-permute-start.6 = (bf16[128,512]{1,0:T(8,128)(2,1)S(1)}, bf16[128,512]{1,0:T(8,128)(2,1)S(1)}, u32[]{:S(2)}, u32[]{:S(2)}) collective-permute-start(bf16[128,512]{1,0:T(8,128)(2,1)S(1)} %value_grad.1.refs_0_), channel_id=1, source_target_pairs={{0,3},{1,2},{2,1},{3,0},{4,7},{5,6},{6,5},{7,4},{8,11},{9,10},{10,... | collective-permute-start | bytes 393224 | tf_op jit(solution)/shard_map/ppermute | solution.py:242
  51.1 2.0 %collective-permute-start.9 = (bf16[512,512]{1,0:T(8,128)(2,1)S(1)}, bf16[512,512]{1,0:T(8,128)(2,1)S(1)}, u32[]{:S(2)}, u32[]{:S(2)}) collective-permute-start(bf16[512,512]{1,0:T(8,128)(2,1)S(1)} %direction.3), channel_id=1, source_target_pairs={{0,4},{4,0},{8,12},{12,8},{16,20},{20,16},{24,28},{28,24},{1,5},{5... | collective-permute-start | bytes 1572872 | tf_op jit(solution)/shard_map/ppermute | solution.py:226
  52.1 19.3 %copy-start.1 = (f32[1024,512]{1,0:T(8,128)S(1)}, f32[1024,512]{1,0:T(8,128)}, u32[]{:S(2)}) copy-start(f32[1024,512]{1,0:T(8,128)} %refs_4_.7) | copy-start | bytes 6291460
  53.2 6.0 %collective-permute-start.10 = (bf16[128,512]{1,0:T(8,128)(2,1)S(1)}, bf16[128,512]{1,0:T(8,128)(2,1)S(1)}, u32[]{:S(2)}, u32[]{:S(2)}) collective-permute-start(bf16[128,512]{1,0:T(8,128)(2,1)S(1)} %get-tuple-element.27), channel_id=1, source_target_pairs={{0,8},{4,12},{8,0},{12,4},{16,24},{20,28},{24,16},{28,20},{1,9},{5... | collective-permute-start | bytes 393224 | tf_op jit(solution)/shard_map/ppermute | solution.py:226
  54.7 8.1 %collective-permute-start.11 = (bf16[128,512]{1,0:T(8,128)(2,1)S(1)}, bf16[128,512]{1,0:T(8,128)(2,1)S(1)}, u32[]{:S(2)}, u32[]{:S(2)}) collective-permute-start(bf16[128,512]{1,0:T(8,128)(2,1)S(1)} %get-tuple-element.28), channel_id=1, source_target_pairs={{0,16},{4,20},{8,24},{12,28},{16,0},{20,4},{24,8},{28,12},{1,17},{... | collective-permute-start | bytes 393224 | tf_op jit(solution)/shard_map/ppermute | solution.py:226
  56.3 6.5 %collective-permute-start.12 = (bf16[128,512]{1,0:T(8,128)(2,1)S(1)}, bf16[128,512]{1,0:T(8,128)(2,1)S(1)}, u32[]{:S(2)}, u32[]{:S(2)}) collective-permute-start(bf16[128,512]{1,0:T(8,128)(2,1)S(1)} %get-tuple-element.29), channel_id=1, source_target_pairs={{0,24},{4,28},{8,16},{12,20},{16,8},{20,12},{24,0},{28,4},{1,25},{... | collective-permute-start | bytes 393224 | tf_op jit(solution)/shard_map/ppermute | solution.py:226
  62.9 6.9 %collective-permute-start.18 = (bf16[128,512]{1,0:T(8,128)(2,1)S(1)}, bf16[128,512]{1,0:T(8,128)(2,1)S(1)}, u32[]{:S(2)}, u32[]{:S(2)}) collective-permute-start(bf16[128,512]{1,0:T(8,128)(2,1)S(1)} %mean_direction.1.refs_0_), channel_id=1, source_target_pairs={{0,24},{4,28},{8,16},{12,20},{16,8},{20,12},{24,0},{28,4},{1,25},{... | collective-permute-start | bytes 393224 | tf_op jit(solution)/shard_map/ppermute | solution.py:226
  64.4 6.5 %collective-permute-start.16 = (bf16[128,512]{1,0:T(8,128)(2,1)S(1)}, bf16[128,512]{1,0:T(8,128)(2,1)S(1)}, u32[]{:S(2)}, u32[]{:S(2)}) collective-permute-start(bf16[128,512]{1,0:T(8,128)(2,1)S(1)} %mean_direction.1.refs_0_), channel_id=1, source_target_pairs={{0,16},{4,20},{8,24},{12,28},{16,0},{20,4},{24,8},{28,12},{1,17},{... | collective-permute-start | bytes 393224 | tf_op jit(solution)/shard_map/ppermute | solution.py:226
  65.6 5.6 %collective-permute-start.14 = (bf16[128,512]{1,0:T(8,128)(2,1)S(1)}, bf16[128,512]{1,0:T(8,128)(2,1)S(1)}, u32[]{:S(2)}, u32[]{:S(2)}) collective-permute-start(bf16[128,512]{1,0:T(8,128)(2,1)S(1)} %mean_direction.1.refs_0_), channel_id=1, source_target_pairs={{0,8},{4,12},{8,0},{12,4},{16,24},{20,28},{24,16},{28,20},{1,9},{5... | collective-permute-start | bytes 393224 | tf_op jit(solution)/shard_map/ppermute | solution.py:226
  66.4 6.5 %collective-permute-start.13 = (bf16[128,512]{1,0:T(8,128)(2,1)S(1)}, bf16[128,512]{1,0:T(8,128)(2,1)S(1)}, u32[]{:S(2)}, u32[]{:S(2)}) collective-permute-start(bf16[128,512]{1,0:T(8,128)(2,1)S(1)} %mean_direction.1.refs_0_), channel_id=1, source_target_pairs={{0,4},{4,0},{8,12},{12,8},{16,20},{20,16},{24,28},{28,24},{1,5},{5... | collective-permute-start | bytes 393224 | tf_op jit(solution)/shard_map/ppermute | solution.py:226
  69.8 3.1 %collective-permute-start.19 = (bf16[128,512]{1,0:T(8,128)(2,1)S(1)}, bf16[128,512]{1,0:T(8,128)(2,1)S(1)}, u32[]{:S(2)}, u32[]{:S(2)}) collective-permute-start(bf16[128,512]{1,0:T(8,128)(2,1)S(1)} %collective-permute-done.18.refs_3_), channel_id=1, source_target_pairs={{0,4},{4,0},{8,12},{12,8},{16,20},{20,16},{24,28},{28,24},{1,5},{5... | collective-permute-start | bytes 393224 | tf_op jit(solution)/shard_map/ppermute | solution.py:226
  70.9 2.0 %collective-permute-start.17 = (bf16[128,512]{1,0:T(8,128)(2,1)S(1)}, bf16[128,512]{1,0:T(8,128)(2,1)S(1)}, u32[]{:S(2)}, u32[]{:S(2)}) collective-permute-start(bf16[128,512]{1,0:T(8,128)(2,1)S(1)} %collective-permute-done.16.refs_2_), channel_id=1, source_target_pairs={{0,4},{4,0},{8,12},{12,8},{16,20},{20,16},{24,28},{28,24},{1,5},{5... | collective-permute-start | bytes 393224 | tf_op jit(solution)/shard_map/ppermute | solution.py:226
  71.2 1.7 %collective-permute-start.15 = (bf16[128,512]{1,0:T(8,128)(2,1)S(1)}, bf16[128,512]{1,0:T(8,128)(2,1)S(1)}, u32[]{:S(2)}, u32[]{:S(2)}) collective-permute-start(bf16[128,512]{1,0:T(8,128)(2,1)S(1)} %collective-permute-done.14.refs_1_), channel_id=1, source_target_pairs={{0,4},{4,0},{8,12},{12,8},{16,20},{20,16},{24,28},{28,24},{1,5},{5... | collective-permute-start | bytes 393224 | tf_op jit(solution)/shard_map/ppermute | solution.py:226

commit v5 on v4

--- a/solution.py
+++ b/solution.py
@@ -253,7 +253,8 @@
     heads_per_group = queries.shape[1] // rotated_key_rows.shape[1]
     cot_scale = math.sqrt(D / (seq_len * n_seq))
     me, tokens = lax.optimization_barrier((lax.axis_index("fsdp"), tokens))
-    hops = (n_seq // 2, *[k for k in range(n_seq - 1, 0, -1) if k != n_seq // 2])
+    hops = (n_seq // 2, *[k for k in range(1, n_seq) if k != n_seq // 2])
+
     def columns(k):
         block = ring_hop(me, k, n_seq)
         return lax.dynamic_slice(tokens, (0, block * rows), (seq_len, rows))
@@ -293,13 +294,12 @@
         )[0]
 
     if n_seq == 4:
-        passed = turn(product(2, BF), 1)
-        back = turn(product(1, BF), 3)
-        joined = local(add_kernel, (block_shape,), product(3, F32), passed, name="joined_value")[0]
-        parts = [turn(joined, 1), back]
+        passed = turn(product(2, BF), 3)
+        back = turn(product(3, BF), 1)
+        joined = local(add_kernel, (block_shape,), product(1, F32), passed, name="joined_value")[0]
+        parts = [turn(joined, 3), back]
     else:
         parts = [turn(product(k, BF), n_seq - k) for k in hops]
-    gathered = (hops[0], *hops[:0:-1])
     features = pl.pallas_call(
         functools.partial(transpose_kernel, n_seq),
         out_shape=jax.ShapeDtypeStruct((rows, n_seq * seq_len), BF),
@@ -308,7 +308,7 @@
         compiler_params=PARAMS,
         cost_estimate=cost(0, 4 * rows * n_seq * seq_len),
         name="transpose_tokens",
-    )(own_block, *[blocks[hops.index(k)] for k in gathered])
+    )(own_block, *blocks)
     value_grad = pl.pallas_call(
         functools.partial(value_grad_kernel, 1 + len(parts), cot_scale),
         out_shape=block_shape,
@@ -318,7 +318,7 @@
         cost_estimate=cost(4 * seq_len * seq_len * width, 20 * seq_len * width),
         name="value_grad",
     )(own_value, *parts, g_hi, g_lo, cross)
-    grads = [value_grad] + [turn(value_grad, k) for k in gathered]
+    grads = [value_grad] + [turn(value_grad, k) for k in hops]
 
     moments = (first_moment, second_moment, value_weights)
     n = n_seq

time: 74.6 us -> 74.2 us (level)
  waiting for transfers between devices: 36.4 us -> 30.6 us
  starting transfers between devices: 26.6 us -> 32 us
    ppermute x9, waiting for transfers between devices: 24.6 us -> 18.7 us  [turn(): return lax.ppermute(x, 'fsdp', [(i, ring_hop(i, k, n)) for i in range(n)])]
    ppermute x9, starting transfers between devices: 19.2 us -> 24.6 us  [turn(): return lax.ppermute(x, 'fsdp', [(i, ring_hop(i, k, n)) for i in range(n)])]
  transfers between devices with their start and end apart: 20 -> 20, of which waited for: 13 -> 12; matrix products, arithmetic and copies ran while one was open for 2% -> 2% of each run, Pallas kernels for 7% -> 7%
where the time goes in v5:
time: 74.2 us; the launch traced here: 74 us
  starting transfers between devices  32 us (43%)
  waiting for transfers between devices  30.6 us (41%)
  Pallas kernels  8.2 us (11%)
  local copies, waits for them, and re-layouts  2.32 us (3%)
  between operations  0.92 us (1%)
    ppermute x9, starting transfers between devices, turn(): return lax.ppermute(x, 'fsdp', [(i, ring_hop(i, k, n)) for i in range(n)])  24.6 us
    ppermute x9, waiting for transfers between devices, turn(): return lax.ppermute(x, 'fsdp', [(i, ring_hop(i, k, n)) for i in range(n)])  18.7 us
    ppermute x11, waiting for transfers between devices, exchange(): return lax.ppermute(x, axis, [(i, i ^ k) for i in range(n)])  11.8 us
    ppermute x11, starting transfers between devices, exchange(): return lax.ppermute(x, axis, [(i, i ^ k) for i in range(n)])  7.41 us
    pallas_call x8, Pallas kernels, local(): pl.pallas_call(kernel, out_shape=tuple(shapes), in_specs=specs, out_specs...  2.93 us
    pallas_call x2, Pallas kernels, outer_pieces(): pl.pallas_call(functools.partial(piece_kernel, places), out_shape=(full_s...  2.92 us
    dynamic_slice x2, local copies, waits for them, and re-layouts, columns(): return lax.dynamic_slice(tokens, (0, block * rows), (seq_len, rows))  2.28 us
  transfers between devices with their start and end apart: 20, of which 12 were waited for; matrix products, arithmetic and copies ran while one was open for 2% of the time, Pallas kernels for 7%

profile of v5, /device:TPU:0, one launch (start us, length us, event | category | flops | bytes accessed | tf_op | source)
XLA Modules:
  0.0 74.0 jit_solution(8014852443097492112)
XLA Ops:
  0.7 1.1 %constant_dynamic-slice_fusion.3 = bf16[128,1024]{1,0:T(8,128)(2,1)S(1)} fusion(bf16[128,4096]{1,0:T(8,128)(2,1)} %param.8, s32[]{:T(128)S(6)} %select_n.32), kind=kLoop, calls=%fused_computation.3 | loop fusion | bytes 524292 | tf_op jit(solution)/shard_map/dynamic_slice | solution.py:260
  1.8 5.1 %collective-permute-start = (bf16[128,1024]{1,0:T(8,128)(2,1)S(1)}, bf16[128,1024]{1,0:T(8,128)(2,1)S(1)}, u32[]{:S(2)}, u32[]{:S(2)}) collective-permute-start(bf16[128,1024]{1,0:T(8,128)(2,1)S(1)} %constant_dynamic-slice_fusion.3), channel_id=1, source_target_pairs={{0,3},{1,2},{2,1},{3,0},{4,7},{5,6},{6,5},{7,4},{8,11},{9,10},{10,... | collective-permute-start | bytes 786440 | tf_op jit(solution)/shard_map/ppermute | solution.py:242
  6.9 1.2 %constant_dynamic-slice_fusion = (bf16[128,1024]{1,0:T(8,128)(2,1)S(1)}, bf16[128,1024]{1,0:T(8,128)(2,1)S(1)}, bf16[128,1024]{1,0:T(8,128)(2,1)S(1)}) fusion(bf16[128,4096]{1,0:T(8,128)(2,1)} %param.8, s32[]{:T(128)S(6)} %select_n.38, s32[]{:T(128)S(6)} %select_n.36, s32[]{:T(128)S(6)} %select_n.34), kind=kLoop, calls=%fused_computation | loop fusion | bytes 1572876 | tf_op jit(solution)/shard_map/dynamic_slice | solution.py:260
  8.1 0.1 collective-permute-start.2
  8.1 2.0 %collective-permute-start.1 = (bf16[128,1024]{1,0:T(8,128)(2,1)S(1)}, bf16[128,1024]{1,0:T(8,128)(2,1)S(1)}, u32[]{:S(2)}, u32[]{:S(2)}) collective-permute-start(bf16[128,1024]{1,0:T(8,128)(2,1)S(1)} %get-tuple-element.33), channel_id=1, source_target_pairs={{0,1},{1,3},{2,0},{3,2},{4,5},{5,7},{6,4},{7,6},{8,9},{9,11},{10,8... | collective-permute-start | bytes 786440 | tf_op jit(solution)/shard_map/ppermute | solution.py:242
  10.1 0.3 own_value.1
  10.5 3.7 %collective-permute-done.refs_1_.refs_0_ = bf16[128,1024]{1,0:T(8,128)(2,1)S(1)} collective-permute-done((bf16[128,1024]{1,0:T(8,128)(2,1)S(1)}, bf16[128,1024]{1,0:T(8,128)(2,1)S(1)}, u32[]{:S(2)}, u32[]{:S(2)}) %collective-permute-start) | collective-permute-done | bytes 262176 | tf_op jit(solution)/shard_map/ppermute | solution.py:242
  14.2 0.3 partial_value.4
  14.5 0.0 copy-start.4
  14.5 12.2 %collective-permute-start.3 = (bf16[128,512]{1,0:T(8,128)(2,1)S(1)}, bf16[128,512]{1,0:T(8,128)(2,1)S(1)}, u32[]{:S(2)}, u32[]{:S(2)}) collective-permute-start(bf16[128,512]{1,0:T(8,128)(2,1)S(1)} %partial_value.4), channel_id=1, source_target_pairs={{0,2},{1,0},{2,3},{3,1},{4,6},{5,4},{6,7},{7,5},{8,10},{9,8},{10,1... | collective-permute-start | bytes 393224 | tf_op jit(solution)/shard_map/ppermute | solution.py:242
  26.7 0.3 partial_value.5
  27.0 0.1 collective-permute-start.5
  27.1 6.0 %collective-permute-done.1.refs_2_.refs_0_ = bf16[128,1024]{1,0:T(8,128)(2,1)S(1)} collective-permute-done((bf16[128,1024]{1,0:T(8,128)(2,1)S(1)}, bf16[128,1024]{1,0:T(8,128)(2,1)S(1)}, u32[]{:S(2)}, u32[]{:S(2)}) %collective-permute-start.1) | collective-permute-done | bytes 262176 | tf_op jit(solution)/shard_map/ppermute | solution.py:242
  33.1 0.3 partial_value.3.one
  33.4 0.0 copy-start.2
  33.4 0.0 copy-start.3
  33.4 0.1 collective-permute-start.4
  33.5 1.5 %attention.1 = (bf16[128,512]{1,0:T(8,128)(2,1)S(1)}, bf16[128,512]{1,0:T(8,128)(2,1)S(1)}, f32[128,512]{1,0:T(8,128)S(1)}) custom-call(bf16[128,2048]{1,0:T(8,128)(2,1)S(1)} %copy-done.4, bf16[128,512]{1,0:T(8,128)(2,1)S(1)} %copy-done.6, bf16[128,2048]{1,0:T(8,128)(2,1)S(1)} %copy-done.5), custom_call_target="tpu_custom_call" | custom-call | flops 201326592 | bytes 1048576 | tf_op jit(solution)/shard_map/attention/pallas_call | solution.py:270
  35.0 1.4 %collective-permute-done.5.refs_2_ = bf16[128,512]{1,0:T(8,128)(2,1)S(1)} collective-permute-done((bf16[128,512]{1,0:T(8,128)(2,1)S(1)}, bf16[128,512]{1,0:T(8,128)(2,1)S(1)}, u32[]{:S(2)}, u32[]{:S(2)}) %collective-permute-start.5) | collective-permute-done | bytes 131104 | tf_op jit(solution)/shard_map/ppermute | solution.py:242
  36.4 2.0 %collective-permute-done.4.refs_1_ = bf16[128,512]{1,0:T(8,128)(2,1)S(1)} collective-permute-done((bf16[128,512]{1,0:T(8,128)(2,1)S(1)}, bf16[128,512]{1,0:T(8,128)(2,1)S(1)}, u32[]{:S(2)}, u32[]{:S(2)}) %collective-permute-start.4) | collective-permute-done | bytes 131104 | tf_op jit(solution)/shard_map/ppermute | solution.py:242
  38.5 0.2 value_grad.1.refs_0_
  38.7 1.2 %collective-permute-start.8 = (bf16[128,512]{1,0:T(8,128)(2,1)S(1)}, bf16[128,512]{1,0:T(8,128)(2,1)S(1)}, u32[]{:S(2)}, u32[]{:S(2)}) collective-permute-start(bf16[128,512]{1,0:T(8,128)(2,1)S(1)} %value_grad.1.refs_0_), channel_id=1, source_target_pairs={{0,2},{1,0},{2,3},{3,1},{4,6},{5,4},{6,7},{7,5},{8,10},{9,8},{10,1... | collective-permute-start | bytes 393224 | tf_op jit(solution)/shard_map/ppermute | solution.py:242
  39.9 0.9 %collective-permute-start.7 = (bf16[128,512]{1,0:T(8,128)(2,1)S(1)}, bf16[128,512]{1,0:T(8,128)(2,1)S(1)}, u32[]{:S(2)}, u32[]{:S(2)}) collective-permute-start(bf16[128,512]{1,0:T(8,128)(2,1)S(1)} %value_grad.1.refs_0_), channel_id=1, source_target_pairs={{0,1},{1,3},{2,0},{3,2},{4,5},{5,7},{6,4},{7,6},{8,9},{9,11},{10,8... | collective-permute-start | bytes 393224 | tf_op jit(solution)/shard_map/ppermute | solution.py:242
  40.8 3.0 %collective-permute-start.6 = (bf16[128,512]{1,0:T(8,128)(2,1)S(1)}, bf16[128,512]{1,0:T(8,128)(2,1)S(1)}, u32[]{:S(2)}, u32[]{:S(2)}) collective-permute-start(bf16[128,512]{1,0:T(8,128)(2,1)S(1)} %value_grad.1.refs_0_), channel_id=1, source_target_pairs={{0,3},{1,2},{2,1},{3,0},{4,7},{5,6},{6,5},{7,4},{8,11},{9,10},{10,... | collective-permute-start | bytes 393224 | tf_op jit(solution)/shard_map/ppermute | solution.py:242
  43.8 0.3 transpose_tokens.1.features
  44.1 1.4 %collective-permute-done.8.refs_3_ = bf16[128,512]{1,0:T(8,128)(2,1)S(1)} collective-permute-done((bf16[128,512]{1,0:T(8,128)(2,1)S(1)}, bf16[128,512]{1,0:T(8,128)(2,1)S(1)}, u32[]{:S(2)}, u32[]{:S(2)}) %collective-permute-start.8) | collective-permute-done | bytes 131104 | tf_op jit(solution)/shard_map/ppermute | solution.py:242
  45.6 4.2 %collective-permute-done.7.refs_2_ = bf16[128,512]{1,0:T(8,128)(2,1)S(1)} collective-permute-done((bf16[128,512]{1,0:T(8,128)(2,1)S(1)}, bf16[128,512]{1,0:T(8,128)(2,1)S(1)}, u32[]{:S(2)}, u32[]{:S(2)}) %collective-permute-start.7) | collective-permute-done | bytes 131104 | tf_op jit(solution)/shard_map/ppermute | solution.py:242
  49.8 0.9 %direction.3 = bf16[512,512]{1,0:T(8,128)(2,1)S(1)} custom-call(bf16[1024,512]{1,0:T(8,128)(2,1)S(1)} %transpose_tokens.1.features, bf16[128,512]{1,0:T(8,128)(2,1)S(1)} %value_grad.1.refs_0_, bf16[128,512]{1,0:T(8,128)(2,1)S(1)} %collective-permute-done.6.refs_1_, bf16[128,512]{1,0:T(8,128)(2,1)S(1)} %collective-permute-done.7.refs_2_, ...), custom_call_target="tpu_custom_call" | custom-call | flops 268435456 | bytes 8388608 | tf_op jit(solution)/shard_map/direction/pallas_call | solution.py:88
  50.7 0.1 collective-permute-start.9
  50.8 0.9 %direction.2.mine = f32[512,512]{1,0:T(8,128)S(1)} custom-call(bf16[1024,512]{1,0:T(8,128)(2,1)S(1)} %transpose_tokens.1.features, bf16[128,512]{1,0:T(8,128)(2,1)S(1)} %value_grad.1.refs_0_, bf16[128,512]{1,0:T(8,128)(2,1)S(1)} %collective-permute-done.6.refs_1_, bf16[128,512]{1,0:T(8,128)(2,1)S(1)} %collective-permute-done.7.refs_2_, ...), custom_call_target="tpu_custom_call" | custom-call | flops 268435456 | bytes 8912896 | tf_op jit(solution)/shard_map/direction/pallas_call | solution.py:88
  51.7 0.0 copy-start.1
  51.7 1.0 %collective-permute-done.9.theirs = bf16[512,512]{1,0:T(8,128)(2,1)S(1)} collective-permute-done((bf16[512,512]{1,0:T(8,128)(2,1)S(1)}, bf16[512,512]{1,0:T(8,128)(2,1)S(1)}, u32[]{:S(2)}, u32[]{:S(2)}) %collective-permute-start.9) | collective-permute-done | bytes 524320 | tf_op jit(solution)/shard_map/ppermute | solution.py:226
  52.7 0.1 chip_sum.1
  52.8 1.6 %collective-permute-start.10 = (bf16[128,512]{1,0:T(8,128)(2,1)S(1)}, bf16[128,512]{1,0:T(8,128)(2,1)S(1)}, u32[]{:S(2)}, u32[]{:S(2)}) collective-permute-start(bf16[128,512]{1,0:T(8,128)(2,1)S(1)} %get-tuple-element.27), channel_id=1, source_target_pairs={{0,8},{4,12},{8,0},{12,4},{16,24},{20,28},{24,16},{28,20},{1,9},{5... | collective-permute-start | bytes 393224 | tf_op jit(solution)/shard_map/ppermute | solution.py:226
  54.4 1.5 %collective-permute-start.11 = (bf16[128,512]{1,0:T(8,128)(2,1)S(1)}, bf16[128,512]{1,0:T(8,128)(2,1)S(1)}, u32[]{:S(2)}, u32[]{:S(2)}) collective-permute-start(bf16[128,512]{1,0:T(8,128)(2,1)S(1)} %get-tuple-element.28), channel_id=1, source_target_pairs={{0,16},{4,20},{8,24},{12,28},{16,0},{20,4},{24,8},{28,12},{1,17},{... | collective-permute-start | bytes 393224 | tf_op jit(solution)/shard_map/ppermute | solution.py:226
  55.9 0.5 collective-permute-start.12
  56.3 2.4 %collective-permute-done.10.refs_0_ = bf16[128,512]{1,0:T(8,128)(2,1)S(1)} collective-permute-done((bf16[128,512]{1,0:T(8,128)(2,1)S(1)}, bf16[128,512]{1,0:T(8,128)(2,1)S(1)}, u32[]{:S(2)}, u32[]{:S(2)}) %collective-permute-start.10) | collective-permute-done | bytes 131104 | tf_op jit(solution)/shard_map/ppermute | solution.py:226
  58.7 3.7 %collective-permute-done.11.refs_1_ = bf16[128,512]{1,0:T(8,128)(2,1)S(1)} collective-permute-done((bf16[128,512]{1,0:T(8,128)(2,1)S(1)}, bf16[128,512]{1,0:T(8,128)(2,1)S(1)}, u32[]{:S(2)}, u32[]{:S(2)}) %collective-permute-start.11) | collective-permute-done | bytes 131104 | tf_op jit(solution)/shard_map/ppermute | solution.py:226
  62.4 0.1 mean_direction.1.refs_0_
  62.5 1.5 %collective-permute-start.18 = (bf16[128,512]{1,0:T(8,128)(2,1)S(1)}, bf16[128,512]{1,0:T(8,128)(2,1)S(1)}, u32[]{:S(2)}, u32[]{:S(2)}) collective-permute-start(bf16[128,512]{1,0:T(8,128)(2,1)S(1)} %mean_direction.1.refs_0_), channel_id=1, source_target_pairs={{0,24},{4,28},{8,16},{12,20},{16,8},{20,12},{24,0},{28,4},{1,25},{... | collective-permute-start | bytes 393224 | tf_op jit(solution)/shard_map/ppermute | solution.py:226
  64.0 1.2 %collective-permute-start.16 = (bf16[128,512]{1,0:T(8,128)(2,1)S(1)}, bf16[128,512]{1,0:T(8,128)(2,1)S(1)}, u32[]{:S(2)}, u32[]{:S(2)}) collective-permute-start(bf16[128,512]{1,0:T(8,128)(2,1)S(1)} %mean_direction.1.refs_0_), channel_id=1, source_target_pairs={{0,16},{4,20},{8,24},{12,28},{16,0},{20,4},{24,8},{28,12},{1,17},{... | collective-permute-start | bytes 393224 | tf_op jit(solution)/shard_map/ppermute | solution.py:226
  65.3 0.8 %collective-permute-start.14 = (bf16[128,512]{1,0:T(8,128)(2,1)S(1)}, bf16[128,512]{1,0:T(8,128)(2,1)S(1)}, u32[]{:S(2)}, u32[]{:S(2)}) collective-permute-start(bf16[128,512]{1,0:T(8,128)(2,1)S(1)} %mean_direction.1.refs_0_), channel_id=1, source_target_pairs={{0,8},{4,12},{8,0},{12,4},{16,24},{20,28},{24,16},{28,20},{1,9},{5... | collective-permute-start | bytes 393224 | tf_op jit(solution)/shard_map/ppermute | solution.py:226
  66.1 3.4 %collective-permute-done.18.refs_3_ = bf16[128,512]{1,0:T(8,128)(2,1)S(1)} collective-permute-done((bf16[128,512]{1,0:T(8,128)(2,1)S(1)}, bf16[128,512]{1,0:T(8,128)(2,1)S(1)}, u32[]{:S(2)}, u32[]{:S(2)}) %collective-permute-start.18) | collective-permute-done | bytes 131104 | tf_op jit(solution)/shard_map/ppermute | solution.py:226
  69.4 1.1 %collective-permute-done.16.refs_2_ = bf16[128,512]{1,0:T(8,128)(2,1)S(1)} collective-permute-done((bf16[128,512]{1,0:T(8,128)(2,1)S(1)}, bf16[128,512]{1,0:T(8,128)(2,1)S(1)}, u32[]{:S(2)}, u32[]{:S(2)}) %collective-permute-start.16) | collective-permute-done | bytes 131104 | tf_op jit(solution)/shard_map/ppermute | solution.py:226
  70.5 0.3 collective-permute-done.14.refs_1_
  70.8 0.2 collective-permute-start.15
  71.0 1.5 %outer_step.2 = (f32[1024,512]{1,0:T(8,128)}, f32[1024,512]{1,0:T(8,128)}) custom-call(bf16[128,512]{1,0:T(8,128)(2,1)S(1)} %mean_direction.1.refs_0_, bf16[128,512]{1,0:T(8,128)(2,1)S(1)} %collective-permute-done.14.refs_1_, bf16[128,512]{1,0:T(8,128)(2,1)S(1)} %collective-permute-done.16.refs_2_, bf16[128,512]{1,0:T(8,128)(2,1)S(1)} %collective-permute-done.18.refs_3_, ...), custom_call_target="tpu_custom_call" | custom-call | bytes 4718592 | tf_op jit(solution)/shard_map/outer_step/pallas_call | solution.py:210
  72.5 1.5 %outer_step.3 = (f32[1024,512]{1,0:T(8,128)}, f32[1024,512]{1,0:T(8,128)}) custom-call(bf16[128,512]{1,0:T(8,128)(2,1)S(1)} %collective-permute-done.13.refs_0_, bf16[128,512]{1,0:T(8,128)(2,1)S(1)} %collective-permute-done.15.refs_1_, bf16[128,512]{1,0:T(8,128)(2,1)S(1)} %collective-permute-done.17.refs_2_, ...), custom_call_target="tpu_custom_call", output_to_operand_aliasing={{0}: (6, {}), {1}: (7, {})} | custom-call | bytes 4718592 | tf_op jit(solution)/shard_map/outer_step/pallas_call | solution.py:210
  (22 shorter events, 0.1 us)
Async XLA Ops:
  0.6 9.5 %copy-start = (f32[1024,512]{1,0:T(8,128)S(1)}, f32[1024,512]{1,0:T(8,128)}, u32[]{:S(2)}) copy-start(f32[1024,512]{1,0:T(8,128)} %refs_5_.7) | copy-start | bytes 6291460
  1.8 12.4 %collective-permute-start = (bf16[128,1024]{1,0:T(8,128)(2,1)S(1)}, bf16[128,1024]{1,0:T(8,128)(2,1)S(1)}, u32[]{:S(2)}, u32[]{:S(2)}) collective-permute-start(bf16[128,1024]{1,0:T(8,128)(2,1)S(1)} %constant_dynamic-slice_fusion.3), channel_id=1, source_target_pairs={{0,3},{1,2},{2,1},{3,0},{4,7},{5,6},{6,5},{7,4},{8,11},{9,10},{10,... | collective-permute-start | bytes 786440 | tf_op jit(solution)/shard_map/ppermute | solution.py:242
  8.1 18.7 %collective-permute-start.2 = (bf16[128,1024]{1,0:T(8,128)(2,1)S(1)}, bf16[128,1024]{1,0:T(8,128)(2,1)S(1)}, u32[]{:S(2)}, u32[]{:S(2)}) collective-permute-start(bf16[128,1024]{1,0:T(8,128)(2,1)S(1)} %get-tuple-element.32), channel_id=1, source_target_pairs={{0,2},{1,0},{2,3},{3,1},{4,6},{5,4},{6,7},{7,5},{8,10},{9,8},{10,1... | collective-permute-start | bytes 786440 | tf_op jit(solution)/shard_map/ppermute | solution.py:242
  8.1 24.9 %collective-permute-start.1 = (bf16[128,1024]{1,0:T(8,128)(2,1)S(1)}, bf16[128,1024]{1,0:T(8,128)(2,1)S(1)}, u32[]{:S(2)}, u32[]{:S(2)}) collective-permute-start(bf16[128,1024]{1,0:T(8,128)(2,1)S(1)} %get-tuple-element.33), channel_id=1, source_target_pairs={{0,1},{1,3},{2,0},{3,2},{4,5},{5,7},{6,4},{7,6},{8,9},{9,11},{10,8... | collective-permute-start | bytes 786440 | tf_op jit(solution)/shard_map/ppermute | solution.py:242
  14.5 19.0 %copy-start.4 = (bf16[128,2048]{1,0:T(8,128)(2,1)S(1)}, bf16[128,2048]{1,0:T(8,128)(2,1)}, u32[]{:S(2)}) copy-start(bf16[128,2048]{1,0:T(8,128)(2,1)} %queries.1) | copy-start | bytes 1572868
  14.5 19.0 %copy-start.5 = (bf16[128,2048]{1,0:T(8,128)(2,1)S(1)}, bf16[128,2048]{1,0:T(8,128)(2,1)}, u32[]{:S(2)}) copy-start(bf16[128,2048]{1,0:T(8,128)(2,1)} %targets.1) | copy-start | bytes 1572868
  14.5 19.0 %copy-start.6 = (bf16[128,512]{1,0:T(8,128)(2,1)S(1)}, bf16[128,512]{1,0:T(8,128)(2,1)}, u32[]{:S(2)}) copy-start(bf16[128,512]{1,0:T(8,128)(2,1)} %keys.1) | copy-start | bytes 393220
  14.5 18.9 %collective-permute-start.3 = (bf16[128,512]{1,0:T(8,128)(2,1)S(1)}, bf16[128,512]{1,0:T(8,128)(2,1)S(1)}, u32[]{:S(2)}, u32[]{:S(2)}) collective-permute-start(bf16[128,512]{1,0:T(8,128)(2,1)S(1)} %partial_value.4), channel_id=1, source_target_pairs={{0,2},{1,0},{2,3},{3,1},{4,6},{5,4},{6,7},{7,5},{8,10},{9,8},{10,1... | collective-permute-start | bytes 393224 | tf_op jit(solution)/shard_map/ppermute | solution.py:242
  27.0 9.4 %collective-permute-start.5 = (bf16[128,512]{1,0:T(8,128)(2,1)S(1)}, bf16[128,512]{1,0:T(8,128)(2,1)S(1)}, u32[]{:S(2)}, u32[]{:S(2)}) collective-permute-start(bf16[128,512]{1,0:T(8,128)(2,1)S(1)} %partial_value.5), channel_id=1, source_target_pairs={{0,1},{1,3},{2,0},{3,2},{4,5},{5,7},{6,4},{7,6},{8,9},{9,11},{10,8... | collective-permute-start | bytes 393224 | tf_op jit(solution)/shard_map/ppermute | solution.py:242
  33.4 16.4 %copy-start.2 = (f32[1,1024,512]{2,1,0:T(8,128)S(1)}, f32[1,1024,512]{2,1,0:T(8,128)}, u32[]{:S(2)}) copy-start(f32[1,1024,512]{2,1,0:T(8,128)} %refs_4_.5) | copy-start | bytes 6291460
  33.4 16.4 %copy-start.3 = (f32[1,1024,512]{2,1,0:T(8,128)S(1)}, f32[1,1024,512]{2,1,0:T(8,128)}, u32[]{:S(2)}) copy-start(f32[1,1024,512]{2,1,0:T(8,128)} %refs_5_.5) | copy-start | bytes 6291460
  33.4 5.0 %collective-permute-start.4 = (bf16[128,512]{1,0:T(8,128)(2,1)S(1)}, bf16[128,512]{1,0:T(8,128)(2,1)S(1)}, u32[]{:S(2)}, u32[]{:S(2)}) collective-permute-start(bf16[128,512]{1,0:T(8,128)(2,1)S(1)} %joined_value.1), channel_id=1, source_target_pairs={{0,2},{1,0},{2,3},{3,1},{4,6},{5,4},{6,7},{7,5},{8,10},{9,8},{10,1... | collective-permute-start | bytes 393224 | tf_op jit(solution)/shard_map/ppermute | solution.py:242
  38.7 6.9 %collective-permute-start.8 = (bf16[128,512]{1,0:T(8,128)(2,1)S(1)}, bf16[128,512]{1,0:T(8,128)(2,1)S(1)}, u32[]{:S(2)}, u32[]{:S(2)}) collective-permute-start(bf16[128,512]{1,0:T(8,128)(2,1)S(1)} %value_grad.1.refs_0_), channel_id=1, source_target_pairs={{0,2},{1,0},{2,3},{3,1},{4,6},{5,4},{6,7},{7,5},{8,10},{9,8},{10,1... | collective-permute-start | bytes 393224 | tf_op jit(solution)/shard_map/ppermute | solution.py:242
  39.9 9.9 %collective-permute-start.7 = (bf16[128,512]{1,0:T(8,128)(2,1)S(1)}, bf16[128,512]{1,0:T(8,128)(2,1)S(1)}, u32[]{:S(2)}, u32[]{:S(2)}) collective-permute-start(bf16[128,512]{1,0:T(8,128)(2,1)S(1)} %value_grad.1.refs_0_), channel_id=1, source_target_pairs={{0,1},{1,3},{2,0},{3,2},{4,5},{5,7},{6,4},{7,6},{8,9},{9,11},{10,8... | collective-permute-start | bytes 393224 | tf_op jit(solution)/shard_map/ppermute | solution.py:242
  40.8 9.0 %collective-permute-start.6 = (bf16[128,512]{1,0:T(8,128)(2,1)S(1)}, bf16[128,512]{1,0:T(8,128)(2,1)S(1)}, u32[]{:S(2)}, u32[]{:S(2)}) collective-permute-start(bf16[128,512]{1,0:T(8,128)(2,1)S(1)} %value_grad.1.refs_0_), channel_id=1, source_target_pairs={{0,3},{1,2},{2,1},{3,0},{4,7},{5,6},{6,5},{7,4},{8,11},{9,10},{10,... | collective-permute-start | bytes 393224 | tf_op jit(solution)/shard_map/ppermute | solution.py:242
  50.7 2.0 %collective-permute-start.9 = (bf16[512,512]{1,0:T(8,128)(2,1)S(1)}, bf16[512,512]{1,0:T(8,128)(2,1)S(1)}, u32[]{:S(2)}, u32[]{:S(2)}) collective-permute-start(bf16[512,512]{1,0:T(8,128)(2,1)S(1)} %direction.3), channel_id=1, source_target_pairs={{0,4},{4,0},{8,12},{12,8},{16,20},{20,16},{24,28},{28,24},{1,5},{5... | collective-permute-start | bytes 1572872 | tf_op jit(solution)/shard_map/ppermute | solution.py:226
  51.7 19.3 %copy-start.1 = (f32[1024,512]{1,0:T(8,128)S(1)}, f32[1024,512]{1,0:T(8,128)}, u32[]{:S(2)}) copy-start(f32[1024,512]{1,0:T(8,128)} %refs_4_.7) | copy-start | bytes 6291460
  52.8 5.9 %collective-permute-start.10 = (bf16[128,512]{1,0:T(8,128)(2,1)S(1)}, bf16[128,512]{1,0:T(8,128)(2,1)S(1)}, u32[]{:S(2)}, u32[]{:S(2)}) collective-permute-start(bf16[128,512]{1,0:T(8,128)(2,1)S(1)} %get-tuple-element.27), channel_id=1, source_target_pairs={{0,8},{4,12},{8,0},{12,4},{16,24},{20,28},{24,16},{28,20},{1,9},{5... | collective-permute-start | bytes 393224 | tf_op jit(solution)/shard_map/ppermute | solution.py:226
  54.4 8.1 %collective-permute-start.11 = (bf16[128,512]{1,0:T(8,128)(2,1)S(1)}, bf16[128,512]{1,0:T(8,128)(2,1)S(1)}, u32[]{:S(2)}, u32[]{:S(2)}) collective-permute-start(bf16[128,512]{1,0:T(8,128)(2,1)S(1)} %get-tuple-element.28), channel_id=1, source_target_pairs={{0,16},{4,20},{8,24},{12,28},{16,0},{20,4},{24,8},{28,12},{1,17},{... | collective-permute-start | bytes 393224 | tf_op jit(solution)/shard_map/ppermute | solution.py:226
  55.9 6.6 %collective-permute-start.12 = (bf16[128,512]{1,0:T(8,128)(2,1)S(1)}, bf16[128,512]{1,0:T(8,128)(2,1)S(1)}, u32[]{:S(2)}, u32[]{:S(2)}) collective-permute-start(bf16[128,512]{1,0:T(8,128)(2,1)S(1)} %get-tuple-element.29), channel_id=1, source_target_pairs={{0,24},{4,28},{8,16},{12,20},{16,8},{20,12},{24,0},{28,4},{1,25},{... | collective-permute-start | bytes 393224 | tf_op jit(solution)/shard_map/ppermute | solution.py:226
  62.5 6.9 %collective-permute-start.18 = (bf16[128,512]{1,0:T(8,128)(2,1)S(1)}, bf16[128,512]{1,0:T(8,128)(2,1)S(1)}, u32[]{:S(2)}, u32[]{:S(2)}) collective-permute-start(bf16[128,512]{1,0:T(8,128)(2,1)S(1)} %mean_direction.1.refs_0_), channel_id=1, source_target_pairs={{0,24},{4,28},{8,16},{12,20},{16,8},{20,12},{24,0},{28,4},{1,25},{... | collective-permute-start | bytes 393224 | tf_op jit(solution)/shard_map/ppermute | solution.py:226
  64.0 6.5 %collective-permute-start.16 = (bf16[128,512]{1,0:T(8,128)(2,1)S(1)}, bf16[128,512]{1,0:T(8,128)(2,1)S(1)}, u32[]{:S(2)}, u32[]{:S(2)}) collective-permute-start(bf16[128,512]{1,0:T(8,128)(2,1)S(1)} %mean_direction.1.refs_0_), channel_id=1, source_target_pairs={{0,16},{4,20},{8,24},{12,28},{16,0},{20,4},{24,8},{28,12},{1,17},{... | collective-permute-start | bytes 393224 | tf_op jit(solution)/shard_map/ppermute | solution.py:226
  65.3 5.6 %collective-permute-start.14 = (bf16[128,512]{1,0:T(8,128)(2,1)S(1)}, bf16[128,512]{1,0:T(8,128)(2,1)S(1)}, u32[]{:S(2)}, u32[]{:S(2)}) collective-permute-start(bf16[128,512]{1,0:T(8,128)(2,1)S(1)} %mean_direction.1.refs_0_), channel_id=1, source_target_pairs={{0,8},{4,12},{8,0},{12,4},{16,24},{20,28},{24,16},{28,20},{1,9},{5... | collective-permute-start | bytes 393224 | tf_op jit(solution)/shard_map/ppermute | solution.py:226
  66.0 6.5 %collective-permute-start.13 = (bf16[128,512]{1,0:T(8,128)(2,1)S(1)}, bf16[128,512]{1,0:T(8,128)(2,1)S(1)}, u32[]{:S(2)}, u32[]{:S(2)}) collective-permute-start(bf16[128,512]{1,0:T(8,128)(2,1)S(1)} %mean_direction.1.refs_0_), channel_id=1, source_target_pairs={{0,4},{4,0},{8,12},{12,8},{16,20},{20,16},{24,28},{28,24},{1,5},{5... | collective-permute-start | bytes 393224 | tf_op jit(solution)/shard_map/ppermute | solution.py:226
  69.4 3.1 %collective-permute-start.19 = (bf16[128,512]{1,0:T(8,128)(2,1)S(1)}, bf16[128,512]{1,0:T(8,128)(2,1)S(1)}, u32[]{:S(2)}, u32[]{:S(2)}) collective-permute-start(bf16[128,512]{1,0:T(8,128)(2,1)S(1)} %collective-permute-done.18.refs_3_), channel_id=1, source_target_pairs={{0,4},{4,0},{8,12},{12,8},{16,20},{20,16},{24,28},{28,24},{1,5},{5... | collective-permute-start | bytes 393224 | tf_op jit(solution)/shard_map/ppermute | solution.py:226
  70.5 2.0 %collective-permute-start.17 = (bf16[128,512]{1,0:T(8,128)(2,1)S(1)}, bf16[128,512]{1,0:T(8,128)(2,1)S(1)}, u32[]{:S(2)}, u32[]{:S(2)}) collective-permute-start(bf16[128,512]{1,0:T(8,128)(2,1)S(1)} %collective-permute-done.16.refs_2_), channel_id=1, source_target_pairs={{0,4},{4,0},{8,12},{12,8},{16,20},{20,16},{24,28},{28,24},{1,5},{5... | collective-permute-start | bytes 393224 | tf_op jit(solution)/shard_map/ppermute | solution.py:226
  70.8 1.7 %collective-permute-start.15 = (bf16[128,512]{1,0:T(8,128)(2,1)S(1)}, bf16[128,512]{1,0:T(8,128)(2,1)S(1)}, u32[]{:S(2)}, u32[]{:S(2)}) collective-permute-start(bf16[128,512]{1,0:T(8,128)(2,1)S(1)} %collective-permute-done.14.refs_1_), channel_id=1, source_target_pairs={{0,4},{4,0},{8,12},{12,8},{16,20},{20,16},{24,28},{28,24},{1,5},{5... | collective-permute-start | bytes 393224 | tf_op jit(solution)/shard_map/ppermute | solution.py:226

commit v6 on v5

--- a/solution.py
+++ b/solution.py
@@ -121,7 +121,8 @@
     summed = dot(features[at, :], stacked)
     first_new = first_decay * first[0, at, :] + (1.0 - first_decay) / math.sqrt(D) * summed
     second_new = second_decay * second[0, at, :] + (1.0 - second_decay) / D * summed * summed
-    return first_new / (jnp.sqrt(second_new) + epsilon) + weight_decay * weights[at, :]
+    root = second_new * lax.rsqrt(second_new)
+    return first_new / (root + epsilon) + weight_decay * weights[at, :]
 
 
 def rows_at(start, count):
@@ -368,10 +369,11 @@
     got = to_chips([mean] * 3)
     theirs = [exchange(g, "rep", 1) for g in (mean, *got)]
     outs = outer_pieces(
-        tuple((k, False) for k in range(4)), [mean, *got], momentum, value_weights, ()
+        (*[(k, False) for k in range(4)], (0, True), (3, True)), [mean, *got, theirs[0], theirs[3]],
+        momentum, value_weights, (),
     )
     return tuple(
-        outer_pieces(tuple((k, True) for k in range(4)), theirs, momentum, value_weights, outs)
+        outer_pieces(((1, True), (2, True)), theirs[1:3], momentum, value_weights, outs)
     )
 
 

time: 74.2 us -> 74 us (level)
  transfers between devices with their start and end apart: 20 -> 20, of which waited for: 12 -> 12; matrix products, arithmetic and copies ran while one was open for 2% -> 2% of each run, Pallas kernels for 7% -> 8%
where the time goes in v6:
time: 74 us; the launch traced here: 73.8 us
  starting transfers between devices  32 us (43%)
  waiting for transfers between devices  30.7 us (41%)
  Pallas kernels  7.87 us (11%)
  local copies, waits for them, and re-layouts  2.32 us (3%)
  between operations  0.91 us (1%)
    ppermute x9, starting transfers between devices, turn(): return lax.ppermute(x, 'fsdp', [(i, ring_hop(i, k, n)) for i in range(n)])  24.6 us
    ppermute x9, waiting for transfers between devices, turn(): return lax.ppermute(x, 'fsdp', [(i, ring_hop(i, k, n)) for i in range(n)])  18.7 us
    ppermute x11, waiting for transfers between devices, exchange(): return lax.ppermute(x, axis, [(i, i ^ k) for i in range(n)])  12 us
    ppermute x11, starting transfers between devices, exchange(): return lax.ppermute(x, axis, [(i, i ^ k) for i in range(n)])  7.41 us
    pallas_call x2, Pallas kernels, outer_pieces(): pl.pallas_call(functools.partial(piece_kernel, places), out_shape=(full_s...  2.93 us
    pallas_call x8, Pallas kernels, local(): pl.pallas_call(kernel, out_shape=tuple(shapes), in_specs=specs, out_specs...  2.58 us
    dynamic_slice x2, local copies, waits for them, and re-layouts, columns(): return lax.dynamic_slice(tokens, (0, block * rows), (seq_len, rows))  2.28 us
  transfers between devices with their start and end apart: 20, of which 12 were waited for; matrix products, arithmetic and copies ran while one was open for 2% of the time, Pallas kernels for 8%

profile of v6, /device:TPU:0, one launch (start us, length us, event | category | flops | bytes accessed | tf_op | source)
XLA Modules:
  0.0 73.8 jit_solution(9149007032201691715)
XLA Ops:
  0.7 1.1 %constant_dynamic-slice_fusion.3 = bf16[128,1024]{1,0:T(8,128)(2,1)S(1)} fusion(bf16[128,4096]{1,0:T(8,128)(2,1)} %param.8, s32[]{:T(128)S(6)} %select_n.32), kind=kLoop, calls=%fused_computation.3 | loop fusion | bytes 524292 | tf_op jit(solution)/shard_map/dynamic_slice | solution.py:261
  1.8 5.1 %collective-permute-start = (bf16[128,1024]{1,0:T(8,128)(2,1)S(1)}, bf16[128,1024]{1,0:T(8,128)(2,1)S(1)}, u32[]{:S(2)}, u32[]{:S(2)}) collective-permute-start(bf16[128,1024]{1,0:T(8,128)(2,1)S(1)} %constant_dynamic-slice_fusion.3), channel_id=1, source_target_pairs={{0,3},{1,2},{2,1},{3,0},{4,7},{5,6},{6,5},{7,4},{8,11},{9,10},{10,... | collective-permute-start | bytes 786440 | tf_op jit(solution)/shard_map/ppermute | solution.py:243
  6.9 1.2 %constant_dynamic-slice_fusion = (bf16[128,1024]{1,0:T(8,128)(2,1)S(1)}, bf16[128,1024]{1,0:T(8,128)(2,1)S(1)}, bf16[128,1024]{1,0:T(8,128)(2,1)S(1)}) fusion(bf16[128,4096]{1,0:T(8,128)(2,1)} %param.8, s32[]{:T(128)S(6)} %select_n.38, s32[]{:T(128)S(6)} %select_n.36, s32[]{:T(128)S(6)} %select_n.34), kind=kLoop, calls=%fused_computation | loop fusion | bytes 1572876 | tf_op jit(solution)/shard_map/dynamic_slice | solution.py:261
  8.1 0.1 collective-permute-start.2
  8.1 2.0 %collective-permute-start.1 = (bf16[128,1024]{1,0:T(8,128)(2,1)S(1)}, bf16[128,1024]{1,0:T(8,128)(2,1)S(1)}, u32[]{:S(2)}, u32[]{:S(2)}) collective-permute-start(bf16[128,1024]{1,0:T(8,128)(2,1)S(1)} %get-tuple-element.33), channel_id=1, source_target_pairs={{0,1},{1,3},{2,0},{3,2},{4,5},{5,7},{6,4},{7,6},{8,9},{9,11},{10,8... | collective-permute-start | bytes 786440 | tf_op jit(solution)/shard_map/ppermute | solution.py:243
  10.1 0.3 own_value.1
  10.5 3.7 %collective-permute-done.refs_1_.refs_0_ = bf16[128,1024]{1,0:T(8,128)(2,1)S(1)} collective-permute-done((bf16[128,1024]{1,0:T(8,128)(2,1)S(1)}, bf16[128,1024]{1,0:T(8,128)(2,1)S(1)}, u32[]{:S(2)}, u32[]{:S(2)}) %collective-permute-start) | collective-permute-done | bytes 262176 | tf_op jit(solution)/shard_map/ppermute | solution.py:243
  14.2 0.3 partial_value.4
  14.5 0.0 copy-start.4
  14.5 0.0 copy-start.5
  14.5 12.2 %collective-permute-start.3 = (bf16[128,512]{1,0:T(8,128)(2,1)S(1)}, bf16[128,512]{1,0:T(8,128)(2,1)S(1)}, u32[]{:S(2)}, u32[]{:S(2)}) collective-permute-start(bf16[128,512]{1,0:T(8,128)(2,1)S(1)} %partial_value.4), channel_id=1, source_target_pairs={{0,2},{1,0},{2,3},{3,1},{4,6},{5,4},{6,7},{7,5},{8,10},{9,8},{10,1... | collective-permute-start | bytes 393224 | tf_op jit(solution)/shard_map/ppermute | solution.py:243
  26.7 0.3 partial_value.5
  27.0 0.1 collective-permute-start.5
  27.1 6.0 %collective-permute-done.1.refs_2_.refs_0_ = bf16[128,1024]{1,0:T(8,128)(2,1)S(1)} collective-permute-done((bf16[128,1024]{1,0:T(8,128)(2,1)S(1)}, bf16[128,1024]{1,0:T(8,128)(2,1)S(1)}, u32[]{:S(2)}, u32[]{:S(2)}) %collective-permute-start.1) | collective-permute-done | bytes 262176 | tf_op jit(solution)/shard_map/ppermute | solution.py:243
  33.1 0.3 partial_value.3.one
  33.4 0.0 copy-start.1
  33.4 0.0 copy-start.2
  33.4 0.1 collective-permute-start.4
  33.5 1.5 %attention.1 = (bf16[128,512]{1,0:T(8,128)(2,1)S(1)}, bf16[128,512]{1,0:T(8,128)(2,1)S(1)}, f32[128,512]{1,0:T(8,128)S(1)}) custom-call(bf16[128,2048]{1,0:T(8,128)(2,1)S(1)} %copy-done.4, bf16[128,512]{1,0:T(8,128)(2,1)S(1)} %copy-done.6, bf16[128,2048]{1,0:T(8,128)(2,1)S(1)} %copy-done.5), custom_call_target="tpu_custom_call" | custom-call | flops 201326592 | bytes 1048576 | tf_op jit(solution)/shard_map/attention/pallas_call | solution.py:271
  35.0 1.4 %collective-permute-done.5.refs_2_ = bf16[128,512]{1,0:T(8,128)(2,1)S(1)} collective-permute-done((bf16[128,512]{1,0:T(8,128)(2,1)S(1)}, bf16[128,512]{1,0:T(8,128)(2,1)S(1)}, u32[]{:S(2)}, u32[]{:S(2)}) %collective-permute-start.5) | collective-permute-done | bytes 131104 | tf_op jit(solution)/shard_map/ppermute | solution.py:243
  36.4 2.0 %collective-permute-done.4.refs_1_ = bf16[128,512]{1,0:T(8,128)(2,1)S(1)} collective-permute-done((bf16[128,512]{1,0:T(8,128)(2,1)S(1)}, bf16[128,512]{1,0:T(8,128)(2,1)S(1)}, u32[]{:S(2)}, u32[]{:S(2)}) %collective-permute-start.4) | collective-permute-done | bytes 131104 | tf_op jit(solution)/shard_map/ppermute | solution.py:243
  38.5 0.2 value_grad.1.refs_0_
  38.7 1.2 %collective-permute-start.8 = (bf16[128,512]{1,0:T(8,128)(2,1)S(1)}, bf16[128,512]{1,0:T(8,128)(2,1)S(1)}, u32[]{:S(2)}, u32[]{:S(2)}) collective-permute-start(bf16[128,512]{1,0:T(8,128)(2,1)S(1)} %value_grad.1.refs_0_), channel_id=1, source_target_pairs={{0,2},{1,0},{2,3},{3,1},{4,6},{5,4},{6,7},{7,5},{8,10},{9,8},{10,1... | collective-permute-start | bytes 393224 | tf_op jit(solution)/shard_map/ppermute | solution.py:243
  39.9 0.9 %collective-permute-start.7 = (bf16[128,512]{1,0:T(8,128)(2,1)S(1)}, bf16[128,512]{1,0:T(8,128)(2,1)S(1)}, u32[]{:S(2)}, u32[]{:S(2)}) collective-permute-start(bf16[128,512]{1,0:T(8,128)(2,1)S(1)} %value_grad.1.refs_0_), channel_id=1, source_target_pairs={{0,1},{1,3},{2,0},{3,2},{4,5},{5,7},{6,4},{7,6},{8,9},{9,11},{10,8... | collective-permute-start | bytes 393224 | tf_op jit(solution)/shard_map/ppermute | solution.py:243
  40.8 3.0 %collective-permute-start.6 = (bf16[128,512]{1,0:T(8,128)(2,1)S(1)}, bf16[128,512]{1,0:T(8,128)(2,1)S(1)}, u32[]{:S(2)}, u32[]{:S(2)}) collective-permute-start(bf16[128,512]{1,0:T(8,128)(2,1)S(1)} %value_grad.1.refs_0_), channel_id=1, source_target_pairs={{0,3},{1,2},{2,1},{3,0},{4,7},{5,6},{6,5},{7,4},{8,11},{9,10},{10,... | collective-permute-start | bytes 393224 | tf_op jit(solution)/shard_map/ppermute | solution.py:243
  43.8 0.3 transpose_tokens.1.features
  44.1 1.4 %collective-permute-done.8.refs_3_ = bf16[128,512]{1,0:T(8,128)(2,1)S(1)} collective-permute-done((bf16[128,512]{1,0:T(8,128)(2,1)S(1)}, bf16[128,512]{1,0:T(8,128)(2,1)S(1)}, u32[]{:S(2)}, u32[]{:S(2)}) %collective-permute-start.8) | collective-permute-done | bytes 131104 | tf_op jit(solution)/shard_map/ppermute | solution.py:243
  45.6 4.2 %collective-permute-done.7.refs_2_ = bf16[128,512]{1,0:T(8,128)(2,1)S(1)} collective-permute-done((bf16[128,512]{1,0:T(8,128)(2,1)S(1)}, bf16[128,512]{1,0:T(8,128)(2,1)S(1)}, u32[]{:S(2)}, u32[]{:S(2)}) %collective-permute-start.7) | collective-permute-done | bytes 131104 | tf_op jit(solution)/shard_map/ppermute | solution.py:243
  49.8 0.7 %direction.3 = bf16[512,512]{1,0:T(8,128)(2,1)S(1)} custom-call(bf16[1024,512]{1,0:T(8,128)(2,1)S(1)} %transpose_tokens.1.features, bf16[128,512]{1,0:T(8,128)(2,1)S(1)} %value_grad.1.refs_0_, bf16[128,512]{1,0:T(8,128)(2,1)S(1)} %collective-permute-done.6.refs_1_, bf16[128,512]{1,0:T(8,128)(2,1)S(1)} %collective-permute-done.7.refs_2_, ...), custom_call_target="tpu_custom_call" | custom-call | flops 268435456 | bytes 8388608 | tf_op jit(solution)/shard_map/direction/pallas_call | solution.py:88
  50.5 0.1 collective-permute-start.9
  50.6 0.7 direction.2.mine
  51.4 1.1 %collective-permute-done.9.theirs = bf16[512,512]{1,0:T(8,128)(2,1)S(1)} collective-permute-done((bf16[512,512]{1,0:T(8,128)(2,1)S(1)}, bf16[512,512]{1,0:T(8,128)(2,1)S(1)}, u32[]{:S(2)}, u32[]{:S(2)}) %collective-permute-start.9) | collective-permute-done | bytes 524320 | tf_op jit(solution)/shard_map/ppermute | solution.py:227
  52.5 0.1 chip_sum.1
  52.6 1.6 %collective-permute-start.10 = (bf16[128,512]{1,0:T(8,128)(2,1)S(1)}, bf16[128,512]{1,0:T(8,128)(2,1)S(1)}, u32[]{:S(2)}, u32[]{:S(2)}) collective-permute-start(bf16[128,512]{1,0:T(8,128)(2,1)S(1)} %get-tuple-element.27), channel_id=1, source_target_pairs={{0,8},{4,12},{8,0},{12,4},{16,24},{20,28},{24,16},{28,20},{1,9},{5... | collective-permute-start | bytes 393224 | tf_op jit(solution)/shard_map/ppermute | solution.py:227
  54.2 1.5 %collective-permute-start.11 = (bf16[128,512]{1,0:T(8,128)(2,1)S(1)}, bf16[128,512]{1,0:T(8,128)(2,1)S(1)}, u32[]{:S(2)}, u32[]{:S(2)}) collective-permute-start(bf16[128,512]{1,0:T(8,128)(2,1)S(1)} %get-tuple-element.28), channel_id=1, source_target_pairs={{0,16},{4,20},{8,24},{12,28},{16,0},{20,4},{24,8},{28,12},{1,17},{... | collective-permute-start | bytes 393224 | tf_op jit(solution)/shard_map/ppermute | solution.py:227
  55.7 0.5 collective-permute-start.12
  56.2 2.4 %collective-permute-done.10.refs_0_ = bf16[128,512]{1,0:T(8,128)(2,1)S(1)} collective-permute-done((bf16[128,512]{1,0:T(8,128)(2,1)S(1)}, bf16[128,512]{1,0:T(8,128)(2,1)S(1)}, u32[]{:S(2)}, u32[]{:S(2)}) %collective-permute-start.10) | collective-permute-done | bytes 131104 | tf_op jit(solution)/shard_map/ppermute | solution.py:227
  58.5 3.7 %collective-permute-done.11.refs_1_ = bf16[128,512]{1,0:T(8,128)(2,1)S(1)} collective-permute-done((bf16[128,512]{1,0:T(8,128)(2,1)S(1)}, bf16[128,512]{1,0:T(8,128)(2,1)S(1)}, u32[]{:S(2)}, u32[]{:S(2)}) %collective-permute-start.11) | collective-permute-done | bytes 131104 | tf_op jit(solution)/shard_map/ppermute | solution.py:227
  62.2 0.1 mean_direction.1.refs_0_
  62.3 1.5 %collective-permute-start.17 = (bf16[128,512]{1,0:T(8,128)(2,1)S(1)}, bf16[128,512]{1,0:T(8,128)(2,1)S(1)}, u32[]{:S(2)}, u32[]{:S(2)}) collective-permute-start(bf16[128,512]{1,0:T(8,128)(2,1)S(1)} %mean_direction.1.refs_0_), channel_id=1, source_target_pairs={{0,24},{4,28},{8,16},{12,20},{16,8},{20,12},{24,0},{28,4},{1,25},{... | collective-permute-start | bytes 393224 | tf_op jit(solution)/shard_map/ppermute | solution.py:227
  63.9 1.2 %collective-permute-start.15 = (bf16[128,512]{1,0:T(8,128)(2,1)S(1)}, bf16[128,512]{1,0:T(8,128)(2,1)S(1)}, u32[]{:S(2)}, u32[]{:S(2)}) collective-permute-start(bf16[128,512]{1,0:T(8,128)(2,1)S(1)} %mean_direction.1.refs_0_), channel_id=1, source_target_pairs={{0,16},{4,20},{8,24},{12,28},{16,0},{20,4},{24,8},{28,12},{1,17},{... | collective-permute-start | bytes 393224 | tf_op jit(solution)/shard_map/ppermute | solution.py:227
  65.1 0.8 %collective-permute-start.13 = (bf16[128,512]{1,0:T(8,128)(2,1)S(1)}, bf16[128,512]{1,0:T(8,128)(2,1)S(1)}, u32[]{:S(2)}, u32[]{:S(2)}) collective-permute-start(bf16[128,512]{1,0:T(8,128)(2,1)S(1)} %mean_direction.1.refs_0_), channel_id=1, source_target_pairs={{0,8},{4,12},{8,0},{12,4},{16,24},{20,28},{24,16},{28,20},{1,9},{5... | collective-permute-start | bytes 393224 | tf_op jit(solution)/shard_map/ppermute | solution.py:227
  65.9 3.4 %collective-permute-done.17.refs_3_ = bf16[128,512]{1,0:T(8,128)(2,1)S(1)} collective-permute-done((bf16[128,512]{1,0:T(8,128)(2,1)S(1)}, bf16[128,512]{1,0:T(8,128)(2,1)S(1)}, u32[]{:S(2)}, u32[]{:S(2)}) %collective-permute-start.17) | collective-permute-done | bytes 131104 | tf_op jit(solution)/shard_map/ppermute | solution.py:227
  69.3 1.1 %collective-permute-done.15.refs_2_ = bf16[128,512]{1,0:T(8,128)(2,1)S(1)} collective-permute-done((bf16[128,512]{1,0:T(8,128)(2,1)S(1)}, bf16[128,512]{1,0:T(8,128)(2,1)S(1)}, u32[]{:S(2)}, u32[]{:S(2)}) %collective-permute-start.15) | collective-permute-done | bytes 131104 | tf_op jit(solution)/shard_map/ppermute | solution.py:227
  70.3 0.3 collective-permute-done.13.refs_1_
  70.6 0.2 collective-permute-start.14
  70.9 1.8 %outer_step.2 = (f32[1024,512]{1,0:T(8,128)}, f32[1024,512]{1,0:T(8,128)}) custom-call(bf16[128,512]{1,0:T(8,128)(2,1)S(1)} %mean_direction.1.refs_0_, bf16[128,512]{1,0:T(8,128)(2,1)S(1)} %collective-permute-done.13.refs_1_, bf16[128,512]{1,0:T(8,128)(2,1)S(1)} %collective-permute-done.15.refs_2_, bf16[128,512]{1,0:T(8,128)(2,1)S(1)} %collective-permute-done.17.refs_3_, ...), custom_call_target="tpu_custom_call" | custom-call | bytes 7077888 | tf_op jit(solution)/shard_map/outer_step/pallas_call | solution.py:211
  72.7 1.1 %outer_step.3 = (f32[1024,512]{1,0:T(8,128)}, f32[1024,512]{1,0:T(8,128)}) custom-call(bf16[128,512]{1,0:T(8,128)(2,1)S(1)} %collective-permute-done.14.refs_0_, bf16[128,512]{1,0:T(8,128)(2,1)S(1)} %collective-permute-done.16.refs_1_, f32[1024,512]{1,0:T(8,128)S(1)} %copy-done.3, ...), custom_call_target="tpu_custom_call", output_to_operand_aliasing={{0}: (4, {}), {1}: (5, {})} | custom-call | bytes 2359296 | tf_op jit(solution)/shard_map/outer_step/pallas_call | solution.py:211
  (22 shorter events, 0.1 us)
Async XLA Ops:
  0.6 9.5 %copy-start = (f32[1024,512]{1,0:T(8,128)S(1)}, f32[1024,512]{1,0:T(8,128)}, u32[]{:S(2)}) copy-start(f32[1024,512]{1,0:T(8,128)} %refs_3_.1) | copy-start | bytes 6291460
  1.8 12.4 %collective-permute-start = (bf16[128,1024]{1,0:T(8,128)(2,1)S(1)}, bf16[128,1024]{1,0:T(8,128)(2,1)S(1)}, u32[]{:S(2)}, u32[]{:S(2)}) collective-permute-start(bf16[128,1024]{1,0:T(8,128)(2,1)S(1)} %constant_dynamic-slice_fusion.3), channel_id=1, source_target_pairs={{0,3},{1,2},{2,1},{3,0},{4,7},{5,6},{6,5},{7,4},{8,11},{9,10},{10,... | collective-permute-start | bytes 786440 | tf_op jit(solution)/shard_map/ppermute | solution.py:243
  8.1 18.7 %collective-permute-start.2 = (bf16[128,1024]{1,0:T(8,128)(2,1)S(1)}, bf16[128,1024]{1,0:T(8,128)(2,1)S(1)}, u32[]{:S(2)}, u32[]{:S(2)}) collective-permute-start(bf16[128,1024]{1,0:T(8,128)(2,1)S(1)} %get-tuple-element.32), channel_id=1, source_target_pairs={{0,2},{1,0},{2,3},{3,1},{4,6},{5,4},{6,7},{7,5},{8,10},{9,8},{10,1... | collective-permute-start | bytes 786440 | tf_op jit(solution)/shard_map/ppermute | solution.py:243
  8.1 24.9 %collective-permute-start.1 = (bf16[128,1024]{1,0:T(8,128)(2,1)S(1)}, bf16[128,1024]{1,0:T(8,128)(2,1)S(1)}, u32[]{:S(2)}, u32[]{:S(2)}) collective-permute-start(bf16[128,1024]{1,0:T(8,128)(2,1)S(1)} %get-tuple-element.33), channel_id=1, source_target_pairs={{0,1},{1,3},{2,0},{3,2},{4,5},{5,7},{6,4},{7,6},{8,9},{9,11},{10,8... | collective-permute-start | bytes 786440 | tf_op jit(solution)/shard_map/ppermute | solution.py:243
  14.5 19.0 %copy-start.4 = (bf16[128,2048]{1,0:T(8,128)(2,1)S(1)}, bf16[128,2048]{1,0:T(8,128)(2,1)}, u32[]{:S(2)}) copy-start(bf16[128,2048]{1,0:T(8,128)(2,1)} %queries.1) | copy-start | bytes 1572868
  14.5 19.0 %copy-start.5 = (bf16[128,2048]{1,0:T(8,128)(2,1)S(1)}, bf16[128,2048]{1,0:T(8,128)(2,1)}, u32[]{:S(2)}) copy-start(bf16[128,2048]{1,0:T(8,128)(2,1)} %targets.1) | copy-start | bytes 1572868
  14.5 19.0 %copy-start.6 = (bf16[128,512]{1,0:T(8,128)(2,1)S(1)}, bf16[128,512]{1,0:T(8,128)(2,1)}, u32[]{:S(2)}) copy-start(bf16[128,512]{1,0:T(8,128)(2,1)} %keys.1) | copy-start | bytes 393220
  14.5 18.9 %collective-permute-start.3 = (bf16[128,512]{1,0:T(8,128)(2,1)S(1)}, bf16[128,512]{1,0:T(8,128)(2,1)S(1)}, u32[]{:S(2)}, u32[]{:S(2)}) collective-permute-start(bf16[128,512]{1,0:T(8,128)(2,1)S(1)} %partial_value.4), channel_id=1, source_target_pairs={{0,2},{1,0},{2,3},{3,1},{4,6},{5,4},{6,7},{7,5},{8,10},{9,8},{10,1... | collective-permute-start | bytes 393224 | tf_op jit(solution)/shard_map/ppermute | solution.py:243
  27.0 9.4 %collective-permute-start.5 = (bf16[128,512]{1,0:T(8,128)(2,1)S(1)}, bf16[128,512]{1,0:T(8,128)(2,1)S(1)}, u32[]{:S(2)}, u32[]{:S(2)}) collective-permute-start(bf16[128,512]{1,0:T(8,128)(2,1)S(1)} %partial_value.5), channel_id=1, source_target_pairs={{0,1},{1,3},{2,0},{3,2},{4,5},{5,7},{6,4},{7,6},{8,9},{9,11},{10,8... | collective-permute-start | bytes 393224 | tf_op jit(solution)/shard_map/ppermute | solution.py:243
  33.4 16.4 %copy-start.1 = (f32[1,1024,512]{2,1,0:T(8,128)S(1)}, f32[1,1024,512]{2,1,0:T(8,128)}, u32[]{:S(2)}) copy-start(f32[1,1024,512]{2,1,0:T(8,128)} %refs_4_.3) | copy-start | bytes 6291460
  33.4 16.4 %copy-start.2 = (f32[1,1024,512]{2,1,0:T(8,128)S(1)}, f32[1,1024,512]{2,1,0:T(8,128)}, u32[]{:S(2)}) copy-start(f32[1,1024,512]{2,1,0:T(8,128)} %refs_5_.3) | copy-start | bytes 6291460
  33.4 5.0 %collective-permute-start.4 = (bf16[128,512]{1,0:T(8,128)(2,1)S(1)}, bf16[128,512]{1,0:T(8,128)(2,1)S(1)}, u32[]{:S(2)}, u32[]{:S(2)}) collective-permute-start(bf16[128,512]{1,0:T(8,128)(2,1)S(1)} %joined_value.1), channel_id=1, source_target_pairs={{0,2},{1,0},{2,3},{3,1},{4,6},{5,4},{6,7},{7,5},{8,10},{9,8},{10,1... | collective-permute-start | bytes 393224 | tf_op jit(solution)/shard_map/ppermute | solution.py:243
  38.7 6.9 %collective-permute-start.8 = (bf16[128,512]{1,0:T(8,128)(2,1)S(1)}, bf16[128,512]{1,0:T(8,128)(2,1)S(1)}, u32[]{:S(2)}, u32[]{:S(2)}) collective-permute-start(bf16[128,512]{1,0:T(8,128)(2,1)S(1)} %value_grad.1.refs_0_), channel_id=1, source_target_pairs={{0,2},{1,0},{2,3},{3,1},{4,6},{5,4},{6,7},{7,5},{8,10},{9,8},{10,1... | collective-permute-start | bytes 393224 | tf_op jit(solution)/shard_map/ppermute | solution.py:243
  39.9 9.9 %collective-permute-start.7 = (bf16[128,512]{1,0:T(8,128)(2,1)S(1)}, bf16[128,512]{1,0:T(8,128)(2,1)S(1)}, u32[]{:S(2)}, u32[]{:S(2)}) collective-permute-start(bf16[128,512]{1,0:T(8,128)(2,1)S(1)} %value_grad.1.refs_0_), channel_id=1, source_target_pairs={{0,1},{1,3},{2,0},{3,2},{4,5},{5,7},{6,4},{7,6},{8,9},{9,11},{10,8... | collective-permute-start | bytes 393224 | tf_op jit(solution)/shard_map/ppermute | solution.py:243
  40.8 9.0 %collective-permute-start.6 = (bf16[128,512]{1,0:T(8,128)(2,1)S(1)}, bf16[128,512]{1,0:T(8,128)(2,1)S(1)}, u32[]{:S(2)}, u32[]{:S(2)}) collective-permute-start(bf16[128,512]{1,0:T(8,128)(2,1)S(1)} %value_grad.1.refs_0_), channel_id=1, source_target_pairs={{0,3},{1,2},{2,1},{3,0},{4,7},{5,6},{6,5},{7,4},{8,11},{9,10},{10,... | collective-permute-start | bytes 393224 | tf_op jit(solution)/shard_map/ppermute | solution.py:243
  50.5 2.0 %collective-permute-start.9 = (bf16[512,512]{1,0:T(8,128)(2,1)S(1)}, bf16[512,512]{1,0:T(8,128)(2,1)S(1)}, u32[]{:S(2)}, u32[]{:S(2)}) collective-permute-start(bf16[512,512]{1,0:T(8,128)(2,1)S(1)} %direction.3), channel_id=1, source_target_pairs={{0,4},{4,0},{8,12},{12,8},{16,20},{20,16},{24,28},{28,24},{1,5},{5... | collective-permute-start | bytes 1572872 | tf_op jit(solution)/shard_map/ppermute | solution.py:227
  51.4 19.5 %copy-start.3 = (f32[1024,512]{1,0:T(8,128)S(1)}, f32[1024,512]{1,0:T(8,128)}, u32[]{:S(2)}) copy-start(f32[1024,512]{1,0:T(8,128)} %refs_2_.1) | copy-start | bytes 6291460
  52.6 5.9 %collective-permute-start.10 = (bf16[128,512]{1,0:T(8,128)(2,1)S(1)}, bf16[128,512]{1,0:T(8,128)(2,1)S(1)}, u32[]{:S(2)}, u32[]{:S(2)}) collective-permute-start(bf16[128,512]{1,0:T(8,128)(2,1)S(1)} %get-tuple-element.27), channel_id=1, source_target_pairs={{0,8},{4,12},{8,0},{12,4},{16,24},{20,28},{24,16},{28,20},{1,9},{5... | collective-permute-start | bytes 393224 | tf_op jit(solution)/shard_map/ppermute | solution.py:227
  54.2 8.1 %collective-permute-start.11 = (bf16[128,512]{1,0:T(8,128)(2,1)S(1)}, bf16[128,512]{1,0:T(8,128)(2,1)S(1)}, u32[]{:S(2)}, u32[]{:S(2)}) collective-permute-start(bf16[128,512]{1,0:T(8,128)(2,1)S(1)} %get-tuple-element.28), channel_id=1, source_target_pairs={{0,16},{4,20},{8,24},{12,28},{16,0},{20,4},{24,8},{28,12},{1,17},{... | collective-permute-start | bytes 393224 | tf_op jit(solution)/shard_map/ppermute | solution.py:227
  55.7 6.6 %collective-permute-start.12 = (bf16[128,512]{1,0:T(8,128)(2,1)S(1)}, bf16[128,512]{1,0:T(8,128)(2,1)S(1)}, u32[]{:S(2)}, u32[]{:S(2)}) collective-permute-start(bf16[128,512]{1,0:T(8,128)(2,1)S(1)} %get-tuple-element.29), channel_id=1, source_target_pairs={{0,24},{4,28},{8,16},{12,20},{16,8},{20,12},{24,0},{28,4},{1,25},{... | collective-permute-start | bytes 393224 | tf_op jit(solution)/shard_map/ppermute | solution.py:227
  62.3 6.9 %collective-permute-start.17 = (bf16[128,512]{1,0:T(8,128)(2,1)S(1)}, bf16[128,512]{1,0:T(8,128)(2,1)S(1)}, u32[]{:S(2)}, u32[]{:S(2)}) collective-permute-start(bf16[128,512]{1,0:T(8,128)(2,1)S(1)} %mean_direction.1.refs_0_), channel_id=1, source_target_pairs={{0,24},{4,28},{8,16},{12,20},{16,8},{20,12},{24,0},{28,4},{1,25},{... | collective-permute-start | bytes 393224 | tf_op jit(solution)/shard_map/ppermute | solution.py:227
  63.9 6.5 %collective-permute-start.15 = (bf16[128,512]{1,0:T(8,128)(2,1)S(1)}, bf16[128,512]{1,0:T(8,128)(2,1)S(1)}, u32[]{:S(2)}, u32[]{:S(2)}) collective-permute-start(bf16[128,512]{1,0:T(8,128)(2,1)S(1)} %mean_direction.1.refs_0_), channel_id=1, source_target_pairs={{0,16},{4,20},{8,24},{12,28},{16,0},{20,4},{24,8},{28,12},{1,17},{... | collective-permute-start | bytes 393224 | tf_op jit(solution)/shard_map/ppermute | solution.py:227
  65.1 5.6 %collective-permute-start.13 = (bf16[128,512]{1,0:T(8,128)(2,1)S(1)}, bf16[128,512]{1,0:T(8,128)(2,1)S(1)}, u32[]{:S(2)}, u32[]{:S(2)}) collective-permute-start(bf16[128,512]{1,0:T(8,128)(2,1)S(1)} %mean_direction.1.refs_0_), channel_id=1, source_target_pairs={{0,8},{4,12},{8,0},{12,4},{16,24},{20,28},{24,16},{28,20},{1,9},{5... | collective-permute-start | bytes 393224 | tf_op jit(solution)/shard_map/ppermute | solution.py:227
  65.9 5.0 %collective-permute-start.18 = (bf16[128,512]{1,0:T(8,128)(2,1)S(1)}, bf16[128,512]{1,0:T(8,128)(2,1)S(1)}, u32[]{:S(2)}, u32[]{:S(2)}) collective-permute-start(bf16[128,512]{1,0:T(8,128)(2,1)S(1)} %mean_direction.1.refs_0_), channel_id=1, source_target_pairs={{0,4},{4,0},{8,12},{12,8},{16,20},{20,16},{24,28},{28,24},{1,5},{5... | collective-permute-start | bytes 393224 | tf_op jit(solution)/shard_map/ppermute | solution.py:227
  69.3 1.6 %collective-permute-start.19 = (bf16[128,512]{1,0:T(8,128)(2,1)S(1)}, bf16[128,512]{1,0:T(8,128)(2,1)S(1)}, u32[]{:S(2)}, u32[]{:S(2)}) collective-permute-start(bf16[128,512]{1,0:T(8,128)(2,1)S(1)} %collective-permute-done.17.refs_3_), channel_id=1, source_target_pairs={{0,4},{4,0},{8,12},{12,8},{16,20},{20,16},{24,28},{28,24},{1,5},{5... | collective-permute-start | bytes 393224 | tf_op jit(solution)/shard_map/ppermute | solution.py:227
  70.3 2.4 %collective-permute-start.16 = (bf16[128,512]{1,0:T(8,128)(2,1)S(1)}, bf16[128,512]{1,0:T(8,128)(2,1)S(1)}, u32[]{:S(2)}, u32[]{:S(2)}) collective-permute-start(bf16[128,512]{1,0:T(8,128)(2,1)S(1)} %collective-permute-done.15.refs_2_), channel_id=1, source_target_pairs={{0,4},{4,0},{8,12},{12,8},{16,20},{20,16},{24,28},{28,24},{1,5},{5... | collective-permute-start | bytes 393224 | tf_op jit(solution)/shard_map/ppermute | solution.py:227
  70.6 2.1 %collective-permute-start.14 = (bf16[128,512]{1,0:T(8,128)(2,1)S(1)}, bf16[128,512]{1,0:T(8,128)(2,1)S(1)}, u32[]{:S(2)}, u32[]{:S(2)}) collective-permute-start(bf16[128,512]{1,0:T(8,128)(2,1)S(1)} %collective-permute-done.13.refs_1_), channel_id=1, source_target_pairs={{0,4},{4,0},{8,12},{12,8},{16,20},{20,16},{24,28},{28,24},{1,5},{5... | collective-permute-start | bytes 393224 | tf_op jit(solution)/shard_map/ppermute | solution.py:227

commit v7 on v6

--- a/solution.py
+++ b/solution.py
@@ -113,7 +113,8 @@
     value = (total * (1.0 / math.sqrt(D))).astype(BF)
     for g in range(out.shape[1] // HEAD_SIZE):
         cols = slice(g * HEAD_SIZE, (g + 1) * HEAD_SIZE)
-        acc = dot(g_hi[:, cols], value[:, cols]) + dot(g_lo[:, cols], value[:, cols])
+        both = jnp.concatenate([g_hi[:, cols], g_lo[:, cols]], axis=1)
+        acc = dot(both, jnp.concatenate([value[:, cols]] * 2, axis=0))
         out[:, cols] = ((acc - cross[:, cols]) * scale).astype(BF)
 
 

time: 74 us -> 74 us (level)
  no operation moved by 1% of the time
where the time goes in v7:
time: 74 us; the launch traced here: 73.8 us
  starting transfers between devices  32 us (43%)
  waiting for transfers between devices  30.7 us (41%)
  Pallas kernels  7.86 us (11%)
  local copies, waits for them, and re-layouts  2.32 us (3%)
  between operations  0.91 us (1%)
    ppermute x9, starting transfers between devices, turn(): return lax.ppermute(x, 'fsdp', [(i, ring_hop(i, k, n)) for i in range(n)])  24.6 us
    ppermute x9, waiting for transfers between devices, turn(): return lax.ppermute(x, 'fsdp', [(i, ring_hop(i, k, n)) for i in range(n)])  18.7 us
    ppermute x11, waiting for transfers between devices, exchange(): return lax.ppermute(x, axis, [(i, i ^ k) for i in range(n)])  12 us
    ppermute x11, starting transfers between devices, exchange(): return lax.ppermute(x, axis, [(i, i ^ k) for i in range(n)])  7.42 us
    pallas_call x2, Pallas kernels, outer_pieces(): pl.pallas_call(functools.partial(piece_kernel, places), out_shape=(full_s...  2.93 us
    pallas_call x8, Pallas kernels, local(): pl.pallas_call(kernel, out_shape=tuple(shapes), in_specs=specs, out_specs...  2.58 us
    dynamic_slice x2, local copies, waits for them, and re-layouts, columns(): return lax.dynamic_slice(tokens, (0, block * rows), (seq_len, rows))  2.28 us
  transfers between devices with their start and end apart: 20, of which 12 were waited for; matrix products, arithmetic and copies ran while one was open for 2% of the time, Pallas kernels for 8%

profile of v7, /device:TPU:0, one launch (start us, length us, event | category | flops | bytes accessed | tf_op | source)
XLA Modules:
  0.0 73.8 jit_solution(10503071732426050095)
XLA Ops:
  0.7 1.1 %constant_dynamic-slice_fusion.3 = bf16[128,1024]{1,0:T(8,128)(2,1)S(1)} fusion(bf16[128,4096]{1,0:T(8,128)(2,1)} %param.8, s32[]{:T(128)S(6)} %select_n.32), kind=kLoop, calls=%fused_computation.3 | loop fusion | bytes 524292 | tf_op jit(solution)/shard_map/dynamic_slice | solution.py:262
  1.8 5.1 %collective-permute-start = (bf16[128,1024]{1,0:T(8,128)(2,1)S(1)}, bf16[128,1024]{1,0:T(8,128)(2,1)S(1)}, u32[]{:S(2)}, u32[]{:S(2)}) collective-permute-start(bf16[128,1024]{1,0:T(8,128)(2,1)S(1)} %constant_dynamic-slice_fusion.3), channel_id=1, source_target_pairs={{0,3},{1,2},{2,1},{3,0},{4,7},{5,6},{6,5},{7,4},{8,11},{9,10},{10,... | collective-permute-start | bytes 786440 | tf_op jit(solution)/shard_map/ppermute | solution.py:244
  6.9 1.2 %constant_dynamic-slice_fusion = (bf16[128,1024]{1,0:T(8,128)(2,1)S(1)}, bf16[128,1024]{1,0:T(8,128)(2,1)S(1)}, bf16[128,1024]{1,0:T(8,128)(2,1)S(1)}) fusion(bf16[128,4096]{1,0:T(8,128)(2,1)} %param.8, s32[]{:T(128)S(6)} %select_n.38, s32[]{:T(128)S(6)} %select_n.36, s32[]{:T(128)S(6)} %select_n.34), kind=kLoop, calls=%fused_computation | loop fusion | bytes 1572876 | tf_op jit(solution)/shard_map/dynamic_slice | solution.py:262
  8.1 0.1 collective-permute-start.2
  8.1 2.0 %collective-permute-start.1 = (bf16[128,1024]{1,0:T(8,128)(2,1)S(1)}, bf16[128,1024]{1,0:T(8,128)(2,1)S(1)}, u32[]{:S(2)}, u32[]{:S(2)}) collective-permute-start(bf16[128,1024]{1,0:T(8,128)(2,1)S(1)} %get-tuple-element.33), channel_id=1, source_target_pairs={{0,1},{1,3},{2,0},{3,2},{4,5},{5,7},{6,4},{7,6},{8,9},{9,11},{10,8... | collective-permute-start | bytes 786440 | tf_op jit(solution)/shard_map/ppermute | solution.py:244
  10.1 0.3 own_value.1
  10.5 3.7 %collective-permute-done.refs_1_.refs_0_ = bf16[128,1024]{1,0:T(8,128)(2,1)S(1)} collective-permute-done((bf16[128,1024]{1,0:T(8,128)(2,1)S(1)}, bf16[128,1024]{1,0:T(8,128)(2,1)S(1)}, u32[]{:S(2)}, u32[]{:S(2)}) %collective-permute-start) | collective-permute-done | bytes 262176 | tf_op jit(solution)/shard_map/ppermute | solution.py:244
  14.2 0.3 partial_value.4
  14.5 0.0 copy-start.4
  14.5 0.0 copy-start.5
  14.5 12.2 %collective-permute-start.3 = (bf16[128,512]{1,0:T(8,128)(2,1)S(1)}, bf16[128,512]{1,0:T(8,128)(2,1)S(1)}, u32[]{:S(2)}, u32[]{:S(2)}) collective-permute-start(bf16[128,512]{1,0:T(8,128)(2,1)S(1)} %partial_value.4), channel_id=1, source_target_pairs={{0,2},{1,0},{2,3},{3,1},{4,6},{5,4},{6,7},{7,5},{8,10},{9,8},{10,1... | collective-permute-start | bytes 393224 | tf_op jit(solution)/shard_map/ppermute | solution.py:244
  26.7 0.3 partial_value.5
  27.0 0.1 collective-permute-start.5
  27.1 6.0 %collective-permute-done.1.refs_2_.refs_0_ = bf16[128,1024]{1,0:T(8,128)(2,1)S(1)} collective-permute-done((bf16[128,1024]{1,0:T(8,128)(2,1)S(1)}, bf16[128,1024]{1,0:T(8,128)(2,1)S(1)}, u32[]{:S(2)}, u32[]{:S(2)}) %collective-permute-start.1) | collective-permute-done | bytes 262176 | tf_op jit(solution)/shard_map/ppermute | solution.py:244
  33.1 0.3 partial_value.3.one
  33.4 0.0 copy-start.1
  33.4 0.0 copy-start.2
  33.4 0.1 collective-permute-start.4
  33.5 1.5 %attention.1 = (bf16[128,512]{1,0:T(8,128)(2,1)S(1)}, bf16[128,512]{1,0:T(8,128)(2,1)S(1)}, f32[128,512]{1,0:T(8,128)S(1)}) custom-call(bf16[128,2048]{1,0:T(8,128)(2,1)S(1)} %copy-done.4, bf16[128,512]{1,0:T(8,128)(2,1)S(1)} %copy-done.6, bf16[128,2048]{1,0:T(8,128)(2,1)S(1)} %copy-done.5), custom_call_target="tpu_custom_call" | custom-call | flops 201326592 | bytes 1048576 | tf_op jit(solution)/shard_map/attention/pallas_call | solution.py:272
  35.0 1.4 %collective-permute-done.5.refs_2_ = bf16[128,512]{1,0:T(8,128)(2,1)S(1)} collective-permute-done((bf16[128,512]{1,0:T(8,128)(2,1)S(1)}, bf16[128,512]{1,0:T(8,128)(2,1)S(1)}, u32[]{:S(2)}, u32[]{:S(2)}) %collective-permute-start.5) | collective-permute-done | bytes 131104 | tf_op jit(solution)/shard_map/ppermute | solution.py:244
  36.4 2.0 %collective-permute-done.4.refs_1_ = bf16[128,512]{1,0:T(8,128)(2,1)S(1)} collective-permute-done((bf16[128,512]{1,0:T(8,128)(2,1)S(1)}, bf16[128,512]{1,0:T(8,128)(2,1)S(1)}, u32[]{:S(2)}, u32[]{:S(2)}) %collective-permute-start.4) | collective-permute-done | bytes 131104 | tf_op jit(solution)/shard_map/ppermute | solution.py:244
  38.5 0.2 value_grad.1.refs_0_
  38.7 1.2 %collective-permute-start.8 = (bf16[128,512]{1,0:T(8,128)(2,1)S(1)}, bf16[128,512]{1,0:T(8,128)(2,1)S(1)}, u32[]{:S(2)}, u32[]{:S(2)}) collective-permute-start(bf16[128,512]{1,0:T(8,128)(2,1)S(1)} %value_grad.1.refs_0_), channel_id=1, source_target_pairs={{0,2},{1,0},{2,3},{3,1},{4,6},{5,4},{6,7},{7,5},{8,10},{9,8},{10,1... | collective-permute-start | bytes 393224 | tf_op jit(solution)/shard_map/ppermute | solution.py:244
  39.9 0.9 %collective-permute-start.7 = (bf16[128,512]{1,0:T(8,128)(2,1)S(1)}, bf16[128,512]{1,0:T(8,128)(2,1)S(1)}, u32[]{:S(2)}, u32[]{:S(2)}) collective-permute-start(bf16[128,512]{1,0:T(8,128)(2,1)S(1)} %value_grad.1.refs_0_), channel_id=1, source_target_pairs={{0,1},{1,3},{2,0},{3,2},{4,5},{5,7},{6,4},{7,6},{8,9},{9,11},{10,8... | collective-permute-start | bytes 393224 | tf_op jit(solution)/shard_map/ppermute | solution.py:244
  40.8 3.0 %collective-permute-start.6 = (bf16[128,512]{1,0:T(8,128)(2,1)S(1)}, bf16[128,512]{1,0:T(8,128)(2,1)S(1)}, u32[]{:S(2)}, u32[]{:S(2)}) collective-permute-start(bf16[128,512]{1,0:T(8,128)(2,1)S(1)} %value_grad.1.refs_0_), channel_id=1, source_target_pairs={{0,3},{1,2},{2,1},{3,0},{4,7},{5,6},{6,5},{7,4},{8,11},{9,10},{10,... | collective-permute-start | bytes 393224 | tf_op jit(solution)/shard_map/ppermute | solution.py:244
  43.8 0.3 transpose_tokens.1.features
  44.1 1.4 %collective-permute-done.8.refs_3_ = bf16[128,512]{1,0:T(8,128)(2,1)S(1)} collective-permute-done((bf16[128,512]{1,0:T(8,128)(2,1)S(1)}, bf16[128,512]{1,0:T(8,128)(2,1)S(1)}, u32[]{:S(2)}, u32[]{:S(2)}) %collective-permute-start.8) | collective-permute-done | bytes 131104 | tf_op jit(solution)/shard_map/ppermute | solution.py:244
  45.6 4.2 %collective-permute-done.7.refs_2_ = bf16[128,512]{1,0:T(8,128)(2,1)S(1)} collective-permute-done((bf16[128,512]{1,0:T(8,128)(2,1)S(1)}, bf16[128,512]{1,0:T(8,128)(2,1)S(1)}, u32[]{:S(2)}, u32[]{:S(2)}) %collective-permute-start.7) | collective-permute-done | bytes 131104 | tf_op jit(solution)/shard_map/ppermute | solution.py:244
  49.8 0.7 %direction.3 = bf16[512,512]{1,0:T(8,128)(2,1)S(1)} custom-call(bf16[1024,512]{1,0:T(8,128)(2,1)S(1)} %transpose_tokens.1.features, bf16[128,512]{1,0:T(8,128)(2,1)S(1)} %value_grad.1.refs_0_, bf16[128,512]{1,0:T(8,128)(2,1)S(1)} %collective-permute-done.6.refs_1_, bf16[128,512]{1,0:T(8,128)(2,1)S(1)} %collective-permute-done.7.refs_2_, ...), custom_call_target="tpu_custom_call" | custom-call | flops 268435456 | bytes 8388608 | tf_op jit(solution)/shard_map/direction/pallas_call | solution.py:88
  50.5 0.1 collective-permute-start.9
  50.6 0.7 direction.2.mine
  51.4 1.1 %collective-permute-done.9.theirs = bf16[512,512]{1,0:T(8,128)(2,1)S(1)} collective-permute-done((bf16[512,512]{1,0:T(8,128)(2,1)S(1)}, bf16[512,512]{1,0:T(8,128)(2,1)S(1)}, u32[]{:S(2)}, u32[]{:S(2)}) %collective-permute-start.9) | collective-permute-done | bytes 524320 | tf_op jit(solution)/shard_map/ppermute | solution.py:228
  52.5 0.1 chip_sum.1
  52.6 1.6 %collective-permute-start.10 = (bf16[128,512]{1,0:T(8,128)(2,1)S(1)}, bf16[128,512]{1,0:T(8,128)(2,1)S(1)}, u32[]{:S(2)}, u32[]{:S(2)}) collective-permute-start(bf16[128,512]{1,0:T(8,128)(2,1)S(1)} %get-tuple-element.27), channel_id=1, source_target_pairs={{0,8},{4,12},{8,0},{12,4},{16,24},{20,28},{24,16},{28,20},{1,9},{5... | collective-permute-start | bytes 393224 | tf_op jit(solution)/shard_map/ppermute | solution.py:228
  54.2 1.5 %collective-permute-start.11 = (bf16[128,512]{1,0:T(8,128)(2,1)S(1)}, bf16[128,512]{1,0:T(8,128)(2,1)S(1)}, u32[]{:S(2)}, u32[]{:S(2)}) collective-permute-start(bf16[128,512]{1,0:T(8,128)(2,1)S(1)} %get-tuple-element.28), channel_id=1, source_target_pairs={{0,16},{4,20},{8,24},{12,28},{16,0},{20,4},{24,8},{28,12},{1,17},{... | collective-permute-start | bytes 393224 | tf_op jit(solution)/shard_map/ppermute | solution.py:228
  55.7 0.5 collective-permute-start.12
  56.2 2.4 %collective-permute-done.10.refs_0_ = bf16[128,512]{1,0:T(8,128)(2,1)S(1)} collective-permute-done((bf16[128,512]{1,0:T(8,128)(2,1)S(1)}, bf16[128,512]{1,0:T(8,128)(2,1)S(1)}, u32[]{:S(2)}, u32[]{:S(2)}) %collective-permute-start.10) | collective-permute-done | bytes 131104 | tf_op jit(solution)/shard_map/ppermute | solution.py:228
  58.5 3.7 %collective-permute-done.11.refs_1_ = bf16[128,512]{1,0:T(8,128)(2,1)S(1)} collective-permute-done((bf16[128,512]{1,0:T(8,128)(2,1)S(1)}, bf16[128,512]{1,0:T(8,128)(2,1)S(1)}, u32[]{:S(2)}, u32[]{:S(2)}) %collective-permute-start.11) | collective-permute-done | bytes 131104 | tf_op jit(solution)/shard_map/ppermute | solution.py:228
  62.2 0.1 mean_direction.1.refs_0_
  62.3 1.5 %collective-permute-start.17 = (bf16[128,512]{1,0:T(8,128)(2,1)S(1)}, bf16[128,512]{1,0:T(8,128)(2,1)S(1)}, u32[]{:S(2)}, u32[]{:S(2)}) collective-permute-start(bf16[128,512]{1,0:T(8,128)(2,1)S(1)} %mean_direction.1.refs_0_), channel_id=1, source_target_pairs={{0,24},{4,28},{8,16},{12,20},{16,8},{20,12},{24,0},{28,4},{1,25},{... | collective-permute-start | bytes 393224 | tf_op jit(solution)/shard_map/ppermute | solution.py:228
  63.9 1.2 %collective-permute-start.15 = (bf16[128,512]{1,0:T(8,128)(2,1)S(1)}, bf16[128,512]{1,0:T(8,128)(2,1)S(1)}, u32[]{:S(2)}, u32[]{:S(2)}) collective-permute-start(bf16[128,512]{1,0:T(8,128)(2,1)S(1)} %mean_direction.1.refs_0_), channel_id=1, source_target_pairs={{0,16},{4,20},{8,24},{12,28},{16,0},{20,4},{24,8},{28,12},{1,17},{... | collective-permute-start | bytes 393224 | tf_op jit(solution)/shard_map/ppermute | solution.py:228
  65.1 0.8 %collective-permute-start.13 = (bf16[128,512]{1,0:T(8,128)(2,1)S(1)}, bf16[128,512]{1,0:T(8,128)(2,1)S(1)}, u32[]{:S(2)}, u32[]{:S(2)}) collective-permute-start(bf16[128,512]{1,0:T(8,128)(2,1)S(1)} %mean_direction.1.refs_0_), channel_id=1, source_target_pairs={{0,8},{4,12},{8,0},{12,4},{16,24},{20,28},{24,16},{28,20},{1,9},{5... | collective-permute-start | bytes 393224 | tf_op jit(solution)/shard_map/ppermute | solution.py:228
  65.9 3.4 %collective-permute-done.17.refs_3_ = bf16[128,512]{1,0:T(8,128)(2,1)S(1)} collective-permute-done((bf16[128,512]{1,0:T(8,128)(2,1)S(1)}, bf16[128,512]{1,0:T(8,128)(2,1)S(1)}, u32[]{:S(2)}, u32[]{:S(2)}) %collective-permute-start.17) | collective-permute-done | bytes 131104 | tf_op jit(solution)/shard_map/ppermute | solution.py:228
  69.3 1.1 %collective-permute-done.15.refs_2_ = bf16[128,512]{1,0:T(8,128)(2,1)S(1)} collective-permute-done((bf16[128,512]{1,0:T(8,128)(2,1)S(1)}, bf16[128,512]{1,0:T(8,128)(2,1)S(1)}, u32[]{:S(2)}, u32[]{:S(2)}) %collective-permute-start.15) | collective-permute-done | bytes 131104 | tf_op jit(solution)/shard_map/ppermute | solution.py:228
  70.3 0.3 collective-permute-done.13.refs_1_
  70.6 0.2 collective-permute-start.14
  70.9 1.8 %outer_step.2 = (f32[1024,512]{1,0:T(8,128)}, f32[1024,512]{1,0:T(8,128)}) custom-call(bf16[128,512]{1,0:T(8,128)(2,1)S(1)} %mean_direction.1.refs_0_, bf16[128,512]{1,0:T(8,128)(2,1)S(1)} %collective-permute-done.13.refs_1_, bf16[128,512]{1,0:T(8,128)(2,1)S(1)} %collective-permute-done.15.refs_2_, bf16[128,512]{1,0:T(8,128)(2,1)S(1)} %collective-permute-done.17.refs_3_, ...), custom_call_target="tpu_custom_call" | custom-call | bytes 7077888 | tf_op jit(solution)/shard_map/outer_step/pallas_call | solution.py:212
  72.7 1.1 %outer_step.3 = (f32[1024,512]{1,0:T(8,128)}, f32[1024,512]{1,0:T(8,128)}) custom-call(bf16[128,512]{1,0:T(8,128)(2,1)S(1)} %collective-permute-done.14.refs_0_, bf16[128,512]{1,0:T(8,128)(2,1)S(1)} %collective-permute-done.16.refs_1_, f32[1024,512]{1,0:T(8,128)S(1)} %copy-done.3, ...), custom_call_target="tpu_custom_call", output_to_operand_aliasing={{0}: (4, {}), {1}: (5, {})} | custom-call | bytes 2359296 | tf_op jit(solution)/shard_map/outer_step/pallas_call | solution.py:212
  (22 shorter events, 0.1 us)
Async XLA Ops:
  0.6 9.5 %copy-start = (f32[1024,512]{1,0:T(8,128)S(1)}, f32[1024,512]{1,0:T(8,128)}, u32[]{:S(2)}) copy-start(f32[1024,512]{1,0:T(8,128)} %refs_3_.1) | copy-start | bytes 6291460
  1.8 12.4 %collective-permute-start = (bf16[128,1024]{1,0:T(8,128)(2,1)S(1)}, bf16[128,1024]{1,0:T(8,128)(2,1)S(1)}, u32[]{:S(2)}, u32[]{:S(2)}) collective-permute-start(bf16[128,1024]{1,0:T(8,128)(2,1)S(1)} %constant_dynamic-slice_fusion.3), channel_id=1, source_target_pairs={{0,3},{1,2},{2,1},{3,0},{4,7},{5,6},{6,5},{7,4},{8,11},{9,10},{10,... | collective-permute-start | bytes 786440 | tf_op jit(solution)/shard_map/ppermute | solution.py:244
  8.1 18.7 %collective-permute-start.2 = (bf16[128,1024]{1,0:T(8,128)(2,1)S(1)}, bf16[128,1024]{1,0:T(8,128)(2,1)S(1)}, u32[]{:S(2)}, u32[]{:S(2)}) collective-permute-start(bf16[128,1024]{1,0:T(8,128)(2,1)S(1)} %get-tuple-element.32), channel_id=1, source_target_pairs={{0,2},{1,0},{2,3},{3,1},{4,6},{5,4},{6,7},{7,5},{8,10},{9,8},{10,1... | collective-permute-start | bytes 786440 | tf_op jit(solution)/shard_map/ppermute | solution.py:244
  8.1 24.9 %collective-permute-start.1 = (bf16[128,1024]{1,0:T(8,128)(2,1)S(1)}, bf16[128,1024]{1,0:T(8,128)(2,1)S(1)}, u32[]{:S(2)}, u32[]{:S(2)}) collective-permute-start(bf16[128,1024]{1,0:T(8,128)(2,1)S(1)} %get-tuple-element.33), channel_id=1, source_target_pairs={{0,1},{1,3},{2,0},{3,2},{4,5},{5,7},{6,4},{7,6},{8,9},{9,11},{10,8... | collective-permute-start | bytes 786440 | tf_op jit(solution)/shard_map/ppermute | solution.py:244
  14.5 19.0 %copy-start.4 = (bf16[128,2048]{1,0:T(8,128)(2,1)S(1)}, bf16[128,2048]{1,0:T(8,128)(2,1)}, u32[]{:S(2)}) copy-start(bf16[128,2048]{1,0:T(8,128)(2,1)} %queries.1) | copy-start | bytes 1572868
  14.5 19.0 %copy-start.5 = (bf16[128,2048]{1,0:T(8,128)(2,1)S(1)}, bf16[128,2048]{1,0:T(8,128)(2,1)}, u32[]{:S(2)}) copy-start(bf16[128,2048]{1,0:T(8,128)(2,1)} %targets.1) | copy-start | bytes 1572868
  14.5 19.0 %copy-start.6 = (bf16[128,512]{1,0:T(8,128)(2,1)S(1)}, bf16[128,512]{1,0:T(8,128)(2,1)}, u32[]{:S(2)}) copy-start(bf16[128,512]{1,0:T(8,128)(2,1)} %keys.1) | copy-start | bytes 393220
  14.5 18.9 %collective-permute-start.3 = (bf16[128,512]{1,0:T(8,128)(2,1)S(1)}, bf16[128,512]{1,0:T(8,128)(2,1)S(1)}, u32[]{:S(2)}, u32[]{:S(2)}) collective-permute-start(bf16[128,512]{1,0:T(8,128)(2,1)S(1)} %partial_value.4), channel_id=1, source_target_pairs={{0,2},{1,0},{2,3},{3,1},{4,6},{5,4},{6,7},{7,5},{8,10},{9,8},{10,1... | collective-permute-start | bytes 393224 | tf_op jit(solution)/shard_map/ppermute | solution.py:244
  27.0 9.4 %collective-permute-start.5 = (bf16[128,512]{1,0:T(8,128)(2,1)S(1)}, bf16[128,512]{1,0:T(8,128)(2,1)S(1)}, u32[]{:S(2)}, u32[]{:S(2)}) collective-permute-start(bf16[128,512]{1,0:T(8,128)(2,1)S(1)} %partial_value.5), channel_id=1, source_target_pairs={{0,1},{1,3},{2,0},{3,2},{4,5},{5,7},{6,4},{7,6},{8,9},{9,11},{10,8... | collective-permute-start | bytes 393224 | tf_op jit(solution)/shard_map/ppermute | solution.py:244
  33.4 16.4 %copy-start.1 = (f32[1,1024,512]{2,1,0:T(8,128)S(1)}, f32[1,1024,512]{2,1,0:T(8,128)}, u32[]{:S(2)}) copy-start(f32[1,1024,512]{2,1,0:T(8,128)} %refs_4_.3) | copy-start | bytes 6291460
  33.4 16.3 %copy-start.2 = (f32[1,1024,512]{2,1,0:T(8,128)S(1)}, f32[1,1024,512]{2,1,0:T(8,128)}, u32[]{:S(2)}) copy-start(f32[1,1024,512]{2,1,0:T(8,128)} %refs_5_.3) | copy-start | bytes 6291460
  33.4 5.0 %collective-permute-start.4 = (bf16[128,512]{1,0:T(8,128)(2,1)S(1)}, bf16[128,512]{1,0:T(8,128)(2,1)S(1)}, u32[]{:S(2)}, u32[]{:S(2)}) collective-permute-start(bf16[128,512]{1,0:T(8,128)(2,1)S(1)} %joined_value.1), channel_id=1, source_target_pairs={{0,2},{1,0},{2,3},{3,1},{4,6},{5,4},{6,7},{7,5},{8,10},{9,8},{10,1... | collective-permute-start | bytes 393224 | tf_op jit(solution)/shard_map/ppermute | solution.py:244
  38.7 6.9 %collective-permute-start.8 = (bf16[128,512]{1,0:T(8,128)(2,1)S(1)}, bf16[128,512]{1,0:T(8,128)(2,1)S(1)}, u32[]{:S(2)}, u32[]{:S(2)}) collective-permute-start(bf16[128,512]{1,0:T(8,128)(2,1)S(1)} %value_grad.1.refs_0_), channel_id=1, source_target_pairs={{0,2},{1,0},{2,3},{3,1},{4,6},{5,4},{6,7},{7,5},{8,10},{9,8},{10,1... | collective-permute-start | bytes 393224 | tf_op jit(solution)/shard_map/ppermute | solution.py:244
  39.9 9.9 %collective-permute-start.7 = (bf16[128,512]{1,0:T(8,128)(2,1)S(1)}, bf16[128,512]{1,0:T(8,128)(2,1)S(1)}, u32[]{:S(2)}, u32[]{:S(2)}) collective-permute-start(bf16[128,512]{1,0:T(8,128)(2,1)S(1)} %value_grad.1.refs_0_), channel_id=1, source_target_pairs={{0,1},{1,3},{2,0},{3,2},{4,5},{5,7},{6,4},{7,6},{8,9},{9,11},{10,8... | collective-permute-start | bytes 393224 | tf_op jit(solution)/shard_map/ppermute | solution.py:244
  40.8 9.0 %collective-permute-start.6 = (bf16[128,512]{1,0:T(8,128)(2,1)S(1)}, bf16[128,512]{1,0:T(8,128)(2,1)S(1)}, u32[]{:S(2)}, u32[]{:S(2)}) collective-permute-start(bf16[128,512]{1,0:T(8,128)(2,1)S(1)} %value_grad.1.refs_0_), channel_id=1, source_target_pairs={{0,3},{1,2},{2,1},{3,0},{4,7},{5,6},{6,5},{7,4},{8,11},{9,10},{10,... | collective-permute-start | bytes 393224 | tf_op jit(solution)/shard_map/ppermute | solution.py:244
  50.5 2.0 %collective-permute-start.9 = (bf16[512,512]{1,0:T(8,128)(2,1)S(1)}, bf16[512,512]{1,0:T(8,128)(2,1)S(1)}, u32[]{:S(2)}, u32[]{:S(2)}) collective-permute-start(bf16[512,512]{1,0:T(8,128)(2,1)S(1)} %direction.3), channel_id=1, source_target_pairs={{0,4},{4,0},{8,12},{12,8},{16,20},{20,16},{24,28},{28,24},{1,5},{5... | collective-permute-start | bytes 1572872 | tf_op jit(solution)/shard_map/ppermute | solution.py:228
  51.3 19.5 %copy-start.3 = (f32[1024,512]{1,0:T(8,128)S(1)}, f32[1024,512]{1,0:T(8,128)}, u32[]{:S(2)}) copy-start(f32[1024,512]{1,0:T(8,128)} %refs_2_.1) | copy-start | bytes 6291460
  52.6 5.9 %collective-permute-start.10 = (bf16[128,512]{1,0:T(8,128)(2,1)S(1)}, bf16[128,512]{1,0:T(8,128)(2,1)S(1)}, u32[]{:S(2)}, u32[]{:S(2)}) collective-permute-start(bf16[128,512]{1,0:T(8,128)(2,1)S(1)} %get-tuple-element.27), channel_id=1, source_target_pairs={{0,8},{4,12},{8,0},{12,4},{16,24},{20,28},{24,16},{28,20},{1,9},{5... | collective-permute-start | bytes 393224 | tf_op jit(solution)/shard_map/ppermute | solution.py:228
  54.2 8.1 %collective-permute-start.11 = (bf16[128,512]{1,0:T(8,128)(2,1)S(1)}, bf16[128,512]{1,0:T(8,128)(2,1)S(1)}, u32[]{:S(2)}, u32[]{:S(2)}) collective-permute-start(bf16[128,512]{1,0:T(8,128)(2,1)S(1)} %get-tuple-element.28), channel_id=1, source_target_pairs={{0,16},{4,20},{8,24},{12,28},{16,0},{20,4},{24,8},{28,12},{1,17},{... | collective-permute-start | bytes 393224 | tf_op jit(solution)/shard_map/ppermute | solution.py:228
  55.7 6.6 %collective-permute-start.12 = (bf16[128,512]{1,0:T(8,128)(2,1)S(1)}, bf16[128,512]{1,0:T(8,128)(2,1)S(1)}, u32[]{:S(2)}, u32[]{:S(2)}) collective-permute-start(bf16[128,512]{1,0:T(8,128)(2,1)S(1)} %get-tuple-element.29), channel_id=1, source_target_pairs={{0,24},{4,28},{8,16},{12,20},{16,8},{20,12},{24,0},{28,4},{1,25},{... | collective-permute-start | bytes 393224 | tf_op jit(solution)/shard_map/ppermute | solution.py:228
  62.3 6.9 %collective-permute-start.17 = (bf16[128,512]{1,0:T(8,128)(2,1)S(1)}, bf16[128,512]{1,0:T(8,128)(2,1)S(1)}, u32[]{:S(2)}, u32[]{:S(2)}) collective-permute-start(bf16[128,512]{1,0:T(8,128)(2,1)S(1)} %mean_direction.1.refs_0_), channel_id=1, source_target_pairs={{0,24},{4,28},{8,16},{12,20},{16,8},{20,12},{24,0},{28,4},{1,25},{... | collective-permute-start | bytes 393224 | tf_op jit(solution)/shard_map/ppermute | solution.py:228
  63.9 6.5 %collective-permute-start.15 = (bf16[128,512]{1,0:T(8,128)(2,1)S(1)}, bf16[128,512]{1,0:T(8,128)(2,1)S(1)}, u32[]{:S(2)}, u32[]{:S(2)}) collective-permute-start(bf16[128,512]{1,0:T(8,128)(2,1)S(1)} %mean_direction.1.refs_0_), channel_id=1, source_target_pairs={{0,16},{4,20},{8,24},{12,28},{16,0},{20,4},{24,8},{28,12},{1,17},{... | collective-permute-start | bytes 393224 | tf_op jit(solution)/shard_map/ppermute | solution.py:228
  65.1 5.6 %collective-permute-start.13 = (bf16[128,512]{1,0:T(8,128)(2,1)S(1)}, bf16[128,512]{1,0:T(8,128)(2,1)S(1)}, u32[]{:S(2)}, u32[]{:S(2)}) collective-permute-start(bf16[128,512]{1,0:T(8,128)(2,1)S(1)} %mean_direction.1.refs_0_), channel_id=1, source_target_pairs={{0,8},{4,12},{8,0},{12,4},{16,24},{20,28},{24,16},{28,20},{1,9},{5... | collective-permute-start | bytes 393224 | tf_op jit(solution)/shard_map/ppermute | solution.py:228
  65.9 5.0 %collective-permute-start.18 = (bf16[128,512]{1,0:T(8,128)(2,1)S(1)}, bf16[128,512]{1,0:T(8,128)(2,1)S(1)}, u32[]{:S(2)}, u32[]{:S(2)}) collective-permute-start(bf16[128,512]{1,0:T(8,128)(2,1)S(1)} %mean_direction.1.refs_0_), channel_id=1, source_target_pairs={{0,4},{4,0},{8,12},{12,8},{16,20},{20,16},{24,28},{28,24},{1,5},{5... | collective-permute-start | bytes 393224 | tf_op jit(solution)/shard_map/ppermute | solution.py:228
  69.3 1.6 %collective-permute-start.19 = (bf16[128,512]{1,0:T(8,128)(2,1)S(1)}, bf16[128,512]{1,0:T(8,128)(2,1)S(1)}, u32[]{:S(2)}, u32[]{:S(2)}) collective-permute-start(bf16[128,512]{1,0:T(8,128)(2,1)S(1)} %collective-permute-done.17.refs_3_), channel_id=1, source_target_pairs={{0,4},{4,0},{8,12},{12,8},{16,20},{20,16},{24,28},{28,24},{1,5},{5... | collective-permute-start | bytes 393224 | tf_op jit(solution)/shard_map/ppermute | solution.py:228
  70.3 2.4 %collective-permute-start.16 = (bf16[128,512]{1,0:T(8,128)(2,1)S(1)}, bf16[128,512]{1,0:T(8,128)(2,1)S(1)}, u32[]{:S(2)}, u32[]{:S(2)}) collective-permute-start(bf16[128,512]{1,0:T(8,128)(2,1)S(1)} %collective-permute-done.15.refs_2_), channel_id=1, source_target_pairs={{0,4},{4,0},{8,12},{12,8},{16,20},{20,16},{24,28},{28,24},{1,5},{5... | collective-permute-start | bytes 393224 | tf_op jit(solution)/shard_map/ppermute | solution.py:228
  70.6 2.1 %collective-permute-start.14 = (bf16[128,512]{1,0:T(8,128)(2,1)S(1)}, bf16[128,512]{1,0:T(8,128)(2,1)S(1)}, u32[]{:S(2)}, u32[]{:S(2)}) collective-permute-start(bf16[128,512]{1,0:T(8,128)(2,1)S(1)} %collective-permute-done.13.refs_1_), channel_id=1, source_target_pairs={{0,4},{4,0},{8,12},{12,8},{16,20},{20,16},{24,28},{28,24},{1,5},{5... | collective-permute-start | bytes 393224 | tf_op jit(solution)/shard_map/ppermute | solution.py:228
